TPU v7x, 256 devices: a whole 4x4x8 slice. The times are simulated.
256 devices in a mesh: ctx: 32 (over y, x, z_hi), tp: 8 (over z_lo, core).
Axes of the slice: x: 4, y: 4, z: 8 (z_hi: 2, z_lo: 4; z = z_hi * 4 + z_lo), core: 2. Of those that a mesh axis runs over, the one named last changes fastest.
Arguments:
- segment_ordering: int32 [64], replicated, may hold values from 0 to 63, as said below
- attention_input: bfloat16 [4096, 8192], P('ctx', 'tp'), may hold values from -6 to 6
- residual: bfloat16 [4096, 3584], P(('ctx', 'tp')), may hold values from -6 to 6
- queries: bfloat16 [4096, 12288], P('ctx', 'tp'), may hold values from -120 to 120
- output_weight: bfloat16 [8192, 3584], P('tp'), may hold values from -0.0625 to 0.0625
- adapter_down_factor: bfloat16 [8192, 256], P('tp'), may hold values from -0.0625 to 0.0625
- adapter_up_factor: bfloat16 [256, 3584], replicated, may hold values from -0.375 to 0.375
- input_norm_gain: bfloat16 [3584], replicated, may hold values from 0.099609375 to 1.8984375
- latent_key_weight: bfloat16 [3584, 576], P('ctx'), may hold values from -0.09375 to 0.09375
- latent_norm_gain: bfloat16 [512], replicated, may hold values from 0.099609375 to 1.8984375
- latent_up_weight: bfloat16 [512, 16384], P(None, 'tp'), may hold values from -0.25 to 0.25
Outputs:
- hidden: bfloat16 [4096, 3584], P(('ctx', 'tp'))
- attn: bfloat16 [4096, 8192], P('ctx', 'tp')
Inputs may be any that keep to these rules, and one draw needn't show every extreme that they name: `segment_ordering`: entries 2 i and 2 i + 1 (the segments stored by one index of ctx) sum to 63, and every segment number appears once.
All inputs are finite; a program needn't handle non-finite values.
Results may differ from a plain program's by a relative error of at most 0.04.
Values may be sent and summed in bfloat16 or wider, within the bound.
No kernel may reach another device: no remote copies, remote signals or barrier semaphores. Data moves between devices by JAX's collectives and lax.ppermute only.
A program may use at most 64 MiB of HBM per device.

v0:
```python
import math

import jax
import jax.numpy as jnp
from jax import lax
from jax.sharding import PartitionSpec as P

LATENT = 512
ROPE = 64
NOPE = 128
VDIM = 128


big_negative = -1e30


def rms_scaled(values, gain):
    mean_square = jnp.mean(values * values, axis=-1, keepdims=True)
    return values * lax.rsqrt(mean_square + 1e-06) * gain.astype(jnp.float32)


def rotate(values, places):
    half_width = values.shape[-1] // 2
    ladder = jnp.arange(half_width, dtype=jnp.float32)
    inverse = jnp.exp(ladder * (-2.0 * math.log(10000.0) / values.shape[-1]))
    angles = places.astype(jnp.float32)[:, None] * inverse[None, :]
    cosine = jnp.cos(angles)
    sine = jnp.sin(angles)
    first = values[:, :half_width]
    second = values[:, half_width:]
    return jnp.concatenate([first * cosine - second * sine, first * sine + second * cosine], axis=1)


def place_rows(segment_ordering, stored, seg_len):
    numbers = jnp.arange(segment_ordering.shape[0], dtype=jnp.int32)
    picked = jnp.sum(
        jnp.where((stored // seg_len)[:, None] == numbers[None, :], segment_ordering[None, :], 0),
        axis=1,
    )
    return picked * seg_len + stored % seg_len


def body(
    segment_ordering,
    attention_input,
    residual,
    queries,
    output_weight,
    adapter_down_factor,
    adapter_up_factor,
    input_norm_gain,
    latent_key_weight,
    latent_norm_gain,
    latent_up_weight,
):
    tok_dev = attention_input.shape[0]
    own_rows = residual.shape[0]
    seg_len = tok_dev // 2
    heads_dev = latent_up_weight.shape[1] // (NOPE + VDIM)
    ctx_index = lax.axis_index("ctx")
    tp_index = lax.axis_index("tp")
    adapter_widened = adapter_up_factor.astype(jnp.float32)
    base_product = jnp.dot(attention_input, output_weight, preferred_element_type=jnp.float32)
    down_partial = jnp.dot(attention_input, adapter_down_factor, preferred_element_type=jnp.float32)
    summed = lax.psum_scatter(
        base_product + jnp.dot(down_partial, adapter_widened, precision=lax.Precision.HIGHEST),
        "tp",
        scatter_dimension=0,
        tiled=True,
    )
    hidden = (residual.astype(jnp.float32) + summed).astype(jnp.bfloat16)
    normed = rms_scaled(hidden.astype(jnp.float32), input_norm_gain).astype(jnp.bfloat16)
    latent = jnp.dot(
        normed,
        lax.all_gather(latent_key_weight, "ctx", axis=0, tiled=True),
        preferred_element_type=jnp.float32,
    )
    own_stored = ctx_index * tok_dev + tp_index * own_rows + jnp.arange(own_rows, dtype=jnp.int32)
    own_places = place_rows(segment_ordering, own_stored, seg_len)
    compressed = rms_scaled(latent[:, :LATENT], latent_norm_gain)
    key_rope = rotate(latent[:, LATENT:], own_places)
    kv_rows = jnp.concatenate([compressed, key_rope], axis=1).astype(jnp.bfloat16)
    query_heads = queries.reshape(tok_dev, heads_dev, NOPE + ROPE)
    query_places = place_rows(
        segment_ordering, ctx_index * tok_dev + jnp.arange(tok_dev, dtype=jnp.int32), seg_len
    )
    score_scale = 1.0 / math.sqrt(NOPE + ROPE)

    def attend(state, block, key_places):
        top_score, totals, weighted = state
        size = block.shape[0]
        lifted = jnp.dot(
            block[:, :LATENT], latent_up_weight, preferred_element_type=jnp.float32
        ).astype(jnp.bfloat16)
        lifted = lifted.reshape(size, heads_dev, NOPE + VDIM)
        shared = jnp.broadcast_to(block[:, None, LATENT:], (size, heads_dev, ROPE))
        keys = jnp.concatenate([lifted[:, :, :NOPE], shared], axis=2)
        scores = (
            jnp.einsum("ihd,jhd->hij", query_heads, keys, preferred_element_type=jnp.float32)
            * score_scale
        )
        visible = (key_places[None, :] <= query_places[:, None])[None, :, :]
        masked = jnp.where(visible, scores, big_negative)
        new_top = jnp.maximum(top_score, jnp.max(masked, axis=2))
        weights = jnp.where(visible, jnp.exp(masked - new_top[:, :, None]), 0.0)
        decay = jnp.exp(top_score - new_top)
        totals = totals * decay + jnp.sum(weights, axis=2)
        mixed = jnp.einsum(
            "hij,jhd->hid",
            weights.astype(jnp.bfloat16),
            lifted[:, :, NOPE:],
            preferred_element_type=jnp.float32,
        )
        weighted = weighted * decay[:, :, None] + mixed
        return (new_top, totals, weighted)

    initial = (
        jnp.full((heads_dev, tok_dev), big_negative, jnp.float32),
        jnp.zeros((heads_dev, tok_dev), jnp.float32),
        jnp.zeros((heads_dev, tok_dev, VDIM), jnp.float32),
    )
    every_row = lax.all_gather(kv_rows, ("ctx", "tp"), axis=0, tiled=True)
    count = every_row.shape[0]
    size = math.gcd(count, 512)

    def one_block(step, inner):
        offset = step * size
        block = lax.dynamic_slice_in_dim(every_row, offset, size, 0)
        stored = 0 + offset + jnp.arange(size, dtype=jnp.int32)
        return attend(inner, block, place_rows(segment_ordering, stored, seg_len))

    state = lax.fori_loop(0, count // size, one_block, initial)
    top_score, totals, weighted = state
    result = weighted / totals[:, :, None]
    attn = jnp.transpose(result, (1, 0, 2)).reshape(tok_dev, heads_dev * VDIM).astype(jnp.bfloat16)
    return (hidden, attn)


def solution(mesh):
    in_specs = (
        P(),
        P("ctx", "tp"),
        P(("ctx", "tp"), None),
        P("ctx", "tp"),
        P("tp", None),
        P("tp", None),
        P(),
        P(),
        P("ctx", None),
        P(),
        P(None, "tp"),
    )
    out_specs = (P(("ctx", "tp"), None), P("ctx", "tp"))
    return jax.shard_map(body, mesh=mesh, in_specs=in_specs, out_specs=out_specs, check_vma=False)
```

profile of v0, /device:TPU:24, one launch (start us, length us, event | category | flops | bytes accessed | tf_op | source)
XLA Modules:
  0.0 385.3 jit_solution(17608961453295449781)
XLA Ops:
  8.1 4.4 %fusion.45 = f32[128,3584]{1,0:T(8,128)S(1)} fusion(bf16[128,1024]{1,0:T(8,128)(2,1)} %param.14, bf16[1024,3584]{1,0:T(8,128)(2,1)} %param.17), kind=kOutput, calls=%fused_computation.91 | convolution fusion | flops 939524096 | bytes 9437184 | tf_op jit(solution)/shard_map/dot_general | solution.py:63
  12.8 2.2 convolution_add_fusion.1
  16.0 42.8 %reduce-scatter.2.cloned.1.call-done = f32[16,3584]{1,0:T(8,128)} async-done(((f32[128,3584]{1,0:T(8,128)}), f32[16,3584]{1,0:T(8,128)}) %reduce-scatter.2.cloned.1.call-update) | async-done | bytes 229392 | tf_op jit(solution)/shard_map/reduce_scatter | solution.py:65
  60.0 76.7 %all-gather.3.cloned.1.call-done = bf16[3584,576]{1,0:T(8,128)(2,1)} async-done(((bf16[112,576]{1,0:T(8,128)(2,1)}), bf16[3584,576]{1,0:T(8,128)(2,1)}) %all-gather.3.cloned.1.call-update) | async-done | bytes 4128784 | tf_op jit(solution)/shard_map/all_gather | solution.py:75
  136.7 3.1 fusion.29
  141.9 110.0 %all-gather.5.cloned.1.call-done = bf16[4096,576]{1,0:T(8,128)(2,1)} async-done(((bf16[16,576]{1,0:T(8,128)(2,1)}), bf16[4096,576]{1,0:T(8,128)(2,1)}) %all-gather.5.cloned.1.call-update) | async-done | bytes 4718608 | tf_op jit(solution)/shard_map/all_gather | solution.py:122
  251.9 7.6 %copy.23 = bf16[4096,576]{0,1:T(8,128)(2,1)} copy(bf16[4096,576]{1,0:T(8,128)(2,1)} %all-gather.5.cloned.1.call-done) | data formatting | bytes 9437184
  259.6 117.4 %while.20 = (s32[]{:T(128)}, f32[8,128]{1,0:T(8,128)S(1)}, f32[8,128]{1,0:T(8,128)S(1)}, f32[8,128,128]{2,1,0:T(8,128)S(1)}, s32[64]{0:T(128)S(1)}, /*index=5*/s...) while((s32[]{:T(128)}, f32[8,128]{1,0:T(8,128)S(1)}, ...), condition=%wide.region_9.10_spmd.clone, body=%wide.region_5.9_spmd.clone.sunk | while | flops 1420873216 | bytes 39203856 | solution.py:132
  259.6 3.0 convolution_convert_fusion.2
  264.4 1.5 copy.38
  267.1 3.6 fusion.74
  270.7 2.2 fusion.75
  273.0 1.2 convolution_add_fusion.3
  274.2 3.0 convolution_convert_fusion.2
  279.1 1.5 copy.38
  281.8 3.6 fusion.74
  285.4 2.2 fusion.75
  287.7 1.2 convolution_add_fusion.3
  288.9 3.0 convolution_convert_fusion.2
  293.8 1.5 copy.38
  296.5 3.6 fusion.74
  300.1 2.2 fusion.75
  302.4 1.2 convolution_add_fusion.3
  303.6 3.0 convolution_convert_fusion.2
  308.5 1.5 copy.38
  311.1 3.6 fusion.74
  314.7 2.2 fusion.75
  317.0 1.2 convolution_add_fusion.3
  318.3 3.0 convolution_convert_fusion.2
  323.2 1.5 copy.38
  325.8 3.6 fusion.74
  329.4 2.2 fusion.75
  331.7 1.2 convolution_add_fusion.3
  333.0 3.0 convolution_convert_fusion.2
  337.8 1.5 copy.38
  340.5 3.6 fusion.74
  344.1 2.2 fusion.75
  346.4 1.2 convolution_add_fusion.3
  347.6 3.0 convolution_convert_fusion.2
  352.5 1.5 copy.38
  355.2 3.6 fusion.74
  358.8 2.2 fusion.75
  361.1 1.2 convolution_add_fusion.3
  362.3 3.0 convolution_convert_fusion.2
  367.2 1.5 copy.38
  369.8 3.6 fusion.74
  373.5 2.2 fusion.75
  375.7 1.2 convolution_add_fusion.3
  (166 shorter events, 29.1 us)
Async XLA Ops:
  8.0 4.8 %copy-start = (bf16[256,3584]{1,0:T(8,128)(2,1)S(1)}, bf16[256,3584]{1,0:T(8,128)(2,1)}, u32[]{:S(2)}) copy-start(bf16[256,3584]{1,0:T(8,128)(2,1)} %param.19) | copy-start | bytes 5505028
  8.0 4.5 %copy-start.3 = (bf16[128,1024]{1,0:T(8,128)(2,1)S(1)}, bf16[128,1024]{1,0:T(8,128)(2,1)}, u32[]{:S(2)}) copy-start(bf16[128,1024]{1,0:T(8,128)(2,1)} %param.14) | copy-start | bytes 786436
  8.0 4.5 %copy-start.4 = (bf16[1024,256]{1,0:T(8,128)(2,1)S(1)}, bf16[1024,256]{1,0:T(8,128)(2,1)}, u32[]{:S(2)}) copy-start(bf16[1024,256]{1,0:T(8,128)(2,1)} %param.18) | copy-start | bytes 1572868
  8.0 50.8 %reduce-scatter.2.cloned.1.call-start = ((), (), s32[]{:S(2)}) async-start(), calls=%async_computation.1 | async-start | bytes 2064384 | tf_op jit(solution)/shard_map/reduce_scatter | solution.py:65
  12.8 2.9 copy-start.9
  12.8 2.9 copy-start.10
  12.8 2.9 copy-start.8
  15.0 43.8 %copy-start.7 = (bf16[16,3584]{1,0:T(8,128)(2,1)S(1)}, bf16[16,3584]{1,0:T(8,128)(2,1)}, u32[]{:S(2)}) copy-start(bf16[16,3584]{1,0:T(8,128)(2,1)} %param.15) | copy-start | bytes 344068
  15.1 121.6 %all-gather.3.cloned.1.call-start = ((), (), s32[]{:S(2)}) async-start(), calls=%async_computation.2 | async-start | bytes 4730880 | tf_op jit(solution)/shard_map/all_gather | solution.py:75
  15.6 236.3 %all-gather.5.cloned.1.call-start = ((), (), s32[]{:S(2)}) async-start(), calls=%async_computation.3 | async-start | bytes 5263360 | tf_op jit(solution)/shard_map/all_gather | solution.py:122
  59.9 79.8 %copy-start.5 = (bf16[16,3584]{1,0:T(8,128)(2,1)}, bf16[16,3584]{1,0:T(8,128)(2,1)S(1)}, u32[]{:S(2)}) copy-start(bf16[16,3584]{1,0:T(8,128)(2,1)S(1)} %get-tuple-element.297) | copy-start | bytes 344068
  136.7 4.2 %copy-start.6 = (bf16[128,1536]{1,0:T(8,128)(2,1)S(1)}, bf16[128,1536]{1,0:T(8,128)(2,1)}, u32[]{:S(2)}) copy-start(bf16[128,1536]{1,0:T(8,128)(2,1)} %param.16) | copy-start | bytes 1179652
  267.1 5.9 %copy-start.2 = (bf16[512,8,128]{2,1,0:T(8,128)(2,1)S(1)}, bf16[512,8,128]{2,1,0:T(8,128)(2,1)}, u32[]{:S(2)}) copy-start(bf16[512,8,128]{2,1,0:T(8,128)(2,1)} %get-tuple-element.369) | copy-start | bytes 3145732 | tf_op jit(solution)/shard_map/while
  270.7 2.3 copy-start.1
  281.8 5.9 %copy-start.2 = (bf16[512,8,128]{2,1,0:T(8,128)(2,1)S(1)}, bf16[512,8,128]{2,1,0:T(8,128)(2,1)}, u32[]{:S(2)}) copy-start(bf16[512,8,128]{2,1,0:T(8,128)(2,1)} %get-tuple-element.369) | copy-start | bytes 3145732 | tf_op jit(solution)/shard_map/while
  285.4 2.3 copy-start.1
  296.4 5.9 %copy-start.2 = (bf16[512,8,128]{2,1,0:T(8,128)(2,1)S(1)}, bf16[512,8,128]{2,1,0:T(8,128)(2,1)}, u32[]{:S(2)}) copy-start(bf16[512,8,128]{2,1,0:T(8,128)(2,1)} %get-tuple-element.369) | copy-start | bytes 3145732 | tf_op jit(solution)/shard_map/while
  300.1 2.3 copy-start.1
  311.1 5.9 %copy-start.2 = (bf16[512,8,128]{2,1,0:T(8,128)(2,1)S(1)}, bf16[512,8,128]{2,1,0:T(8,128)(2,1)}, u32[]{:S(2)}) copy-start(bf16[512,8,128]{2,1,0:T(8,128)(2,1)} %get-tuple-element.369) | copy-start | bytes 3145732 | tf_op jit(solution)/shard_map/while
  314.7 2.3 copy-start.1
  325.8 5.9 %copy-start.2 = (bf16[512,8,128]{2,1,0:T(8,128)(2,1)S(1)}, bf16[512,8,128]{2,1,0:T(8,128)(2,1)}, u32[]{:S(2)}) copy-start(bf16[512,8,128]{2,1,0:T(8,128)(2,1)} %get-tuple-element.369) | copy-start | bytes 3145732 | tf_op jit(solution)/shard_map/while
  329.4 2.3 copy-start.1
  340.5 5.9 %copy-start.2 = (bf16[512,8,128]{2,1,0:T(8,128)(2,1)S(1)}, bf16[512,8,128]{2,1,0:T(8,128)(2,1)}, u32[]{:S(2)}) copy-start(bf16[512,8,128]{2,1,0:T(8,128)(2,1)} %get-tuple-element.369) | copy-start | bytes 3145732 | tf_op jit(solution)/shard_map/while
  344.1 2.3 copy-start.1
  355.2 5.9 %copy-start.2 = (bf16[512,8,128]{2,1,0:T(8,128)(2,1)S(1)}, bf16[512,8,128]{2,1,0:T(8,128)(2,1)}, u32[]{:S(2)}) copy-start(bf16[512,8,128]{2,1,0:T(8,128)(2,1)} %get-tuple-element.369) | copy-start | bytes 3145732 | tf_op jit(solution)/shard_map/while
  358.8 2.3 copy-start.1
  369.8 5.9 %copy-start.2 = (bf16[512,8,128]{2,1,0:T(8,128)(2,1)S(1)}, bf16[512,8,128]{2,1,0:T(8,128)(2,1)}, u32[]{:S(2)}) copy-start(bf16[512,8,128]{2,1,0:T(8,128)(2,1)} %get-tuple-element.369) | copy-start | bytes 3145732 | tf_op jit(solution)/shard_map/while
  373.4 2.3 copy-start.1
Sparse Core Ops, SparseCore 0:
  15.2 43.5 reduce-scatter.1
  141.0 110.9 all-gather.4
Sparse Core Ops, SparseCore 1:
  18.9 117.7 all-gather.2
where the time goes:
time: 388 us; the launch traced here: 385 us
  waiting for transfers between devices  230 us (59%)
  matrix products  72.9 us (19%)
  local copies, waits for them, and re-layouts  42.1 us (11%)
  other arithmetic  23.6 us (6%)
  between operations  15.7 us (4%)
    all_gather x1, waiting for transfers between devices, body(): every_row = lax.all_gather(kv_rows, ('ctx', 'tp'), axis=0, tiled=True)  110 us
    all_gather x1, waiting for transfers between devices, body(): lax.all_gather(latent_key_weight, 'ctx', axis=0, tiled=True)  76.7 us
    reduce_scatter x1, waiting for transfers between devices, body(): lax.psum_scatter(base_product + jnp.dot(down_partial, adapter_widened, pr...  42.8 us
    dot_general x8, matrix products, attend(): jnp.einsum('ihd,jhd->hij', query_heads, keys, preferred_element_type=jnp....  28.9 us
    dot_general x8, matrix products, attend(): jnp.dot(block[:, :LATENT], latent_up_weight, preferred_element_type=jnp.f...  24.4 us
    reduce_sum x8, other arithmetic, attend(): totals = totals * decay + jnp.sum(weights, axis=2)  18 us
    while x56, local copies, waits for them, and re-layouts  17.3 us
    dot_general x8, matrix products, attend(): jnp.einsum('hij,jhd->hid', weights.astype(jnp.bfloat16), lifted[:, :, NOP...  9.65 us
  transfers between devices with their start and end apart: 3, of which 3 were waited for; matrix products, arithmetic and copies ran while one was open for 1% of the time, Pallas kernels for 0%

commit v1 on v0

v1 whole, which is shorter than its diff:
```python
import functools
import math

import jax
import jax.numpy as jnp
from jax import lax
from jax.experimental import pallas as pl
from jax.experimental.pallas import tpu as pltpu
from jax.sharding import Mesh, PartitionSpec as P

LATENT = 512
ROPE = 64
NOPE = 128
VDIM = 128
HEADS = 8
WIDE = 640
COLS = 896
BF = jnp.bfloat16
F32 = jnp.float32
MIB = 1 << 20
AXES = ("y", "x", "zh", "zl", "core")
SIZES = (4, 4, 2, 4, 2)
ORDER = (2, 1, 3, 0)


def dot(a, b):
    return jnp.dot(a, b, preferred_element_type=F32)


def shift(value, axis, k):
    return lax.ppermute(value, axis, [(i, (i + k) % 4) for i in range(4)])


def swap(value, axis):
    return lax.ppermute(value, axis, [(0, 1), (1, 0)])


def flat(y, x, zh, zl, core):
    return (((y * 4 + x) * 2 + zh) * 4 + zl) * 2 + core


def transposed_blocks(value):
    perm = []
    for y in range(4):
        for x in range(4):
            for zh in range(2):
                for zl in range(4):
                    for core in range(2):
                        perm.append((flat(zl, x, core, y, zh), flat(y, x, zh, zl, core)))
    return lax.ppermute(value, AXES, perm)


def params(mib):
    return pltpu.CompilerParams(vmem_limit_bytes=mib * MIB)


def shape(dims, dtype=BF):
    return jax.ShapeDtypeStruct(dims, dtype)


def project_kernel(s, x_ref, ad_ref, wo_ref, au_ref, res_ref, send_ref, keep_ref, xr, d3):
    core, zl = s[4], s[3]

    @pl.when(pl.program_id(0) == 0)
    def _():
        xr[0:64, :] = x_ref[:, 1 - core].reshape(64, 1024)
        xr[64:128, :] = x_ref[:, core].reshape(64, 1024)
        down = dot(xr[...], ad_ref[...])
        high = down.astype(BF)
        rest = down - high.astype(F32)
        middle = rest.astype(BF)
        d3[0] = high
        d3[1] = middle
        d3[2] = (rest - middle.astype(F32)).astype(BF)

    acc = dot(xr[...], wo_ref[...])
    for piece in range(3):
        acc += dot(d3[piece], au_ref[...])
    send_ref[0] = acc[:64].astype(BF)
    keep_ref[0] = acc[64:]
    rows = pl.ds(pl.multiple_of(zl * 16, 16), 16)
    keep_ref[0, rows, :] = keep_ref[0, rows, :] + res_ref[...].astype(F32)


def project(scalars, x4, down, weight, up, residual):
    block = lambda i, s: (0, s[8 + i])
    return pl.pallas_call(
        project_kernel,
        grid_spec=pltpu.PrefetchScalarGridSpec(
            num_scalar_prefetch=1,
            grid=(4,),
            in_specs=[
                pl.BlockSpec((4, 2, 16, 1024), lambda i, s: (0, 0, 0, 0)),
                pl.BlockSpec((1024, 256), lambda i, s: (0, 0)),
                pl.BlockSpec((1024, COLS), block),
                pl.BlockSpec((256, COLS), block),
                pl.BlockSpec((16, COLS), block),
            ],
            out_specs=[pl.BlockSpec((1, 64, COLS), lambda i, s: (i, 0, 0))] * 2,
            scratch_shapes=[pltpu.VMEM((128, 1024), BF), pltpu.VMEM((3, 128, 256), BF)],
        ),
        out_shape=[shape((4, 64, COLS)), shape((4, 64, COLS), F32)],
        compiler_params=params(24),
        name="project",
    )(scalars, x4, down, weight, up, residual)


def pair_sum_kernel(keep_ref, got_ref, *outs):
    for k in range(3):
        outs[k][...] = (keep_ref[k] + got_ref[k].astype(F32)).astype(BF)


def pair_sum(keep, got):
    spec = pl.BlockSpec((3, 64, COLS), lambda i: (0, 0, 0))
    return pl.pallas_call(
        pair_sum_kernel,
        grid=(1,),
        in_specs=[spec, spec],
        out_specs=[pl.BlockSpec((64, COLS), lambda i: (0, 0))] * 3,
        out_shape=[shape((64, COLS))] * 3,
        compiler_params=params(16),
        name="pair_sum",
    )(keep, got)


def assemble_kernel(s, *refs):
    out_ref = refs[8]
    x, core = s[1], s[4]
    out_ref[:, 512:] = jnp.zeros((COLS, WIDE - 512), BF)
    for k in range(4):
        for other in range(2):
            zh = (core + other) % 2
            row = pl.multiple_of(((x + k) % 4) * 224 + zh * 112, 16)
            out_ref[pl.ds(row, 112), 0:576] = refs[4 * other + k][...]


def assemble(scalars, blocks):
    return pl.pallas_call(
        assemble_kernel,
        in_specs=[pl.BlockSpec(memory_space=pltpu.SMEM)] + [pl.BlockSpec(memory_space=pltpu.VMEM)] * 8,
        out_specs=pl.BlockSpec(memory_space=pltpu.VMEM),
        out_shape=shape((COLS, WIDE)),
        compiler_params=params(16),
        name="assemble",
    )(scalars, *blocks)


def latent_kernel(s, keep_ref, got_ref, r1, r2, r3, gain_ref, w_ref, part_ref, h0, h1, h2, h3, hid):
    zl = s[3]
    total = keep_ref[0] + got_ref[0].astype(F32) + r1[...].astype(F32) + r2[...].astype(F32) + r3[...].astype(F32)
    hidden = total.astype(BF)
    hid[...] = hidden
    for k, out in enumerate((h0, h1, h2, h3)):
        out[...] = hid[pl.ds(pl.multiple_of(((zl + k) % 4) * 16, 16), 16), :]
    wide = hidden.astype(F32)
    squares = jnp.sum(wide * wide, axis=1, keepdims=True)
    part = dot((wide * gain_ref[...].astype(F32)).astype(BF), w_ref[...])
    lane = lax.broadcasted_iota(jnp.int32, (64, 128), 1)
    high = squares.astype(BF).astype(F32)
    tail = jnp.where(lane == 64, high, jnp.where(lane == 65, squares - high, part[:, 512:]))
    part_ref[:, :512] = part[:, :512].astype(BF)
    part_ref[:, 512:] = tail.astype(BF)


def latent_part(scalars, keep, got, r1, r2, r3, gain, weight):
    own = pl.BlockSpec((1, 64, COLS), lambda i, s: (3, 0, 0))
    block = pl.BlockSpec((64, COLS), lambda i, s: (0, 0))
    small = pl.BlockSpec((16, COLS), lambda i, s: (0, 0))
    return pl.pallas_call(
        latent_kernel,
        grid_spec=pltpu.PrefetchScalarGridSpec(
            num_scalar_prefetch=1,
            grid=(1,),
            in_specs=[
                own,
                own,
                block,
                block,
                block,
                pl.BlockSpec((1, COLS), lambda i, s: (0, s[3])),
                pl.BlockSpec((COLS, WIDE), lambda i, s: (0, 0)),
            ],
            out_specs=[pl.BlockSpec((64, WIDE), lambda i, s: (0, 0))] + [small] * 4,
            scratch_shapes=[pltpu.VMEM((64, COLS), BF)],
        ),
        out_shape=[shape((64, WIDE))] + [shape((16, COLS))] * 4,
        compiler_params=params(24),
        name="latent_part",
    )(scalars, keep, got, r1, r2, r3, gain, weight)


def rows_kernel(p0, p1, p2, p3, cos_ref, sin_ref, gain_ref, out_ref):
    total = p0[...].astype(F32) + p1[...].astype(F32) + p2[...].astype(F32) + p3[...].astype(F32)
    tail = total[:, 512:]
    inverse = lax.rsqrt((tail[:, 64:65] + tail[:, 65:66]) / 3584.0 + 1e-06)
    latent = total[:, :512] * inverse
    mean_square = jnp.mean(latent * latent, axis=1, keepdims=True)
    out_ref[:, :512] = (latent * lax.rsqrt(mean_square + 1e-06) * gain_ref[...].astype(F32)).astype(BF)
    rope = tail[:, :64] * inverse
    swapped = jnp.concatenate([rope[:, 32:], rope[:, :32]], axis=1)
    rotated = rope * cos_ref[...] + swapped * sin_ref[...]
    out_ref[:, 512:] = jnp.concatenate([rotated, jnp.zeros((64, 64), F32)], axis=1).astype(BF)


def kv_rows(parts, cosine, sine, gain):
    return pl.pallas_call(
        rows_kernel,
        out_shape=shape((64, WIDE)),
        compiler_params=params(16),
        name="kv_rows",
    )(*parts, cosine, sine, gain)


def attend_kernel(heads, s, seg, q0, q1, q2, q3, *refs):
    keys = refs[:8]
    up_ref = refs[8]
    outs = refs[9:13]
    kv, bias, stats = refs[13:]
    step = pl.program_id(0)
    y, x, zh, core = s[0], s[1], s[2], s[4]
    factor = math.log2(math.e) / math.sqrt(NOPE + ROPE)

    @pl.when(step == 0)
    def _():
        for k in range(4):
            for other in range(2):
                kv[k * 256 + other * 128 : k * 256 + other * 128 + 128, :] = keys[4 * other + k][...]
        lane = lax.broadcasted_iota(jnp.int32, (1, 1024), 1)
        group = lane // 256 * 4 + (lane // 64) % 2 * 2 + (lane // 32) % 2
        segment = jnp.zeros((1, 1024), jnp.int32)
        for k in range(4):
            for a in range(2):
                for half in range(2):
                    ctx = ((y + k) % 4) * 8 + x * 2 + (zh + a) % 2
                    segment = jnp.where(group == k * 4 + a * 2 + half, seg[2 * ctx + half], segment)
        side = ((lane // 128) % 2 + core) % 2
        place = segment * 64 + (lane // 16) % 2 * 32 + side * 16 + lane % 16
        row = lax.broadcasted_iota(jnp.int32, (64, 1024), 0)
        for j in range(4):
            ctx = y * 8 + ((x + j) % 4) * 2 + zh
            for half in range(2):
                mine = row + seg[2 * ctx + half] * 64
                start = j * 128 + half * 64
                bias[start : start + 64, :] = jnp.where(place <= mine, 0.0, -1e30)
        stats[...] = jnp.zeros_like(stats)

    lane = lax.broadcasted_iota(jnp.int32, (128, 128), 1)
    for side in range(2):
        lifted = dot(kv[:, :LATENT], up_ref[:, side * 256 : side * 256 + 256]).astype(BF)
        key = jnp.concatenate([lifted[:, :NOPE], kv[:, LATENT:]], axis=1)
        value = lifted[:, NOPE:]
        head = 2 * step + side
        for j, q in enumerate((q0, q1, q2, q3)):
            first = side * 192
            query = jnp.concatenate([q[:, first : first + 192], jnp.zeros((128, 64), BF)], axis=1)
            scores = lax.dot_general(query, key, (((1,), (1,)), ((), ())), preferred_element_type=F32)
            scores = scores + bias[j * 128 : j * 128 + 128, :]
            top = jnp.max(scores, axis=1, keepdims=True)
            weights = jnp.exp2((scores - top) * factor)
            total = jnp.sum(weights, axis=1, keepdims=True)
            mixed = dot(weights.astype(BF), value) / total
            outs[j][:, pl.ds(pl.multiple_of(head * 128, 128), 128)] = mixed.astype(BF)
            level = top * factor + jnp.log2(total)
            high = level.astype(BF).astype(F32)
            middle = (level - high).astype(BF).astype(F32)
            low = level - high - middle
            stats[j] = stats[j] + jnp.where(
                lane == head,
                high,
                jnp.where(lane == head + 8, middle, jnp.where(lane == head + 16, low, 0.0)),
            )

    @pl.when(step == pl.num_programs(0) - 1)
    def _():
        for j in range(4):
            outs[j][:, heads * 128 :] = stats[j].astype(BF)


def attend(scalars, seg, queries, keys, up, first_pair, pairs):
    heads = 2 * pairs
    width = heads * 128 + 128
    return pl.pallas_call(
        functools.partial(attend_kernel, heads),
        grid_spec=pltpu.PrefetchScalarGridSpec(
            num_scalar_prefetch=2,
            grid=(pairs,),
            in_specs=[pl.BlockSpec((128, 384), lambda i, s, g: (0, i + first_pair))] * 4
            + [pl.BlockSpec((128, WIDE), lambda i, s, g: (0, 0))] * 8
            + [pl.BlockSpec((LATENT, 512), lambda i, s, g: (0, i + first_pair))],
            out_specs=[pl.BlockSpec((128, width), lambda i, s, g: (0, 0))] * 4,
            scratch_shapes=[
                pltpu.VMEM((1024, WIDE), BF),
                pltpu.VMEM((512, 1024), F32),
                pltpu.VMEM((4, 128, 128), F32),
            ],
        ),
        out_shape=[shape((128, width))] * 4,
        compiler_params=params(48),
        name="attend",
    )(scalars, seg, *queries, *keys, up)


def merge_kernel(heads, *refs):
    out_ref = refs[-1]
    for part in range(2):
        group = refs[4 * part : 4 * part + 4]
        for head in range(heads):
            levels = []
            for ref in group:
                stat = ref[:, heads * 128 :].astype(F32)
                levels.append(stat[:, head : head + 1] + stat[:, head + 8 : head + 9] + stat[:, head + 16 : head + 17])
            top = functools.reduce(jnp.maximum, levels)
            scales = [jnp.exp2(level - top) for level in levels]
            total = sum(scales[1:], scales[0])
            mixed = sum(
                ref[:, head * 128 : head * 128 + 128].astype(F32) * (scale / total)
                for ref, scale in zip(group, scales)
            )
            column = (part * heads + head) * 128
            out_ref[:, column : column + 128] = mixed.astype(BF)


def merge(first, second):
    return pl.pallas_call(
        functools.partial(merge_kernel, 4),
        out_shape=shape((128, HEADS * VDIM)),
        compiler_params=params(16),
        name="merge",
    )(*first, *second)


def hidden_kernel(s, h0, h1, h2, h3, out_ref):
    zl = s[3]
    for k, ref in enumerate((h0, h1, h2, h3)):
        column = pl.multiple_of(((zl + 4 - k) % 4) * COLS, 128)
        out_ref[:, pl.ds(column, COLS)] = ref[...]


def hidden_rows(scalars, blocks):
    return pl.pallas_call(
        hidden_kernel,
        in_specs=[pl.BlockSpec(memory_space=pltpu.SMEM)] + [pl.BlockSpec(memory_space=pltpu.VMEM)] * 4,
        out_specs=pl.BlockSpec(memory_space=pltpu.VMEM),
        out_shape=shape((16, 4 * COLS)),
        compiler_params=params(16),
        name="hidden_rows",
    )(scalars, *blocks)


def rotary_tables(segment_ordering, ctx, core):
    row = jnp.arange(64, dtype=jnp.int32)
    token = row // 16 * 32 + core * 16 + row % 16
    pair = lax.dynamic_slice_in_dim(segment_ordering, 2 * ctx, 2)
    places = jnp.where(token < 64, pair[0], pair[1]) * 64 + token % 64
    ladder = jnp.arange(ROPE // 2, dtype=F32)
    inverse = jnp.exp(ladder * (-2.0 * math.log(10000.0) / ROPE))
    angles = places.astype(F32)[:, None] * inverse[None, :]
    cosine, sine = jnp.cos(angles), jnp.sin(angles)
    return jnp.concatenate([cosine, cosine], axis=1), jnp.concatenate([-sine, sine], axis=1)


def body(
    segment_ordering,
    attention_input,
    residual,
    queries,
    output_weight,
    adapter_down_factor,
    adapter_up_factor,
    input_norm_gain,
    latent_key_weight,
    latent_norm_gain,
    latent_up_weight,
):
    y, x, zh, zl, core = (lax.axis_index(name) for name in AXES)
    scalars = jnp.stack([y, x, zh, zl, core, 0, 0, 0] + [(zl + k) % 4 for k in ORDER]).astype(jnp.int32)

    own = transposed_blocks(latent_key_weight)
    lined = [own] + [shift(own, "x", -k) for k in (1, 2, 3)]
    weight = assemble(scalars, lined + [swap(block, "core") for block in lined])
    asked = [queries] + [shift(queries, "x", -k) for k in (1, 2, 3)]
    cosine, sine = rotary_tables(segment_ordering, y * 8 + x * 2 + zh, core)

    send, keep = project(
        scalars,
        attention_input.reshape(4, 2, 16, 1024),
        adapter_down_factor,
        output_weight,
        adapter_up_factor,
        residual,
    )
    got = swap(send, "core")
    sums = pair_sum(keep, got)
    r2, r1, r3 = (shift(value, "zl", k) for value, k in zip(sums, ORDER))
    part, h0, h1, h2, h3 = latent_part(
        scalars, keep, got, r1, r2, r3, input_norm_gain.reshape(1, -1), weight
    )
    parts = [part] + [shift(part, "zl", k) for k in (1, 2, 3)]
    rows = kv_rows(parts, cosine, sine, latent_norm_gain.reshape(1, -1))
    both = jnp.concatenate([rows, swap(rows, "zh")], axis=0)
    column = [both] + [shift(both, "y", -k) for k in (1, 2, 3)]
    keys = column + [swap(value, "core") for value in column]

    hidden = hidden_rows(scalars, [h0] + [shift(h, "zl", k) for k, h in ((1, h1), (2, h2), (3, h3))])

    halves = []
    for first in (0, 2):
        partial = attend(scalars, segment_ordering, asked, keys, latent_up_weight, first, 2)
        halves.append([partial[0]] + [shift(partial[j], "x", j) for j in (1, 2, 3)])
    return hidden, merge(*halves)


def solution(mesh):
    split = Mesh(mesh.devices.reshape(SIZES), AXES)
    ctx, tp = ("y", "x", "zh"), ("zl", "core")
    in_specs = (
        P(),
        P(ctx, tp),
        P(ctx + tp, None),
        P(ctx, tp),
        P(tp, None),
        P(tp, None),
        P(),
        P(),
        P(ctx, None),
        P(),
        P(None, tp),
    )
    out_specs = (P(ctx + tp, None), P(ctx, tp))
    return jax.shard_map(body, mesh=split, in_specs=in_specs, out_specs=out_specs, check_vma=False)
```

time: 388 us -> 127 us (0.33)
  the two profiles are of different devices: /device:TPU:24 before, /device:TPU:6 now
where the time goes in v1:
time: 127 us
  starting transfers between devices  47.2 us (37%)
  waiting for transfers between devices  36 us (28%)
  Pallas kernels  32.9 us (26%)
  local copies, waits for them, and re-layouts  8.25 us (6%)
  other arithmetic  1.61 us (1%)
    ppermute x24, starting transfers between devices, shift(): return lax.ppermute(value, axis, [(i, (i + k) % 4) for i in range(4)])  34.9 us
    ppermute x24, waiting for transfers between devices, shift(): return lax.ppermute(value, axis, [(i, (i + k) % 4) for i in range(4)])  29.6 us
    pallas_call x2, Pallas kernels, attend(): pl.pallas_call(functools.partial(attend_kernel, heads), grid_spec=pltpu.P...  22.7 us
    ppermute x10, starting transfers between devices, swap(): return lax.ppermute(value, axis, [(0, 1), (1, 0)])  10.7 us
    unnamed x20, local copies, waits for them, and re-layouts  7.5 us
    ppermute x10, waiting for transfers between devices, swap(): return lax.ppermute(value, axis, [(0, 1), (1, 0)])  6.39 us
    pallas_call x1, Pallas kernels, project(): pl.pallas_call(project_kernel, grid_spec=pltpu.PrefetchScalarGridSpec(num...  4.36 us
    pallas_call x1, Pallas kernels, merge(): pl.pallas_call(functools.partial(merge_kernel, 4), out_shape=shape((128,...  2.77 us
  transfers between devices with their start and end apart: 35, of which 15 were waited for; matrix products, arithmetic and copies ran while one was open for 2% of the time, Pallas kernels for 15%

profile of v1, /device:TPU:6, one launch (start us, length us, event | category | flops | bytes accessed | tf_op | source)
XLA Modules:
  0.0 126.8 jit_solution(16320847138496248141)
XLA Ops:
  0.6 1.6 %collective-permute-start.4 = (bf16[112,576]{1,0:T(8,128)(2,1)}, bf16[112,576]{1,0:T(8,128)(2,1)S(1)}, u32[]{:S(2)}, u32[]{:S(2)}) collective-permute-start(bf16[112,576]{1,0:T(8,128)(2,1)} %param.19), channel_id=1, source_target_pairs={{0,0},{8,1},{64,2},{72,3},{128,4},{136,5},{192,6},{200,7},{1,8},{9... | collective-permute-start | bytes 387080 | tf_op jit(solution)/shard_map/ppermute | solution.py:50
  2.3 3.1 %copy-done.1 = bf16[1024,3584]{1,0:T(8,128)(2,1)S(1)} copy-done((bf16[1024,3584]{1,0:T(8,128)(2,1)S(1)}, bf16[1024,3584]{1,0:T(8,128)(2,1)}, u32[]{:S(2)}) %copy-start.1) | copy-done | bytes 7340056
  5.4 1.5 %copy-done.2 = bf16[256,3584]{1,0:T(8,128)(2,1)S(1)} copy-done((bf16[256,3584]{1,0:T(8,128)(2,1)S(1)}, bf16[256,3584]{1,0:T(8,128)(2,1)}, u32[]{:S(2)}) %copy-start.2) | copy-done | bytes 1835032
  6.9 1.0 copy-done.4
  7.9 0.9 copy-done.5
  8.9 0.9 copy-done.6
  9.8 4.4 %project.1 = (bf16[4,64,896]{2,1,0:T(8,128)(2,1)S(1)}, f32[4,64,896]{2,1,0:T(8,128)S(1)}) custom-call(s32[12]{0:T(128)S(1)} %stack.39.s, bf16[4,2,16,1024]{3,2,1,0:T(8,128)(2,1)S(1)} %bitcast.12, bf16[1024,256]{1,0:T(8,128)(2,1)S(1)} %copy-done.4, bf16[1024,3584]{1,0:T(8,128)(2,1)S(1)} %copy-done.1, bf16[256,3584]{1,0:T(8,128)(2,1)S(1)} %copy-done.2, ...), custom_call_target="tpu_custom_call" | custom-call | tf_op jit(solution)/shard_map/project/pallas_call | solution.py:87
  14.1 7.8 %collective-permute-start = (bf16[4,64,896]{2,1,0:T(8,128)(2,1)S(1)}, bf16[4,64,896]{2,1,0:T(8,128)(2,1)S(1)}, u32[]{:S(2)}, u32[]{:S(2)}) collective-permute-start(bf16[4,64,896]{2,1,0:T(8,128)(2,1)S(1)} %get-tuple-element.21), channel_id=1, source_target_pairs={{0,1},{1,0},{2,3},{3,2},{4,5},{5,4},{6,7},{7,6},{8,9},{9,8},{10,11... | collective-permute-start | bytes 1376264 | tf_op jit(solution)/shard_map/ppermute | solution.py:35
  21.9 1.4 %collective-permute-start.6 = (bf16[112,576]{1,0:T(8,128)(2,1)S(1)}, bf16[112,576]{1,0:T(8,128)(2,1)S(1)}, u32[]{:S(2)}, u32[]{:S(2)}) collective-permute-start(bf16[112,576]{1,0:T(8,128)(2,1)S(1)} %collective-permute-done.4.refs_0_), channel_id=1, source_target_pairs={{0,32},{16,48},{32,0},{48,16},{1,33},{17,49},{33,1},{49,17},{2,34}... | collective-permute-start | bytes 387080 | tf_op jit(solution)/shard_map/ppermute | solution.py:31
  23.3 2.1 %collective-permute-start.7 = (bf16[112,576]{1,0:T(8,128)(2,1)S(1)}, bf16[112,576]{1,0:T(8,128)(2,1)S(1)}, u32[]{:S(2)}, u32[]{:S(2)}) collective-permute-start(bf16[112,576]{1,0:T(8,128)(2,1)S(1)} %collective-permute-done.4.refs_0_), channel_id=1, source_target_pairs={{0,16},{16,32},{32,48},{48,0},{1,17},{17,33},{33,49},{49,1},{2,18}... | collective-permute-start | bytes 387080 | tf_op jit(solution)/shard_map/ppermute | solution.py:31
  26.1 4.0 %collective-permute-done.6.refs_2_ = bf16[112,576]{1,0:T(8,128)(2,1)S(1)} collective-permute-done((bf16[112,576]{1,0:T(8,128)(2,1)S(1)}, bf16[112,576]{1,0:T(8,128)(2,1)S(1)}, u32[]{:S(2)}, u32[]{:S(2)}) %collective-permute-start.6) | collective-permute-done | bytes 129056 | tf_op jit(solution)/shard_map/ppermute | solution.py:31
  30.6 1.3 %fusion.7 = f32[64]{0:T(128)S(1)} fusion(s32[]{:T(128)} %bitcast.11, s32[]{:T(128)} %bitcast.10, s32[]{:T(128)S(6)} %mul.54), kind=kLoop, calls=%fused_computation.21 | loop fusion | flops 1984 | bytes 268 | tf_op jit(solution)/shard_map/convert_element_type | solution.py:357
  31.9 0.9 collective-permute-done.5.refs_1_
  32.8 0.8 collective-permute-start.15
  34.0 1.6 %collective-permute-start.1 = (bf16[64,896]{1,0:T(8,128)(2,1)S(1)}, bf16[64,896]{1,0:T(8,128)(2,1)S(1)}, u32[]{:S(2)}, u32[]{:S(2)}) collective-permute-start(bf16[64,896]{1,0:T(8,128)(2,1)S(1)} %get-tuple-element.22), channel_id=1, source_target_pairs={{0,2},{2,4},{4,6},{6,0},{1,3},{3,5},{5,7},{7,1},{8,10},{10,12},{12... | collective-permute-start | bytes 344072 | tf_op jit(solution)/shard_map/ppermute | solution.py:31
  35.6 2.0 %collective-permute-start.2 = (bf16[64,896]{1,0:T(8,128)(2,1)S(1)}, bf16[64,896]{1,0:T(8,128)(2,1)S(1)}, u32[]{:S(2)}, u32[]{:S(2)}) collective-permute-start(bf16[64,896]{1,0:T(8,128)(2,1)S(1)} %get-tuple-element.23), channel_id=1, source_target_pairs={{0,4},{2,6},{4,0},{6,2},{1,5},{3,7},{5,1},{7,3},{8,12},{10,14},{12... | collective-permute-start | bytes 344072 | tf_op jit(solution)/shard_map/ppermute | solution.py:31
  37.6 2.5 %collective-permute-start.3 = (bf16[64,896]{1,0:T(8,128)(2,1)S(1)}, bf16[64,896]{1,0:T(8,128)(2,1)S(1)}, u32[]{:S(2)}, u32[]{:S(2)}) collective-permute-start(bf16[64,896]{1,0:T(8,128)(2,1)S(1)} %get-tuple-element.24), channel_id=1, source_target_pairs={{0,6},{2,0},{4,2},{6,4},{1,7},{3,1},{5,3},{7,5},{8,14},{10,8},{12,... | collective-permute-start | bytes 344072 | tf_op jit(solution)/shard_map/ppermute | solution.py:31
  40.4 2.2 %collective-permute-start.16 = (bf16[128,1536]{1,0:T(8,128)(2,1)S(1)}, bf16[128,1536]{1,0:T(8,128)(2,1)S(1)}, u32[]{:S(2)}, u32[]{:S(2)}) collective-permute-start(bf16[128,1536]{1,0:T(8,128)(2,1)S(1)} %copy-done.3), channel_id=1, source_target_pairs={{0,32},{16,48},{32,0},{48,16},{1,33},{17,49},{33,1},{49,17},{2,34}... | collective-permute-start | bytes 1179656 | tf_op jit(solution)/shard_map/ppermute | solution.py:31
  42.6 0.7 assemble.1.w_ref
  43.3 2.9 %collective-permute-done.2.r2 = bf16[64,896]{1,0:T(8,128)(2,1)S(1)} collective-permute-done((bf16[64,896]{1,0:T(8,128)(2,1)S(1)}, bf16[64,896]{1,0:T(8,128)(2,1)S(1)}, u32[]{:S(2)}, u32[]{:S(2)}) %collective-permute-start.2) | collective-permute-done | bytes 114720 | tf_op jit(solution)/shard_map/ppermute | solution.py:31
  46.2 0.9 latent_part.1
  47.1 3.0 %collective-permute-start.18 = (bf16[64,640]{1,0:T(8,128)(2,1)S(1)}, bf16[64,640]{1,0:T(8,128)(2,1)S(1)}, u32[]{:S(2)}, u32[]{:S(2)}) collective-permute-start(bf16[64,640]{1,0:T(8,128)(2,1)S(1)} %get-tuple-element.29.p0), channel_id=1, source_target_pairs={{0,2},{2,4},{4,6},{6,0},{1,3},{3,5},{5,7},{7,1},{8,10},{10,12},{12... | collective-permute-start | bytes 245768 | tf_op jit(solution)/shard_map/ppermute | solution.py:31
  50.1 2.3 %collective-permute-start.19 = (bf16[64,640]{1,0:T(8,128)(2,1)S(1)}, bf16[64,640]{1,0:T(8,128)(2,1)S(1)}, u32[]{:S(2)}, u32[]{:S(2)}) collective-permute-start(bf16[64,640]{1,0:T(8,128)(2,1)S(1)} %get-tuple-element.29.p0), channel_id=1, source_target_pairs={{0,4},{2,6},{4,0},{6,2},{1,5},{3,7},{5,1},{7,3},{8,12},{10,14},{12... | collective-permute-start | bytes 245768 | tf_op jit(solution)/shard_map/ppermute | solution.py:31
  52.6 2.5 %collective-permute-done.18.p1 = bf16[64,640]{1,0:T(8,128)(2,1)S(1)} collective-permute-done((bf16[64,640]{1,0:T(8,128)(2,1)S(1)}, bf16[64,640]{1,0:T(8,128)(2,1)S(1)}, u32[]{:S(2)}, u32[]{:S(2)}) %collective-permute-start.18) | collective-permute-done | bytes 81952 | tf_op jit(solution)/shard_map/ppermute | solution.py:31
  55.1 2.5 %collective-permute-done.19.p2 = bf16[64,640]{1,0:T(8,128)(2,1)S(1)} collective-permute-done((bf16[64,640]{1,0:T(8,128)(2,1)S(1)}, bf16[64,640]{1,0:T(8,128)(2,1)S(1)}, u32[]{:S(2)}, u32[]{:S(2)}) %collective-permute-start.19) | collective-permute-done | bytes 81952 | tf_op jit(solution)/shard_map/ppermute | solution.py:31
  58.3 2.2 %collective-permute-start.21 = (bf16[64,640]{1,0:T(8,128)(2,1)S(1)}, bf16[64,640]{1,0:T(8,128)(2,1)S(1)}, u32[]{:S(2)}, u32[]{:S(2)}) collective-permute-start(bf16[64,640]{1,0:T(8,128)(2,1)S(1)} %kv_rows.1), channel_id=1, source_target_pairs={{0,8},{8,0},{1,9},{9,1},{2,10},{10,2},{3,11},{11,3},{4,12},{12,4},... | collective-permute-start | bytes 245768 | tf_op jit(solution)/shard_map/ppermute | solution.py:35
  60.4 2.4 %collective-permute-start.17 = (bf16[128,1536]{1,0:T(8,128)(2,1)S(1)}, bf16[128,1536]{1,0:T(8,128)(2,1)S(1)}, u32[]{:S(2)}, u32[]{:S(2)}) collective-permute-start(bf16[128,1536]{1,0:T(8,128)(2,1)S(1)} %copy-done.3), channel_id=1, source_target_pairs={{0,16},{16,32},{32,48},{48,0},{1,17},{17,33},{33,49},{49,1},{2,18}... | collective-permute-start | bytes 1179656 | tf_op jit(solution)/shard_map/ppermute | solution.py:31
  62.8 5.0 %collective-permute-done.21 = bf16[64,640]{1,0:T(8,128)(2,1)S(1)} collective-permute-done((bf16[64,640]{1,0:T(8,128)(2,1)S(1)}, bf16[64,640]{1,0:T(8,128)(2,1)S(1)}, u32[]{:S(2)}, u32[]{:S(2)}) %collective-permute-start.21) | collective-permute-done | bytes 81952 | tf_op jit(solution)/shard_map/ppermute | solution.py:35
  67.8 0.8 collective-permute-start.22
  68.7 1.4 %collective-permute-start.23 = (bf16[128,640]{1,0:T(8,128)(2,1)S(1)}, bf16[128,640]{1,0:T(8,128)(2,1)S(1)}, u32[]{:S(2)}, u32[]{:S(2)}) collective-permute-start(bf16[128,640]{1,0:T(8,128)(2,1)S(1)} %pad_maximum_fusion.refs_0_), channel_id=1, source_target_pairs={{0,128},{64,192},{128,0},{192,64},{1,129},{65,193},{129,1},{193,65... | collective-permute-start | bytes 491528 | tf_op jit(solution)/shard_map/ppermute | solution.py:31
  70.3 4.5 %collective-permute-done.22.refs_1_ = bf16[128,640]{1,0:T(8,128)(2,1)S(1)} collective-permute-done((bf16[128,640]{1,0:T(8,128)(2,1)S(1)}, bf16[128,640]{1,0:T(8,128)(2,1)S(1)}, u32[]{:S(2)}, u32[]{:S(2)}) %collective-permute-start.22) | collective-permute-done | bytes 163872 | tf_op jit(solution)/shard_map/ppermute | solution.py:31
  74.8 2.3 %collective-permute-done.23.refs_2_ = bf16[128,640]{1,0:T(8,128)(2,1)S(1)} collective-permute-done((bf16[128,640]{1,0:T(8,128)(2,1)S(1)}, bf16[128,640]{1,0:T(8,128)(2,1)S(1)}, u32[]{:S(2)}, u32[]{:S(2)}) %collective-permute-start.23) | collective-permute-done | bytes 163872 | tf_op jit(solution)/shard_map/ppermute | solution.py:31
  77.1 1.7 %collective-permute-done.24.refs_3_ = bf16[128,640]{1,0:T(8,128)(2,1)S(1)} collective-permute-done((bf16[128,640]{1,0:T(8,128)(2,1)S(1)}, bf16[128,640]{1,0:T(8,128)(2,1)S(1)}, u32[]{:S(2)}, u32[]{:S(2)}) %collective-permute-start.24) | collective-permute-done | bytes 163872 | tf_op jit(solution)/shard_map/ppermute | solution.py:31
  78.9 1.4 %collective-permute-done.28.refs_7_ = bf16[128,640]{1,0:T(8,128)(2,1)S(1)} collective-permute-done((bf16[128,640]{1,0:T(8,128)(2,1)S(1)}, bf16[128,640]{1,0:T(8,128)(2,1)S(1)}, u32[]{:S(2)}, u32[]{:S(2)}) %collective-permute-start.28) | collective-permute-done | bytes 163872 | tf_op jit(solution)/shard_map/ppermute | solution.py:35
  80.2 11.4 %attend.3 = (bf16[128,640]{1,0:T(8,128)(2,1)S(1)}, bf16[128,640]{1,0:T(8,128)(2,1)S(1)}, bf16[128,640]{1,0:T(8,128)(2,1)S(1)}, bf16[128,640]{1,0:T(8,128)(2,1)S(1)}) custom-call(s32[12]{0:T(128)S(1)} %stack.39.s, s32[64]{0:T(128)S(1)} %copy-done.7, bf16[128,1536]{1,0:T(8,128)(2,1)S(1)} %copy-done.3, bf16[128,1536]{1,0:T(8,128)(2,1)S(1)} %collective-permute-done.15.q1, ...), custom_call_target="tpu_custom_call" | custom-call | tf_op jit(solution)/shard_map/attend/pallas_call | solution.py:282
  91.6 2.5 %collective-permute-start.32 = (bf16[128,640]{1,0:T(8,128)(2,1)S(1)}, bf16[128,640]{1,0:T(8,128)(2,1)S(1)}, u32[]{:S(2)}, u32[]{:S(2)}) collective-permute-start(bf16[128,640]{1,0:T(8,128)(2,1)S(1)} %get-tuple-element.35), channel_id=1, source_target_pairs={{0,16},{16,32},{32,48},{48,0},{1,17},{17,33},{33,49},{49,1},{2,18}... | collective-permute-start | bytes 491528 | tf_op jit(solution)/shard_map/ppermute | solution.py:31
  94.1 0.8 collective-permute-start.12
  94.8 1.9 %collective-permute-start.13 = (bf16[16,896]{1,0:T(8,128)(2,1)S(1)}, bf16[16,896]{1,0:T(8,128)(2,1)S(1)}, u32[]{:S(2)}, u32[]{:S(2)}) collective-permute-start(bf16[16,896]{1,0:T(8,128)(2,1)S(1)} %get-tuple-element.27), channel_id=1, source_target_pairs={{0,4},{2,6},{4,0},{6,2},{1,5},{3,7},{5,1},{7,3},{8,12},{10,14},{12... | collective-permute-start | bytes 86024 | tf_op jit(solution)/shard_map/ppermute | solution.py:31
  96.7 1.2 collective-permute-start.14
  97.9 1.2 collective-permute-start.33
  99.0 11.4 %attend.2 = (bf16[128,640]{1,0:T(8,128)(2,1)S(1)}, bf16[128,640]{1,0:T(8,128)(2,1)S(1)}, bf16[128,640]{1,0:T(8,128)(2,1)S(1)}, bf16[128,640]{1,0:T(8,128)(2,1)S(1)}) custom-call(s32[12]{0:T(128)S(1)} %stack.39.s, s32[64]{0:T(128)S(1)} %copy-done.7, bf16[128,1536]{1,0:T(8,128)(2,1)S(1)} %copy-done.3, bf16[128,1536]{1,0:T(8,128)(2,1)S(1)} %collective-permute-done.15.q1, ...), custom_call_target="tpu_custom_call" | custom-call | tf_op jit(solution)/shard_map/attend/pallas_call | solution.py:282
  110.5 3.2 %collective-permute-start.29 = (bf16[128,640]{1,0:T(8,128)(2,1)S(1)}, bf16[128,640]{1,0:T(8,128)(2,1)S(1)}, u32[]{:S(2)}, u32[]{:S(2)}) collective-permute-start(bf16[128,640]{1,0:T(8,128)(2,1)S(1)} %get-tuple-element.31), channel_id=1, source_target_pairs={{0,16},{16,32},{32,48},{48,0},{1,17},{17,33},{33,49},{49,1},{2,18}... | collective-permute-start | bytes 491528 | tf_op jit(solution)/shard_map/ppermute | solution.py:31
  113.7 1.2 collective-permute-start.30
  114.9 1.2 hidden_rows.1
  116.1 3.5 %collective-permute-done.34.refs_7_ = bf16[128,640]{1,0:T(8,128)(2,1)S(1)} collective-permute-done((bf16[128,640]{1,0:T(8,128)(2,1)S(1)}, bf16[128,640]{1,0:T(8,128)(2,1)S(1)}, u32[]{:S(2)}, u32[]{:S(2)}) %collective-permute-start.34) | collective-permute-done | bytes 163872 | tf_op jit(solution)/shard_map/ppermute | solution.py:31
  119.7 2.1 %collective-permute-done.30.refs_2_ = bf16[128,640]{1,0:T(8,128)(2,1)S(1)} collective-permute-done((bf16[128,640]{1,0:T(8,128)(2,1)S(1)}, bf16[128,640]{1,0:T(8,128)(2,1)S(1)}, u32[]{:S(2)}, u32[]{:S(2)}) %collective-permute-start.30) | collective-permute-done | bytes 163872 | tf_op jit(solution)/shard_map/ppermute | solution.py:31
  121.8 2.3 %collective-permute-done.31.refs_3_ = bf16[128,640]{1,0:T(8,128)(2,1)S(1)} collective-permute-done((bf16[128,640]{1,0:T(8,128)(2,1)S(1)}, bf16[128,640]{1,0:T(8,128)(2,1)S(1)}, u32[]{:S(2)}, u32[]{:S(2)}) %collective-permute-start.31) | collective-permute-done | bytes 163872 | tf_op jit(solution)/shard_map/ppermute | solution.py:31
  124.1 2.8 %merge.1 = bf16[128,1024]{1,0:T(8,128)(2,1)} custom-call(bf16[128,640]{1,0:T(8,128)(2,1)S(1)} %get-tuple-element.30.refs_0_, bf16[128,640]{1,0:T(8,128)(2,1)S(1)} %collective-permute-done.29.refs_1_, bf16[128,640]{1,0:T(8,128)(2,1)S(1)} %collective-permute-done.30.refs_2_, bf16[128,640]{1,0:T(8,128)(2,1)S(1)} %collective-permute-done.31.refs_3_, ...), custom_call_target="tpu_custom_call" | custom-call | tf_op jit(solution)/shard_map/merge/pallas_call | solution.py:324
  (62 shorter events, 3.2 us)
Async XLA Ops:
  0.6 21.3 %collective-permute-start.4 = (bf16[112,576]{1,0:T(8,128)(2,1)}, bf16[112,576]{1,0:T(8,128)(2,1)S(1)}, u32[]{:S(2)}, u32[]{:S(2)}) collective-permute-start(bf16[112,576]{1,0:T(8,128)(2,1)} %param.19), channel_id=1, source_target_pairs={{0,0},{8,1},{64,2},{72,3},{128,4},{136,5},{192,6},{200,7},{1,8},{9... | collective-permute-start | bytes 387080 | tf_op jit(solution)/shard_map/ppermute | solution.py:50
  2.3 3.1 %copy-start.1 = (bf16[1024,3584]{1,0:T(8,128)(2,1)S(1)}, bf16[1024,3584]{1,0:T(8,128)(2,1)}, u32[]{:S(2)}) copy-start(bf16[1024,3584]{1,0:T(8,128)(2,1)} %wo_ref.1) | copy-start | bytes 22020100
  5.4 1.5 %copy-start.2 = (bf16[256,3584]{1,0:T(8,128)(2,1)S(1)}, bf16[256,3584]{1,0:T(8,128)(2,1)}, u32[]{:S(2)}) copy-start(bf16[256,3584]{1,0:T(8,128)(2,1)} %au_ref.1) | copy-start | bytes 5505028
  6.9 1.0 copy-start.4
  7.9 0.9 copy-start.5
  8.9 0.9 copy-start.6
  9.8 15.7 %copy-start.7 = (s32[64]{0:T(128)S(1)}, s32[64]{0:T(128)}, u32[]{:S(2)}) copy-start(s32[64]{0:T(128)} %seg.3) | copy-start | bytes 772
  9.8 23.1 %copy-start.3 = (bf16[128,1536]{1,0:T(8,128)(2,1)S(1)}, bf16[128,1536]{1,0:T(8,128)(2,1)}, u32[]{:S(2)}) copy-start(bf16[128,1536]{1,0:T(8,128)(2,1)} %q0.3) | copy-start | bytes 1179652
  9.8 30.6 %copy-start.8 = (bf16[3584]{0:T(1024)(128)(2,1)S(1)}, bf16[3584]{0:T(1024)(128)(2,1)}, u32[]{:S(2)}) copy-start(bf16[3584]{0:T(1024)(128)(2,1)} %param.18) | copy-start | bytes 21508
  14.1 19.5 %collective-permute-start = (bf16[4,64,896]{2,1,0:T(8,128)(2,1)S(1)}, bf16[4,64,896]{2,1,0:T(8,128)(2,1)S(1)}, u32[]{:S(2)}, u32[]{:S(2)}) collective-permute-start(bf16[4,64,896]{2,1,0:T(8,128)(2,1)S(1)} %get-tuple-element.21), channel_id=1, source_target_pairs={{0,1},{1,0},{2,3},{3,2},{4,5},{5,4},{6,7},{7,6},{8,9},{9,8},{10,11... | collective-permute-start | bytes 1376264 | tf_op jit(solution)/shard_map/ppermute | solution.py:35
  21.9 8.1 %collective-permute-start.6 = (bf16[112,576]{1,0:T(8,128)(2,1)S(1)}, bf16[112,576]{1,0:T(8,128)(2,1)S(1)}, u32[]{:S(2)}, u32[]{:S(2)}) collective-permute-start(bf16[112,576]{1,0:T(8,128)(2,1)S(1)} %collective-permute-done.4.refs_0_), channel_id=1, source_target_pairs={{0,32},{16,48},{32,0},{48,16},{1,33},{17,49},{33,1},{49,17},{2,34}... | collective-permute-start | bytes 387080 | tf_op jit(solution)/shard_map/ppermute | solution.py:31
  23.3 6.7 %collective-permute-start.7 = (bf16[112,576]{1,0:T(8,128)(2,1)S(1)}, bf16[112,576]{1,0:T(8,128)(2,1)S(1)}, u32[]{:S(2)}, u32[]{:S(2)}) collective-permute-start(bf16[112,576]{1,0:T(8,128)(2,1)S(1)} %collective-permute-done.4.refs_0_), channel_id=1, source_target_pairs={{0,16},{16,32},{32,48},{48,0},{1,17},{17,33},{33,49},{49,1},{2,18}... | collective-permute-start | bytes 387080 | tf_op jit(solution)/shard_map/ppermute | solution.py:31
  26.1 6.7 %collective-permute-start.5 = (bf16[112,576]{1,0:T(8,128)(2,1)S(1)}, bf16[112,576]{1,0:T(8,128)(2,1)S(1)}, u32[]{:S(2)}, u32[]{:S(2)}) collective-permute-start(bf16[112,576]{1,0:T(8,128)(2,1)S(1)} %collective-permute-done.4.refs_0_), channel_id=1, source_target_pairs={{0,48},{16,0},{32,16},{48,32},{1,49},{17,1},{33,17},{49,33},{2,50}... | collective-permute-start | bytes 387080 | tf_op jit(solution)/shard_map/ppermute | solution.py:31
  26.1 7.9 %collective-permute-start.8 = (bf16[112,576]{1,0:T(8,128)(2,1)S(1)}, bf16[112,576]{1,0:T(8,128)(2,1)S(1)}, u32[]{:S(2)}, u32[]{:S(2)}) collective-permute-start(bf16[112,576]{1,0:T(8,128)(2,1)S(1)} %collective-permute-done.4.refs_0_), channel_id=1, source_target_pairs={{0,1},{1,0},{2,3},{3,2},{4,5},{5,4},{6,7},{7,6},{8,9},{9,8},{10,11... | collective-permute-start | bytes 387080 | tf_op jit(solution)/shard_map/ppermute | solution.py:35
  30.1 5.6 %collective-permute-start.10 = (bf16[112,576]{1,0:T(8,128)(2,1)S(1)}, bf16[112,576]{1,0:T(8,128)(2,1)S(1)}, u32[]{:S(2)}, u32[]{:S(2)}) collective-permute-start(bf16[112,576]{1,0:T(8,128)(2,1)S(1)} %collective-permute-done.6.refs_2_), channel_id=1, source_target_pairs={{0,1},{1,0},{2,3},{3,2},{4,5},{5,4},{6,7},{7,6},{8,9},{9,8},{10,11... | collective-permute-start | bytes 387080 | tf_op jit(solution)/shard_map/ppermute | solution.py:35
  30.1 7.5 %collective-permute-start.11 = (bf16[112,576]{1,0:T(8,128)(2,1)S(1)}, bf16[112,576]{1,0:T(8,128)(2,1)S(1)}, u32[]{:S(2)}, u32[]{:S(2)}) collective-permute-start(bf16[112,576]{1,0:T(8,128)(2,1)S(1)} %collective-permute-done.7.refs_3_), channel_id=1, source_target_pairs={{0,1},{1,0},{2,3},{3,2},{4,5},{5,4},{6,7},{7,6},{8,9},{9,8},{10,11... | collective-permute-start | bytes 387080 | tf_op jit(solution)/shard_map/ppermute | solution.py:35
  32.8 37.2 %collective-permute-start.15 = (bf16[128,1536]{1,0:T(8,128)(2,1)S(1)}, bf16[128,1536]{1,0:T(8,128)(2,1)S(1)}, u32[]{:S(2)}, u32[]{:S(2)}) collective-permute-start(bf16[128,1536]{1,0:T(8,128)(2,1)S(1)} %copy-done.3), channel_id=1, source_target_pairs={{0,48},{16,0},{32,16},{48,32},{1,49},{17,1},{33,17},{49,33},{2,50}... | collective-permute-start | bytes 1179656 | tf_op jit(solution)/shard_map/ppermute | solution.py:31
  33.7 6.7 %collective-permute-start.9 = (bf16[112,576]{1,0:T(8,128)(2,1)S(1)}, bf16[112,576]{1,0:T(8,128)(2,1)S(1)}, u32[]{:S(2)}, u32[]{:S(2)}) collective-permute-start(bf16[112,576]{1,0:T(8,128)(2,1)S(1)} %collective-permute-done.5.refs_1_), channel_id=1, source_target_pairs={{0,1},{1,0},{2,3},{3,2},{4,5},{5,4},{6,7},{7,6},{8,9},{9,8},{10,11... | collective-permute-start | bytes 387080 | tf_op jit(solution)/shard_map/ppermute | solution.py:35
  34.0 9.3 %collective-permute-start.1 = (bf16[64,896]{1,0:T(8,128)(2,1)S(1)}, bf16[64,896]{1,0:T(8,128)(2,1)S(1)}, u32[]{:S(2)}, u32[]{:S(2)}) collective-permute-start(bf16[64,896]{1,0:T(8,128)(2,1)S(1)} %get-tuple-element.22), channel_id=1, source_target_pairs={{0,2},{2,4},{4,6},{6,0},{1,3},{3,5},{5,7},{7,1},{8,10},{10,12},{12... | collective-permute-start | bytes 344072 | tf_op jit(solution)/shard_map/ppermute | solution.py:31
  35.6 10.6 %collective-permute-start.2 = (bf16[64,896]{1,0:T(8,128)(2,1)S(1)}, bf16[64,896]{1,0:T(8,128)(2,1)S(1)}, u32[]{:S(2)}, u32[]{:S(2)}) collective-permute-start(bf16[64,896]{1,0:T(8,128)(2,1)S(1)} %get-tuple-element.23), channel_id=1, source_target_pairs={{0,4},{2,6},{4,0},{6,2},{1,5},{3,7},{5,1},{7,3},{8,12},{10,14},{12... | collective-permute-start | bytes 344072 | tf_op jit(solution)/shard_map/ppermute | solution.py:31
  37.6 8.6 %collective-permute-start.3 = (bf16[64,896]{1,0:T(8,128)(2,1)S(1)}, bf16[64,896]{1,0:T(8,128)(2,1)S(1)}, u32[]{:S(2)}, u32[]{:S(2)}) collective-permute-start(bf16[64,896]{1,0:T(8,128)(2,1)S(1)} %get-tuple-element.24), channel_id=1, source_target_pairs={{0,6},{2,0},{4,2},{6,4},{1,7},{3,1},{5,3},{7,5},{8,14},{10,8},{12,... | collective-permute-start | bytes 344072 | tf_op jit(solution)/shard_map/ppermute | solution.py:31
  40.4 29.9 %collective-permute-start.16 = (bf16[128,1536]{1,0:T(8,128)(2,1)S(1)}, bf16[128,1536]{1,0:T(8,128)(2,1)S(1)}, u32[]{:S(2)}, u32[]{:S(2)}) collective-permute-start(bf16[128,1536]{1,0:T(8,128)(2,1)S(1)} %copy-done.3), channel_id=1, source_target_pairs={{0,32},{16,48},{32,0},{48,16},{1,33},{17,49},{33,1},{49,17},{2,34}... | collective-permute-start | bytes 1179656 | tf_op jit(solution)/shard_map/ppermute | solution.py:31
  43.3 9.4 %copy-start.9 = (bf16[512]{0:T(512)(128)(2,1)S(1)}, bf16[512]{0:T(512)(128)(2,1)}, u32[]{:S(2)}) copy-start(bf16[512]{0:T(512)(128)(2,1)} %param.20) | copy-start | bytes 3076
  43.3 37.0 %copy-start = (bf16[512,2048]{1,0:T(8,128)(2,1)S(1)}, bf16[512,2048]{1,0:T(8,128)(2,1)}, u32[]{:S(2)}) copy-start(bf16[512,2048]{1,0:T(8,128)(2,1)} %refs_8_.3) | copy-start | bytes 6291460
  47.1 8.1 %collective-permute-start.18 = (bf16[64,640]{1,0:T(8,128)(2,1)S(1)}, bf16[64,640]{1,0:T(8,128)(2,1)S(1)}, u32[]{:S(2)}, u32[]{:S(2)}) collective-permute-start(bf16[64,640]{1,0:T(8,128)(2,1)S(1)} %get-tuple-element.29.p0), channel_id=1, source_target_pairs={{0,2},{2,4},{4,6},{6,0},{1,3},{3,5},{5,7},{7,1},{8,10},{10,12},{12... | collective-permute-start | bytes 245768 | tf_op jit(solution)/shard_map/ppermute | solution.py:31
  50.1 7.5 %collective-permute-start.19 = (bf16[64,640]{1,0:T(8,128)(2,1)S(1)}, bf16[64,640]{1,0:T(8,128)(2,1)S(1)}, u32[]{:S(2)}, u32[]{:S(2)}) collective-permute-start(bf16[64,640]{1,0:T(8,128)(2,1)S(1)} %get-tuple-element.29.p0), channel_id=1, source_target_pairs={{0,4},{2,6},{4,0},{6,2},{1,5},{3,7},{5,1},{7,3},{8,12},{10,14},{12... | collective-permute-start | bytes 245768 | tf_op jit(solution)/shard_map/ppermute | solution.py:31
  52.4 5.6 %collective-permute-start.20 = (bf16[64,640]{1,0:T(8,128)(2,1)S(1)}, bf16[64,640]{1,0:T(8,128)(2,1)S(1)}, u32[]{:S(2)}, u32[]{:S(2)}) collective-permute-start(bf16[64,640]{1,0:T(8,128)(2,1)S(1)} %get-tuple-element.29.p0), channel_id=1, source_target_pairs={{0,6},{2,0},{4,2},{6,4},{1,7},{3,1},{5,3},{7,5},{8,14},{10,8},{12,... | collective-permute-start | bytes 245768 | tf_op jit(solution)/shard_map/ppermute | solution.py:31
  58.3 9.6 %collective-permute-start.21 = (bf16[64,640]{1,0:T(8,128)(2,1)S(1)}, bf16[64,640]{1,0:T(8,128)(2,1)S(1)}, u32[]{:S(2)}, u32[]{:S(2)}) collective-permute-start(bf16[64,640]{1,0:T(8,128)(2,1)S(1)} %kv_rows.1), channel_id=1, source_target_pairs={{0,8},{8,0},{1,9},{9,1},{2,10},{10,2},{3,11},{11,3},{4,12},{12,4},... | collective-permute-start | bytes 245768 | tf_op jit(solution)/shard_map/ppermute | solution.py:35
  60.4 18.4 %collective-permute-start.17 = (bf16[128,1536]{1,0:T(8,128)(2,1)S(1)}, bf16[128,1536]{1,0:T(8,128)(2,1)S(1)}, u32[]{:S(2)}, u32[]{:S(2)}) collective-permute-start(bf16[128,1536]{1,0:T(8,128)(2,1)S(1)} %copy-done.3), channel_id=1, source_target_pairs={{0,16},{16,32},{32,48},{48,0},{1,17},{17,33},{33,49},{49,1},{2,18}... | collective-permute-start | bytes 1179656 | tf_op jit(solution)/shard_map/ppermute | solution.py:31
  67.8 6.9 %collective-permute-start.22 = (bf16[128,640]{1,0:T(8,128)(2,1)S(1)}, bf16[128,640]{1,0:T(8,128)(2,1)S(1)}, u32[]{:S(2)}, u32[]{:S(2)}) collective-permute-start(bf16[128,640]{1,0:T(8,128)(2,1)S(1)} %pad_maximum_fusion.refs_0_), channel_id=1, source_target_pairs={{0,192},{64,0},{128,64},{192,128},{1,193},{65,1},{129,65},{193,129... | collective-permute-start | bytes 491528 | tf_op jit(solution)/shard_map/ppermute | solution.py:31
  68.7 8.4 %collective-permute-start.23 = (bf16[128,640]{1,0:T(8,128)(2,1)S(1)}, bf16[128,640]{1,0:T(8,128)(2,1)S(1)}, u32[]{:S(2)}, u32[]{:S(2)}) collective-permute-start(bf16[128,640]{1,0:T(8,128)(2,1)S(1)} %pad_maximum_fusion.refs_0_), channel_id=1, source_target_pairs={{0,128},{64,192},{128,0},{192,64},{1,129},{65,193},{129,1},{193,65... | collective-permute-start | bytes 491528 | tf_op jit(solution)/shard_map/ppermute | solution.py:31
  70.0 8.8 %collective-permute-start.24 = (bf16[128,640]{1,0:T(8,128)(2,1)S(1)}, bf16[128,640]{1,0:T(8,128)(2,1)S(1)}, u32[]{:S(2)}, u32[]{:S(2)}) collective-permute-start(bf16[128,640]{1,0:T(8,128)(2,1)S(1)} %pad_maximum_fusion.refs_0_), channel_id=1, source_target_pairs={{0,64},{64,128},{128,192},{192,0},{1,65},{65,129},{129,193},{193,1... | collective-permute-start | bytes 491528 | tf_op jit(solution)/shard_map/ppermute | solution.py:31
  70.3 8.5 %collective-permute-start.25 = (bf16[128,640]{1,0:T(8,128)(2,1)S(1)}, bf16[128,640]{1,0:T(8,128)(2,1)S(1)}, u32[]{:S(2)}, u32[]{:S(2)}) collective-permute-start(bf16[128,640]{1,0:T(8,128)(2,1)S(1)} %pad_maximum_fusion.refs_0_), channel_id=1, source_target_pairs={{0,1},{1,0},{2,3},{3,2},{4,5},{5,4},{6,7},{7,6},{8,9},{9,8},{10,11... | collective-permute-start | bytes 491528 | tf_op jit(solution)/shard_map/ppermute | solution.py:35
  74.8 4.1 %collective-permute-start.26 = (bf16[128,640]{1,0:T(8,128)(2,1)S(1)}, bf16[128,640]{1,0:T(8,128)(2,1)S(1)}, u32[]{:S(2)}, u32[]{:S(2)}) collective-permute-start(bf16[128,640]{1,0:T(8,128)(2,1)S(1)} %collective-permute-done.22.refs_1_), channel_id=1, source_target_pairs={{0,1},{1,0},{2,3},{3,2},{4,5},{5,4},{6,7},{7,6},{8,9},{9,8},{10,11... | collective-permute-start | bytes 491528 | tf_op jit(solution)/shard_map/ppermute | solution.py:35
  77.1 1.8 %collective-permute-start.27 = (bf16[128,640]{1,0:T(8,128)(2,1)S(1)}, bf16[128,640]{1,0:T(8,128)(2,1)S(1)}, u32[]{:S(2)}, u32[]{:S(2)}) collective-permute-start(bf16[128,640]{1,0:T(8,128)(2,1)S(1)} %collective-permute-done.23.refs_2_), channel_id=1, source_target_pairs={{0,1},{1,0},{2,3},{3,2},{4,5},{5,4},{6,7},{7,6},{8,9},{9,8},{10,11... | collective-permute-start | bytes 491528 | tf_op jit(solution)/shard_map/ppermute | solution.py:35
  78.8 1.4 %collective-permute-start.28 = (bf16[128,640]{1,0:T(8,128)(2,1)S(1)}, bf16[128,640]{1,0:T(8,128)(2,1)S(1)}, u32[]{:S(2)}, u32[]{:S(2)}) collective-permute-start(bf16[128,640]{1,0:T(8,128)(2,1)S(1)} %collective-permute-done.24.refs_3_), channel_id=1, source_target_pairs={{0,1},{1,0},{2,3},{3,2},{4,5},{5,4},{6,7},{7,6},{8,9},{9,8},{10,11... | collective-permute-start | bytes 491528 | tf_op jit(solution)/shard_map/ppermute | solution.py:35
  91.6 23.3 %collective-permute-start.32 = (bf16[128,640]{1,0:T(8,128)(2,1)S(1)}, bf16[128,640]{1,0:T(8,128)(2,1)S(1)}, u32[]{:S(2)}, u32[]{:S(2)}) collective-permute-start(bf16[128,640]{1,0:T(8,128)(2,1)S(1)} %get-tuple-element.35), channel_id=1, source_target_pairs={{0,16},{16,32},{32,48},{48,0},{1,17},{17,33},{33,49},{49,1},{2,18}... | collective-permute-start | bytes 491528 | tf_op jit(solution)/shard_map/ppermute | solution.py:31
  94.1 16.4 %collective-permute-start.12 = (bf16[16,896]{1,0:T(8,128)(2,1)S(1)}, bf16[16,896]{1,0:T(8,128)(2,1)S(1)}, u32[]{:S(2)}, u32[]{:S(2)}) collective-permute-start(bf16[16,896]{1,0:T(8,128)(2,1)S(1)} %get-tuple-element.26), channel_id=1, source_target_pairs={{0,2},{2,4},{4,6},{6,0},{1,3},{3,5},{5,7},{7,1},{8,10},{10,12},{12... | collective-permute-start | bytes 86024 | tf_op jit(solution)/shard_map/ppermute | solution.py:31
  94.8 15.7 %collective-permute-start.13 = (bf16[16,896]{1,0:T(8,128)(2,1)S(1)}, bf16[16,896]{1,0:T(8,128)(2,1)S(1)}, u32[]{:S(2)}, u32[]{:S(2)}) collective-permute-start(bf16[16,896]{1,0:T(8,128)(2,1)S(1)} %get-tuple-element.27), channel_id=1, source_target_pairs={{0,4},{2,6},{4,0},{6,2},{1,5},{3,7},{5,1},{7,3},{8,12},{10,14},{12... | collective-permute-start | bytes 86024 | tf_op jit(solution)/shard_map/ppermute | solution.py:31
  96.7 17.1 %collective-permute-start.14 = (bf16[16,896]{1,0:T(8,128)(2,1)S(1)}, bf16[16,896]{1,0:T(8,128)(2,1)S(1)}, u32[]{:S(2)}, u32[]{:S(2)}) collective-permute-start(bf16[16,896]{1,0:T(8,128)(2,1)S(1)} %get-tuple-element.28), channel_id=1, source_target_pairs={{0,6},{2,0},{4,2},{6,4},{1,7},{3,1},{5,3},{7,5},{8,14},{10,8},{12,... | collective-permute-start | bytes 86024 | tf_op jit(solution)/shard_map/ppermute | solution.py:31
  97.9 18.2 %collective-permute-start.33 = (bf16[128,640]{1,0:T(8,128)(2,1)S(1)}, bf16[128,640]{1,0:T(8,128)(2,1)S(1)}, u32[]{:S(2)}, u32[]{:S(2)}) collective-permute-start(bf16[128,640]{1,0:T(8,128)(2,1)S(1)} %get-tuple-element.36), channel_id=1, source_target_pairs={{0,32},{16,48},{32,0},{48,16},{1,33},{17,49},{33,1},{49,17},{2,34}... | collective-permute-start | bytes 491528 | tf_op jit(solution)/shard_map/ppermute | solution.py:31
  110.4 9.2 %collective-permute-start.34 = (bf16[128,640]{1,0:T(8,128)(2,1)S(1)}, bf16[128,640]{1,0:T(8,128)(2,1)S(1)}, u32[]{:S(2)}, u32[]{:S(2)}) collective-permute-start(bf16[128,640]{1,0:T(8,128)(2,1)S(1)} %get-tuple-element.37), channel_id=1, source_target_pairs={{0,48},{16,0},{32,16},{48,32},{1,49},{17,1},{33,17},{49,33},{2,50}... | collective-permute-start | bytes 491528 | tf_op jit(solution)/shard_map/ppermute | solution.py:31
  110.5 9.1 %collective-permute-start.29 = (bf16[128,640]{1,0:T(8,128)(2,1)S(1)}, bf16[128,640]{1,0:T(8,128)(2,1)S(1)}, u32[]{:S(2)}, u32[]{:S(2)}) collective-permute-start(bf16[128,640]{1,0:T(8,128)(2,1)S(1)} %get-tuple-element.31), channel_id=1, source_target_pairs={{0,16},{16,32},{32,48},{48,0},{1,17},{17,33},{33,49},{49,1},{2,18}... | collective-permute-start | bytes 491528 | tf_op jit(solution)/shard_map/ppermute | solution.py:31
  113.7 8.0 %collective-permute-start.30 = (bf16[128,640]{1,0:T(8,128)(2,1)S(1)}, bf16[128,640]{1,0:T(8,128)(2,1)S(1)}, u32[]{:S(2)}, u32[]{:S(2)}) collective-permute-start(bf16[128,640]{1,0:T(8,128)(2,1)S(1)} %get-tuple-element.32), channel_id=1, source_target_pairs={{0,32},{16,48},{32,0},{48,16},{1,33},{17,49},{33,1},{49,17},{2,34}... | collective-permute-start | bytes 491528 | tf_op jit(solution)/shard_map/ppermute | solution.py:31
  114.9 9.1 %collective-permute-start.31 = (bf16[128,640]{1,0:T(8,128)(2,1)S(1)}, bf16[128,640]{1,0:T(8,128)(2,1)S(1)}, u32[]{:S(2)}, u32[]{:S(2)}) collective-permute-start(bf16[128,640]{1,0:T(8,128)(2,1)S(1)} %get-tuple-element.33), channel_id=1, source_target_pairs={{0,48},{16,0},{32,16},{48,32},{1,49},{17,1},{33,17},{49,33},{2,50}... | collective-permute-start | bytes 491528 | tf_op jit(solution)/shard_map/ppermute | solution.py:31

commit v2 on v0

v2 whole, which is shorter than its diff:
```python
import functools
import math

import jax
import jax.numpy as jnp
from jax import lax
from jax.experimental import pallas as pl
from jax.experimental.pallas import tpu as pltpu
from jax.sharding import Mesh, PartitionSpec as P

LATENT = 512
ROPE = 64
NOPE = 128
VDIM = 128
HEADS = 8
WIDE = 640
MESSAGE = HEADS * VDIM + 128
COLS = 896
BF = jnp.bfloat16
F32 = jnp.float32
MIB = 1 << 20
AXES = ("y", "x", "zh", "zl", "core")
SIZES = (4, 4, 2, 4, 2)
ORDER = (2, 1, 3, 0)


def dot(a, b):
    return jnp.dot(a, b, preferred_element_type=F32)


def shift(value, axis, k):
    return lax.ppermute(value, axis, [(i, (i + k) % 4) for i in range(4)])


def swap(value, axis, bit=1, size=2):
    return lax.ppermute(value, axis, [(i, i ^ bit) for i in range(size)])


def flat(y, x, zh, zl, core):
    return (((y * 4 + x) * 2 + zh) * 4 + zl) * 2 + core


def turn(value, k):
    perm = []
    for x in range(4):
        for core in range(2):
            perm.append((x * 2 + core, (x + (k if core == 0 else -k)) % 4 * 2 + core))
    return lax.ppermute(value, ("x", "core"), perm)


def tie(*values):
    return lax.optimization_barrier(values)


def transposed_block(value):
    perm = []
    for y in range(4):
        for x in range(4):
            for zh in range(2):
                for zl in range(4):
                    for core in range(2):
                        perm.append((flat(zl, x, core, y, zh), flat(y, x, zh, zl, core)))
    return lax.ppermute(value, AXES, perm)


def coords(s):
    f = s[0]
    return f // 64, f // 16 % 4, f // 8 % 2, f // 2 % 4, f % 2


def params(mib):
    return pltpu.CompilerParams(vmem_limit_bytes=mib * MIB)


def shape(dims, dtype=BF):
    return jax.ShapeDtypeStruct(dims, dtype)


def project_kernel(s, x_hbm, ad_hbm, w_hbm, au_hbm, res_hbm, send_ref, keep_ref, x, ad, w, au, res, xr, kept, sem):
    _, _, _, zl, core = coords(s)
    columns = [pl.ds(pl.multiple_of((zl + k) % 4 * COLS, 128), COLS) for k in ORDER]

    def fetch(source, target, index):
        copy = pltpu.make_async_copy(source, target, sem.at[index])
        copy.start()
        return copy

    first = [fetch(x_hbm, x, 0), fetch(ad_hbm, ad, 1)]
    weights = [fetch(w_hbm.at[:, column], w.at[b], 4 + b) for b, column in enumerate(columns[:1])]
    second = [fetch(au_hbm, au, 2), fetch(res_hbm, res, 3)]
    weights += [fetch(w_hbm.at[:, column], w.at[b + 1], 5 + b) for b, column in enumerate(columns[1:])]
    for copy in first:
        copy.wait()
    xr[0:64, :] = x[:, 1 - core].reshape(64, 1024)
    xr[64:128, :] = x[:, core].reshape(64, 1024)
    down = dot(xr[...], ad[...])
    high = down.astype(BF)
    pieces = jnp.concatenate([high, (down - high.astype(F32)).astype(BF)], axis=0)
    rows = pl.ds(pl.multiple_of(zl * 16, 16), 16)
    for b, column in enumerate(columns):
        weights[b].wait()
        acc = dot(xr[...], w[b])
        if b == 0:
            for copy in second:
                copy.wait()
        adapter = dot(pieces, au[:, column])
        acc = acc + adapter[:128] + adapter[128:]
        send_ref[b] = acc[:64].astype(BF)
        kept[...] = acc[64:]
        kept[rows, :] = kept[rows, :] + res[:, column].astype(F32)
        keep_ref[b] = kept[...].astype(BF)


def project(scalars, *operands):
    return pl.pallas_call(
        project_kernel,
        in_specs=[pl.BlockSpec(memory_space=pltpu.SMEM)] + [pl.BlockSpec(memory_space=pltpu.HBM)] * 5,
        out_specs=[pl.BlockSpec(memory_space=pltpu.VMEM)] * 2,
        out_shape=[shape((4, 64, COLS))] * 2,
        scratch_shapes=[
            pltpu.VMEM((4, 2, 16, 1024), BF),
            pltpu.VMEM((1024, 256), BF),
            pltpu.VMEM((4, 1024, COLS), BF),
            pltpu.VMEM((256, 4 * COLS), BF),
            pltpu.VMEM((16, 4 * COLS), BF),
            pltpu.VMEM((128, 1024), BF),
            pltpu.VMEM((64, COLS), F32),
            pltpu.SemaphoreType.DMA((8,)),
        ],
        compiler_params=params(56),
        name="project",
    )(scalars, *operands)


def local(kernel, outs, mib, name, smem=0, vmem=0, scratch=()):
    space = lambda kind, n: [pl.BlockSpec(memory_space=kind)] * n
    out_specs = pl.BlockSpec(memory_space=pltpu.VMEM)
    return pl.pallas_call(
        kernel,
        in_specs=space(pltpu.SMEM, smem) + space(pltpu.VMEM, vmem),
        out_specs=[out_specs] * len(outs) if isinstance(outs, list) else out_specs,
        out_shape=outs,
        scratch_shapes=scratch,
        compiler_params=params(mib),
        name=name,
    )


def pair_sum_kernel(keep_ref, got_ref, *outs):
    for k, out in enumerate(outs):
        out[...] = (keep_ref[k].astype(F32) + got_ref[k].astype(F32)).astype(BF)


def pair_sum(keep, got, count):
    return local(pair_sum_kernel, [shape((64, COLS))] * count, 16, "pair_sum", vmem=2)(keep, got)


def pack_kernel(count, *refs):
    out_ref = refs[-1]
    start = 0
    for ref in refs[:count]:
        size = ref.shape[0]
        out_ref[start : start + size] = ref[...]
        start += size


def pack(blocks, after):
    dims = (sum(block.shape[0] for block in blocks),) + blocks[0].shape[1:]
    kernel = functools.partial(pack_kernel, len(blocks))
    return local(kernel, shape(dims), 16, "pack", vmem=len(blocks) + len(after))(*blocks, *after)


def assemble_kernel(s, own_ref, other_ref, out_ref):
    _, x, _, _, core = coords(s)
    out_ref[:, 512:] = jnp.zeros((COLS, WIDE - 512), BF)
    for k in range(4):
        for other, ref in enumerate((own_ref, other_ref)):
            zh = (core + other) % 2
            row = pl.multiple_of((x ^ k) * 224 + zh * 112, 16)
            out_ref[pl.ds(row, 112), 0:576] = ref[k]


def assemble(scalars, own, other):
    return local(assemble_kernel, shape((COLS, WIDE)), 16, "assemble", 1, 2)(scalars, own, other)


def tables_kernel(s, seg, cos_ref, sin_ref):
    y, x, zh, _, core = coords(s)
    ctx = y * 8 + x * 2 + zh
    row = lax.broadcasted_iota(jnp.int32, (64, ROPE), 0)
    lane = lax.broadcasted_iota(jnp.int32, (64, ROPE), 1)
    token = row // 16 * 32 + core * 16 + row % 16
    places = jnp.where(token < 64, seg[2 * ctx], seg[2 * ctx + 1]) * 64 + token % 64
    inverse = jnp.exp((lane % 32).astype(F32) * (-2.0 * math.log(10000.0) / ROPE))
    angles = places.astype(F32) * inverse
    cos_ref[...] = jnp.cos(angles)
    sine = jnp.sin(angles)
    sin_ref[...] = jnp.where(lane < 32, -sine, sine)


def tables(scalars, seg):
    return local(tables_kernel, [shape((64, ROPE), F32)] * 2, 16, "tables", 2)(scalars, seg)


def latent_kernel(s, keep_ref, got_ref, r1, r2, r3, gain_ref, w_ref, part_ref, h0, h1, h2, h3, hid):
    _, _, _, zl, _ = coords(s)
    total = sum(ref[...].astype(F32) for ref in (keep_ref.at[3], got_ref.at[3], r1, r2, r3))
    hidden = total.astype(BF)
    hid[...] = hidden
    for k, out in enumerate((h0, h1, h2, h3)):
        out[...] = hid[pl.ds(pl.multiple_of(((zl + k) % 4) * 16, 16), 16), :]
    wide = hidden.astype(F32)
    squares = jnp.sum(wide * wide, axis=1, keepdims=True)
    gain = gain_ref[:, pl.ds(pl.multiple_of(zl * COLS, 128), COLS)].astype(F32)
    part = dot((wide * gain).astype(BF), w_ref[...])
    lane = lax.broadcasted_iota(jnp.int32, (64, 128), 1)
    high = squares.astype(BF).astype(F32)
    tail = jnp.where(lane == 64, high, jnp.where(lane == 65, squares - high, part[:, 512:]))
    part_ref[:, :512] = part[:, :512].astype(BF)
    part_ref[:, 512:] = tail.astype(BF)


def latent_part(scalars, *operands):
    outs = [shape((64, WIDE))] + [shape((16, COLS))] * 4
    scratch = [pltpu.VMEM((64, COLS), BF)]
    return local(latent_kernel, outs, 16, "latent_part", 1, 7, scratch)(scalars, *operands)


def rows_kernel(p0, p1, p2, p3, cos_ref, sin_ref, gain_ref, out_ref):
    total = p0[...].astype(F32) + p1[...].astype(F32) + p2[...].astype(F32) + p3[...].astype(F32)
    tail = total[:, 512:]
    inverse = lax.rsqrt((tail[:, 64:65] + tail[:, 65:66]) / 3584.0 + 1e-06)
    latent = total[:, :512] * inverse
    mean_square = jnp.mean(latent * latent, axis=1, keepdims=True)
    out_ref[:, :512] = (latent * lax.rsqrt(mean_square + 1e-06) * gain_ref[...].astype(F32)).astype(BF)
    rope = tail[:, :64] * inverse
    swapped = jnp.concatenate([rope[:, 32:], rope[:, :32]], axis=1)
    rotated = rope * cos_ref[...] + swapped * sin_ref[...]
    out_ref[:, 512:] = jnp.concatenate([rotated, jnp.zeros((64, 64), F32)], axis=1).astype(BF)


def kv_rows(parts, cosine, sine, gain):
    return local(rows_kernel, shape((64, WIDE)), 16, "kv_rows", vmem=7)(*parts, cosine, sine, gain)


def lift_kernel(s, seg, *refs):
    keys = refs[:8]
    up_ref, key_ref, value_ref, kv = refs[8:]
    y, x, zh, _, _ = coords(s)
    for k in range(4):
        for a in range(2):
            ctx = ((y + k) % 4) * 8 + x * 2 + (zh + a) % 2
            first_upper = (seg[2 * ctx] > seg[2 * ctx + 1]).astype(jnp.int32)
            for half in range(2):
                upper = first_upper if half == 0 else 1 - first_upper
                for other in range(2):
                    row = pl.multiple_of(upper * 512 + (k * 2 + a) * 64 + other * 32, 32)
                    start = a * 64 + half * 32
                    kv[pl.ds(row, 32), :] = keys[4 * other + k][start : start + 32, :]
    ones = jnp.ones((1024, 128), BF)
    for head in range(HEADS):
        lifted = dot(kv[:, :LATENT], up_ref[:, head * 256 : head * 256 + 256]).astype(BF)
        key_ref[head, :, :NOPE] = lifted[:, :NOPE]
        key_ref[head, :, NOPE:] = kv[:, LATENT:]
        value_ref[head, :, :VDIM] = lifted[:, NOPE:]
        value_ref[head, :, VDIM:] = ones


def lift(scalars, seg, keys, up):
    outs = [shape((HEADS, 1024, 256))] * 2
    scratch = [pltpu.VMEM((1024, WIDE), BF)]
    return local(lift_kernel, outs, 24, "lift", 2, 9, scratch)(scalars, seg, *keys, up)


def stat_pieces(level, lane):
    high = level.astype(BF).astype(F32)
    middle = (level - high).astype(BF).astype(F32)
    return jnp.where(lane < 8, high, jnp.where(lane < 16, middle, level - high - middle))


def attend_kernel(chunks, s, seg, *refs):
    count = len(chunks)
    queries = refs[:count]
    key_ref, value_ref = refs[count : count + 2]
    outs = refs[count + 2 :]
    y, x, zh, _, core = coords(s)
    hops = (0, 1 + 2 * core, 2, 3 - 2 * core)
    factor = math.log2(math.e) / math.sqrt(NOPE + ROPE)
    lane = lax.broadcasted_iota(jnp.int32, (1, 512), 1)
    lower = jnp.zeros((1, 512), jnp.int32)
    upper = lower
    for k in range(4):
        for a in range(2):
            ctx = ((y + k) % 4) * 8 + x * 2 + (zh + a) % 2
            one, two = seg[2 * ctx], seg[2 * ctx + 1]
            lower = jnp.where(lane // 64 == k * 2 + a, jnp.minimum(one, two), lower)
            upper = jnp.where(lane // 64 == k * 2 + a, jnp.maximum(one, two), upper)
    inside = (lane // 16) % 2 * 32 + ((lane // 32) % 2 + core) % 2 * 16 + lane % 16
    row = lax.broadcasted_iota(jnp.int32, (64, 512), 0)
    low_rows, high_rows, low_bias, high_bias = [], [], [], []
    for chunk in chunks:
        ctx = y * 8 + ((x + hops[chunk]) % 4) * 2 + zh
        one, two = seg[2 * ctx], seg[2 * ctx + 1]
        flipped = (one > two).astype(jnp.int32)
        low_rows.append(pl.ds(pl.multiple_of(flipped * 64, 64), 64))
        high_rows.append(pl.ds(pl.multiple_of(64 - flipped * 64, 64), 64))
        low_bias.append(jnp.where(lower * 64 + inside <= row + jnp.minimum(one, two) * 64, 0.0, -1e30))
        high_bias.append(jnp.where(upper * 64 + inside <= row + jnp.maximum(one, two) * 64, 0.0, -1e30))
    low_bias = jnp.concatenate(low_bias, axis=0)
    high_bias = jnp.concatenate(high_bias, axis=0)
    rows = 64 * count
    stat_lane = lax.broadcasted_iota(jnp.int32, (2 * rows, 128), 1)
    stats = jnp.zeros((2 * rows, 128), F32)
    across = (((1,), (1,)), ((), ()))
    near, far = [], []
    for head in range(HEADS):
        column = slice(head * 192, head * 192 + 192)
        pieces = [q[r, column] for q, r in zip(queries, low_rows)] + [q[r, column] for q, r in zip(queries, high_rows)]
        query = jnp.concatenate([jnp.concatenate(pieces, axis=0), jnp.zeros((2 * rows, 64), BF)], axis=1)
        near.append(lax.dot_general(query, key_ref[head, :512, :], across, preferred_element_type=F32))
        high = lax.dot_general(query[rows:], key_ref[head, 512:, :], across, preferred_element_type=F32)
        far.append(high + high_bias)
    low = [scores[:rows] + low_bias for scores in near]
    mid = [scores[rows:] for scores in near]
    low_top = [jnp.max(scores, axis=1, keepdims=True) for scores in low]
    high_top = [jnp.max(jnp.maximum(a, b), axis=1, keepdims=True) for a, b in zip(mid, far)]
    weigh = lambda scores, top: jnp.exp2((scores - top) * factor).astype(BF)
    low = [weigh(a, t) for a, t in zip(low, low_top)]
    mid = [weigh(a, t) for a, t in zip(mid, high_top)]
    far = [weigh(a, t) for a, t in zip(far, high_top)]
    first = [dot(jnp.concatenate([a, b], axis=0), value_ref[h, :512, :]) for h, (a, b) in enumerate(zip(low, mid))]
    second = [dot(a, value_ref[h, 512:, :]) for h, a in enumerate(far)]
    for head in range(HEADS):
        both = jnp.concatenate([first[head][:rows], first[head][rows:] + second[head]], axis=0)
        top = jnp.concatenate([low_top[head], high_top[head]], axis=0)
        mixed = (both[:, :VDIM] / both[:, VDIM:]).astype(BF)
        level = top * factor + jnp.log2(both[:, VDIM:])
        stats = jnp.where(stat_lane % 8 == head, level, stats)
        for c in range(count):
            column = slice(head * 128, head * 128 + 128)
            outs[c][low_rows[c], column] = mixed[64 * c : 64 * c + 64]
            outs[c][high_rows[c], column] = mixed[rows + 64 * c : rows + 64 * c + 64]
    stats = jnp.where(stat_lane < 24, stat_pieces(stats, stat_lane), 0.0).astype(BF)
    for c in range(count):
        outs[c][low_rows[c], HEADS * 128 :] = stats[64 * c : 64 * c + 64]
        outs[c][high_rows[c], HEADS * 128 :] = stats[rows + 64 * c : rows + 64 * c + 64]


def attend(chunks, scalars, seg, queries, lifted):
    kernel = functools.partial(attend_kernel, chunks)
    outs = [shape((128, MESSAGE))] * len(chunks)
    return local(kernel, outs, 32, "attend", 2, len(chunks) + 2)(scalars, seg, *queries, *lifted)


def spread_levels(ref, width, group):
    row = lax.broadcasted_iota(jnp.int32, (128, width), 0)
    lane = lax.broadcasted_iota(jnp.int32, (128, width), 1)
    picks = (row < 24) & (row % 8 == (lane // group) % 8)
    return dot(ref[:, HEADS * 128 :], picks.astype(F32).astype(BF))


def merged(refs):
    levels = [spread_levels(ref, 1024, 128) for ref in refs]
    top = functools.reduce(jnp.maximum, levels)
    scales = [jnp.exp2(level - top) for level in levels]
    mixed = sum(ref[:, : HEADS * 128].astype(F32) * scale for ref, scale in zip(refs, scales))
    return (mixed / sum(scales[1:], scales[0])).astype(BF)


def relay_kernel(got_ref, own_ref, out_ref):
    refs = (got_ref, own_ref)
    out_ref[:, : HEADS * 128] = merged(refs)
    one, two = [spread_levels(ref, 128, 1) for ref in refs]
    top = jnp.maximum(one, two)
    level = top + jnp.log2(jnp.exp2(one - top) + jnp.exp2(two - top))
    lane = lax.broadcasted_iota(jnp.int32, (128, 128), 1)
    out_ref[:, HEADS * 128 :] = jnp.where(lane < 24, stat_pieces(level, lane), 0.0).astype(BF)


def relay(got, own):
    return local(relay_kernel, shape((128, MESSAGE)), 16, "relay", vmem=2)(got, own)


def merge_kernel(a_ref, b_ref, c_ref, out_ref):
    out_ref[...] = merged((a_ref, b_ref, c_ref))


def merge(a, b, c):
    return local(merge_kernel, shape((128, HEADS * VDIM)), 16, "merge", vmem=3)(a, b, c)


def hidden_kernel(s, h0, h1, h2, h3, out_ref):
    _, _, _, zl, _ = coords(s)
    for k, ref in enumerate((h0, h1, h2, h3)):
        column = pl.multiple_of(((zl + 4 - k) % 4) * COLS, 128)
        out_ref[:, pl.ds(column, COLS)] = ref[...]


def hidden_rows(scalars, blocks):
    return local(hidden_kernel, shape((16, 4 * COLS)), 16, "hidden_rows", 1, 4)(scalars, *blocks)


def body(
    segment_ordering,
    attention_input,
    residual,
    queries,
    output_weight,
    adapter_down_factor,
    adapter_up_factor,
    input_norm_gain,
    latent_key_weight,
    latent_norm_gain,
    latent_up_weight,
):
    scalars = lax.axis_index(AXES).astype(jnp.int32).reshape(1)
    near, away, far, back = 0, 1, 2, 3

    block = transposed_block(latent_key_weight)[None]
    send, keep = project(
        scalars,
        attention_input.reshape(4, 2, 16, 1024),
        adapter_down_factor,
        output_weight,
        adapter_up_factor,
        residual,
    )
    block, send = tie(block, send)
    got = swap(send, "core")
    blocks = [block] + [swap(block, "x", k, 4) for k in (1, 2, 3)]
    sums = pair_sum(keep, got, 3)
    r2, r1, r3 = (shift(value, "zl", k) for value, k in zip(sums, ORDER))
    four = pack(blocks, (r1, r2, r3))
    weight = assemble(scalars, four, swap(four, "core"))
    q_far, q_back = shift(queries, "x", 2), turn(queries, 1)
    q_away = turn(tie(queries, q_far)[0], -1)
    part, h0, h1, h2, h3 = latent_part(
        scalars, keep, got, r1, r2, r3, input_norm_gain.reshape(1, -1), weight
    )
    cosine, sine = tables(scalars, tie(segment_ordering, part)[0])
    p1, p2, p3 = (shift(part, "zl", k) for k in (1, 2, 3))
    rows = kv_rows([part, p1, p2, p3], cosine, sine, latent_norm_gain.reshape(1, -1))
    rows, h1, h2, h3 = tie(rows, h1, h2, h3)
    beside = swap(rows, "zh")
    pieces = [h0] + [shift(h, "zl", k) for k, h in ((1, h1), (2, h2), (3, h3))]
    both = pack([rows, beside], (q_far, q_back, *pieces[1:]))
    column = [both] + [shift(both, "y", -k) for k in (1, 2, 3)]
    keys = column + [swap(value, "core") for value in column]

    *keys, q_away = tie(*keys, q_away)
    lifted = lift(scalars, segment_ordering, keys, latent_up_weight)
    relayed, direct = attend((far, back), scalars, segment_ordering, [q_far, q_back], lifted)
    got = turn(relayed, 1)
    mine, own = attend((away, near), scalars, segment_ordering, [q_away, queries], lifted)
    direct, own = tie(direct, own)
    direct = turn(direct, -1)
    passed = turn(relay(got, mine), 1)
    hidden = hidden_rows(scalars, pieces)
    return hidden, merge(own, direct, passed)


def solution(mesh):
    split = Mesh(mesh.devices.reshape(SIZES), AXES)
    ctx, tp = ("y", "x", "zh"), ("zl", "core")
    in_specs = (
        P(),
        P(ctx, tp),
        P(ctx + tp, None),
        P(ctx, tp),
        P(tp, None),
        P(tp, None),
        P(),
        P(),
        P(ctx, None),
        P(),
        P(None, tp),
    )
    out_specs = (P(ctx + tp, None), P(ctx, tp))
    return jax.shard_map(body, mesh=split, in_specs=in_specs, out_specs=out_specs, check_vma=False)
```

time: 388 us -> 100 us (0.26)
  waiting for transfers between devices: 230 us -> 32.8 us
  matrix products: 72.9 us -> 0 us
  starting transfers between devices: 0.12 us -> 43.7 us
  local copies, waits for them, and re-layouts: 42.1 us -> 1.06 us
  other arithmetic: 23.6 us -> 0 us
  Pallas kernels: 0 us -> 20.7 us
  between operations: 15.7 us -> 0.88 us
    all_gather x2 -> x0, waiting for transfers between devices: 187 us -> none  [the longest x1 110 us: body(): every_row = lax.all_gather(kv_rows, ('ctx', 'tp'), axis=0, tiled=True)]
    dot_general x28 -> x0, matrix products: 72.9 us -> none  [the longest x8 28.9 us: attend(): jnp.einsum('ihd,jhd->hij', query_heads, keys, preferred_element_type=jnp....]
    ppermute x0 -> x29, starting transfers between devices: none -> 43.7 us  [the longest x13 17 us: shift(): return lax.ppermute(value, axis, [(i, (i + k) % 4) for i in range(4)])]
    reduce_scatter x1 -> x0, waiting for transfers between devices: 42.8 us -> none  [body(): lax.psum_scatter(base_product + jnp.dot(down_partial, adapter_widened, pr...]
    ppermute x0 -> x29, waiting for transfers between devices: none -> 32.8 us  [the longest x13 22 us: shift(): return lax.ppermute(value, axis, [(i, (i + k) % 4) for i in range(4)])]
    pallas_call x0 -> x14, Pallas kernels: none -> 20.7 us  [the longest x2 7.3 us: attend(): local(kernel, outs, 32, 'attend', 2, len(chunks) + 2)]
    reduce_sum x20 -> x0, other arithmetic: 20.3 us -> none  [the longest x8 18 us: attend(): totals = totals * decay + jnp.sum(weights, axis=2)]
    while x56 -> x0, local copies, waits for them, and re-layouts: 17.3 us -> none
  transfers between devices with their start and end apart: 3 -> 29, of which waited for: 3 -> 15; matrix products, arithmetic and copies ran while one was open for 1% -> 0% of each run, Pallas kernels for 0% -> 12%
where the time goes in v2:
time: 100 us; the launch traced here: 99.2 us
  starting transfers between devices  43.7 us (44%)
  waiting for transfers between devices  32.8 us (33%)
  Pallas kernels  20.7 us (21%)
  local copies, waits for them, and re-layouts  1.06 us (1%)
    ppermute x13, waiting for transfers between devices, shift(): return lax.ppermute(value, axis, [(i, (i + k) % 4) for i in range(4)])  22 us
    ppermute x13, starting transfers between devices, shift(): return lax.ppermute(value, axis, [(i, (i + k) % 4) for i in range(4)])  17 us
    ppermute x10, starting transfers between devices, swap(): return lax.ppermute(value, axis, [(i, i ^ bit) for i in range(size)])  13.7 us
    ppermute x5, waiting for transfers between devices, turn(): return lax.ppermute(value, ('x', 'core'), perm)  8.22 us
    pallas_call x2, Pallas kernels, attend(): local(kernel, outs, 32, 'attend', 2, len(chunks) + 2)  7.3 us
    ppermute x5, starting transfers between devices, turn(): return lax.ppermute(value, ('x', 'core'), perm)  6.87 us
    ppermute x1, starting transfers between devices, transposed_block(): return lax.ppermute(value, AXES, perm)  6.19 us
    pallas_call x1, Pallas kernels, project(): pl.pallas_call(project_kernel, in_specs=[pl.BlockSpec(memory_space=pltpu....  5.81 us
  transfers between devices with their start and end apart: 29, of which 15 were waited for; matrix products, arithmetic and copies ran while one was open for 0% of the time, Pallas kernels for 12%

profile of v2, /device:TPU:24, one launch (start us, length us, event | category | flops | bytes accessed | tf_op | source)
XLA Modules:
  0.0 99.2 jit_solution(12930952887516788959)
XLA Ops:
  0.6 6.2 %collective-permute-start = (bf16[112,576]{1,0:T(8,128)(2,1)}, bf16[112,576]{1,0:T(8,128)(2,1)S(1)}, u32[]{:S(2)}, u32[]{:S(2)}) collective-permute-start(bf16[112,576]{1,0:T(8,128)(2,1)} %param.19), channel_id=1, source_target_pairs={{0,0},{8,1},{64,2},{72,3},{128,4},{136,5},{192,6},{200,7},{1,8},{9... | collective-permute-start | bytes 387080 | tf_op jit(solution)/shard_map/ppermute | solution.py:63
  6.9 5.8 %project.1 = (bf16[4,64,896]{2,1,0:T(8,128)(2,1)}, bf16[4,64,896]{2,1,0:T(8,128)(2,1)}) custom-call(s32[1]{0:T(128)} %bitcast.s, bf16[4,2,16,1024]{3,2,1,0:T(8,128)(2,1)} %bitcast.7, bf16[1024,256]{1,0:T(8,128)(2,1)} %ad_hbm.1, bf16[1024,3584]{1,0:T(8,128)(2,1)} %w_hbm.1, bf16[256,3584]{1,0:T(8,128)(2,1)} %au_hbm.1, bf16[16,3584]{1,0:T(8,128)(2,1)} %res_hbm.1), custom_call_target="tpu_custom_call" | custom-call | tf_op jit(solution)/shard_map/project/pallas_call | solution.py:115
  12.7 3.1 %collective-permute-start.1 = (bf16[4,64,896]{2,1,0:T(8,128)(2,1)}, bf16[4,64,896]{2,1,0:T(8,128)(2,1)S(1)}, u32[]{:S(2)}, u32[]{:S(2)}) collective-permute-start(bf16[4,64,896]{2,1,0:T(8,128)(2,1)} %get-tuple-element.41), channel_id=1, source_target_pairs={{0,1},{1,0},{2,3},{3,2},{4,5},{5,4},{6,7},{7,6},{8,9},{9,8},{10,11... | collective-permute-start | bytes 1376264 | tf_op jit(solution)/shard_map/ppermute | solution.py:36
  15.8 2.8 %collective-permute-start.7 = (bf16[1,112,576]{2,1,0:T(8,128)(2,1)S(1)}, bf16[1,112,576]{2,1,0:T(8,128)(2,1)S(1)}, u32[]{:S(2)}, u32[]{:S(2)}) collective-permute-start(bf16[1,112,576]{2,1,0:T(8,128)(2,1)S(1)} %bitcast.3), channel_id=1, source_target_pairs={{0,48},{16,32},{32,16},{48,0},{1,49},{17,33},{33,17},{49,1},{2,50}... | collective-permute-start | bytes 387080 | tf_op jit(solution)/shard_map/ppermute | solution.py:36
  18.5 0.8 collective-permute-start.6
  19.3 0.5 collective-permute-start.5
  19.9 1.0 %copy-done.1 = bf16[4,64,896]{2,1,0:T(8,128)(2,1)S(1)} copy-done((bf16[4,64,896]{2,1,0:T(8,128)(2,1)S(1)}, bf16[4,64,896]{2,1,0:T(8,128)(2,1)}, u32[]{:S(2)}) %copy-start.1) | copy-done | bytes 458776
  20.9 0.1 pair_sum.1
  21.0 0.9 collective-permute-start.2
  21.9 1.7 %collective-permute-start.3 = (bf16[64,896]{1,0:T(8,128)(2,1)S(1)}, bf16[64,896]{1,0:T(8,128)(2,1)S(1)}, u32[]{:S(2)}, u32[]{:S(2)}) collective-permute-start(bf16[64,896]{1,0:T(8,128)(2,1)S(1)} %get-tuple-element.43), channel_id=1, source_target_pairs={{0,4},{2,6},{4,0},{6,2},{1,5},{3,7},{5,1},{7,3},{8,12},{10,14},{12... | collective-permute-start | bytes 344072 | tf_op jit(solution)/shard_map/ppermute | solution.py:32
  23.6 1.2 %collective-permute-done.7.refs_3_ = bf16[1,112,576]{2,1,0:T(8,128)(2,1)S(1)} collective-permute-done((bf16[1,112,576]{2,1,0:T(8,128)(2,1)S(1)}, bf16[1,112,576]{2,1,0:T(8,128)(2,1)S(1)}, u32[]{:S(2)}, u32[]{:S(2)}) %collective-permute-start.7) | collective-permute-done | bytes 129056 | tf_op jit(solution)/shard_map/ppermute | solution.py:36
  24.8 2.1 %collective-permute-start.4 = (bf16[64,896]{1,0:T(8,128)(2,1)S(1)}, bf16[64,896]{1,0:T(8,128)(2,1)S(1)}, u32[]{:S(2)}, u32[]{:S(2)}) collective-permute-start(bf16[64,896]{1,0:T(8,128)(2,1)S(1)} %get-tuple-element.44), channel_id=1, source_target_pairs={{0,6},{2,0},{4,2},{6,4},{1,7},{3,1},{5,3},{7,5},{8,14},{10,8},{12,... | collective-permute-start | bytes 344072 | tf_op jit(solution)/shard_map/ppermute | solution.py:32
  26.9 2.1 %collective-permute-done.2.refs_4_.r1 = bf16[64,896]{1,0:T(8,128)(2,1)S(1)} collective-permute-done((bf16[64,896]{1,0:T(8,128)(2,1)S(1)}, bf16[64,896]{1,0:T(8,128)(2,1)S(1)}, u32[]{:S(2)}, u32[]{:S(2)}) %collective-permute-start.2) | collective-permute-done | bytes 114720 | tf_op jit(solution)/shard_map/ppermute | solution.py:32
  29.0 3.1 %collective-permute-done.3.refs_5_.r2 = bf16[64,896]{1,0:T(8,128)(2,1)S(1)} collective-permute-done((bf16[64,896]{1,0:T(8,128)(2,1)S(1)}, bf16[64,896]{1,0:T(8,128)(2,1)S(1)}, u32[]{:S(2)}, u32[]{:S(2)}) %collective-permute-start.3) | collective-permute-done | bytes 114720 | tf_op jit(solution)/shard_map/ppermute | solution.py:32
  32.2 0.5 collective-permute-done.4.refs_6_.r3
  32.8 0.1 collective-permute-start.8
  32.9 2.8 %collective-permute-start.15 = (bf16[128,1536]{1,0:T(8,128)(2,1)S(1)}, bf16[128,1536]{1,0:T(8,128)(2,1)S(1)}, u32[]{:S(2)}, u32[]{:S(2)}) collective-permute-start(bf16[128,1536]{1,0:T(8,128)(2,1)S(1)} %copy-done.3), channel_id=1, source_target_pairs={{0,32},{16,48},{32,0},{48,16},{1,33},{17,49},{33,1},{49,17},{2,34}... | collective-permute-start | bytes 1179656 | tf_op jit(solution)/shard_map/ppermute | solution.py:32
  35.7 1.4 %collective-permute-start.16 = (bf16[128,1536]{1,0:T(8,128)(2,1)S(1)}, bf16[128,1536]{1,0:T(8,128)(2,1)S(1)}, u32[]{:S(2)}, u32[]{:S(2)}) collective-permute-start(bf16[128,1536]{1,0:T(8,128)(2,1)S(1)} %copy-done.3), channel_id=1, source_target_pairs={{0,16},{1,49},{16,32},{17,1},{32,48},{33,17},{48,0},{49,33},{2,18}... | collective-permute-start | bytes 1179656 | tf_op jit(solution)/shard_map/ppermute | solution.py:48
  37.1 0.1 assemble.1.w_ref
  37.3 0.3 latent_part.1
  37.6 2.2 %collective-permute-start.11 = (bf16[64,640]{1,0:T(8,128)(2,1)S(1)}, bf16[64,640]{1,0:T(8,128)(2,1)S(1)}, u32[]{:S(2)}, u32[]{:S(2)}) collective-permute-start(bf16[64,640]{1,0:T(8,128)(2,1)S(1)} %get-tuple-element.47.p0), channel_id=1, source_target_pairs={{0,6},{2,0},{4,2},{6,4},{1,7},{3,1},{5,3},{7,5},{8,14},{10,8},{12,... | collective-permute-start | bytes 245768 | tf_op jit(solution)/shard_map/ppermute | solution.py:32
  39.8 1.1 %collective-permute-start.10 = (bf16[64,640]{1,0:T(8,128)(2,1)S(1)}, bf16[64,640]{1,0:T(8,128)(2,1)S(1)}, u32[]{:S(2)}, u32[]{:S(2)}) collective-permute-start(bf16[64,640]{1,0:T(8,128)(2,1)S(1)} %get-tuple-element.47.p0), channel_id=1, source_target_pairs={{0,4},{2,6},{4,0},{6,2},{1,5},{3,7},{5,1},{7,3},{8,12},{10,14},{12... | collective-permute-start | bytes 245768 | tf_op jit(solution)/shard_map/ppermute | solution.py:32
  41.0 0.7 tables.1
  41.7 1.0 collective-permute-done.11.p3
  42.7 6.3 %collective-permute-done.10.p2 = bf16[64,640]{1,0:T(8,128)(2,1)S(1)} collective-permute-done((bf16[64,640]{1,0:T(8,128)(2,1)S(1)}, bf16[64,640]{1,0:T(8,128)(2,1)S(1)}, u32[]{:S(2)}, u32[]{:S(2)}) %collective-permute-start.10) | collective-permute-done | bytes 81952 | tf_op jit(solution)/shard_map/ppermute | solution.py:32
  49.0 0.3 kv_rows.1.refs_0_
  49.3 6.4 %collective-permute-start.17 = (bf16[64,640]{1,0:T(8,128)(2,1)S(1)}, bf16[64,640]{1,0:T(8,128)(2,1)S(1)}, u32[]{:S(2)}, u32[]{:S(2)}) collective-permute-start(bf16[64,640]{1,0:T(8,128)(2,1)S(1)} %kv_rows.1.refs_0_), channel_id=1, source_target_pairs={{0,8},{8,0},{1,9},{9,1},{2,10},{10,2},{3,11},{11,3},{4,12},{12,4},... | collective-permute-start | bytes 245768 | tf_op jit(solution)/shard_map/ppermute | solution.py:36
  55.7 1.7 %collective-permute-start.25 = (bf16[128,1536]{1,0:T(8,128)(2,1)S(1)}, bf16[128,1536]{1,0:T(8,128)(2,1)S(1)}, u32[]{:S(2)}, u32[]{:S(2)}) collective-permute-start(bf16[128,1536]{1,0:T(8,128)(2,1)S(1)} %copy-done.3), channel_id=1, source_target_pairs={{0,48},{1,17},{16,0},{17,33},{32,16},{33,49},{48,32},{49,1},{2,50}... | collective-permute-start | bytes 1179656 | tf_op jit(solution)/shard_map/ppermute | solution.py:48
  57.5 0.4 collective-permute-start.13
  57.8 3.5 %collective-permute-start.14 = (bf16[16,896]{1,0:T(8,128)(2,1)S(1)}, bf16[16,896]{1,0:T(8,128)(2,1)S(1)}, u32[]{:S(2)}, u32[]{:S(2)}) collective-permute-start(bf16[16,896]{1,0:T(8,128)(2,1)S(1)} %get-tuple-element.56), channel_id=1, source_target_pairs={{0,6},{2,0},{4,2},{6,4},{1,7},{3,1},{5,3},{7,5},{8,14},{10,8},{12,... | collective-permute-start | bytes 86024 | tf_op jit(solution)/shard_map/ppermute | solution.py:32
  61.3 1.8 %collective-permute-done.12.h1.refs_4_ = bf16[16,896]{1,0:T(8,128)(2,1)S(1)} collective-permute-done((bf16[16,896]{1,0:T(8,128)(2,1)S(1)}, bf16[16,896]{1,0:T(8,128)(2,1)S(1)}, u32[]{:S(2)}, u32[]{:S(2)}) %collective-permute-start.12) | collective-permute-done | bytes 28704 | tf_op jit(solution)/shard_map/ppermute | solution.py:32
  63.1 0.6 collective-permute-done.14.h3.refs_6_
  63.8 2.2 %collective-permute-start.19 = (bf16[128,640]{1,0:T(8,128)(2,1)S(1)}, bf16[128,640]{1,0:T(8,128)(2,1)S(1)}, u32[]{:S(2)}, u32[]{:S(2)}) collective-permute-start(bf16[128,640]{1,0:T(8,128)(2,1)S(1)} %pack.3.refs_0_), channel_id=1, source_target_pairs={{0,128},{64,192},{128,0},{192,64},{1,129},{65,193},{129,1},{193,65... | collective-permute-start | bytes 491528 | tf_op jit(solution)/shard_map/ppermute | solution.py:32
  66.0 3.1 %collective-permute-done.20.refs_3_ = bf16[128,640]{1,0:T(8,128)(2,1)S(1)} collective-permute-done((bf16[128,640]{1,0:T(8,128)(2,1)S(1)}, bf16[128,640]{1,0:T(8,128)(2,1)S(1)}, u32[]{:S(2)}, u32[]{:S(2)}) %collective-permute-start.20) | collective-permute-done | bytes 163872 | tf_op jit(solution)/shard_map/ppermute | solution.py:32
  69.1 1.6 %collective-permute-done.19.refs_2_ = bf16[128,640]{1,0:T(8,128)(2,1)S(1)} collective-permute-done((bf16[128,640]{1,0:T(8,128)(2,1)S(1)}, bf16[128,640]{1,0:T(8,128)(2,1)S(1)}, u32[]{:S(2)}, u32[]{:S(2)}) %collective-permute-start.19) | collective-permute-done | bytes 163872 | tf_op jit(solution)/shard_map/ppermute | solution.py:32
  70.7 1.8 %collective-permute-done.18.refs_1_ = bf16[128,640]{1,0:T(8,128)(2,1)S(1)} collective-permute-done((bf16[128,640]{1,0:T(8,128)(2,1)S(1)}, bf16[128,640]{1,0:T(8,128)(2,1)S(1)}, u32[]{:S(2)}, u32[]{:S(2)}) %collective-permute-start.18) | collective-permute-done | bytes 163872 | tf_op jit(solution)/shard_map/ppermute | solution.py:32
  72.6 1.4 %collective-permute-done.22.refs_5_ = bf16[128,640]{1,0:T(8,128)(2,1)S(1)} collective-permute-done((bf16[128,640]{1,0:T(8,128)(2,1)S(1)}, bf16[128,640]{1,0:T(8,128)(2,1)S(1)}, u32[]{:S(2)}, u32[]{:S(2)}) %collective-permute-start.22) | collective-permute-done | bytes 163872 | tf_op jit(solution)/shard_map/ppermute | solution.py:36
  73.9 3.5 %lift.1 = (bf16[8,1024,256]{2,1,0:T(8,128)(2,1)S(1)}, bf16[8,1024,256]{2,1,0:T(8,128)(2,1)S(1)}) custom-call(s32[1]{0:T(128)} %bitcast.s, s32[64]{0:T(128)S(1)} %copy-done.4, bf16[128,640]{1,0:T(8,128)(2,1)S(1)} %pack.3.refs_0_, bf16[128,640]{1,0:T(8,128)(2,1)S(1)} %collective-permute-done.18.refs_1_, bf16[128,640]{1,0:T(8,128)(2,1)S(1)} %collective-permute-done.19.refs_2_, ...), custom_call_target="tpu_custom_call" | custom-call | tf_op jit(solution)/shard_map/lift/pallas_call | solution.py:272
  77.4 3.7 %attend.2 = (bf16[128,1152]{1,0:T(8,128)(2,1)S(1)}, bf16[128,1152]{1,0:T(8,128)(2,1)S(1)}) custom-call(s32[1]{0:T(128)} %bitcast.s, s32[64]{0:T(128)S(1)} %copy-done.4, bf16[128,1536]{1,0:T(8,128)(2,1)S(1)} %collective-permute-done.15.refs_2_.refs_0_, bf16[128,1536]{1,0:T(8,128)(2,1)S(1)} %collective-permute-done.16.refs_3_.refs_1_, ...), custom_call_target="tpu_custom_call" | custom-call | tf_op jit(solution)/shard_map/attend/pallas_call | solution.py:352
  81.1 0.6 collective-permute-start.27
  81.6 3.6 %attend.3 = (bf16[128,1152]{1,0:T(8,128)(2,1)S(1)}, bf16[128,1152]{1,0:T(8,128)(2,1)S(1)}) custom-call(s32[1]{0:T(128)} %bitcast.s, s32[64]{0:T(128)S(1)} %copy-done.4, bf16[128,1536]{1,0:T(8,128)(2,1)S(1)} %collective-permute-done.25.refs_0_, bf16[128,1536]{1,0:T(8,128)(2,1)S(1)} %copy-done.3, bf16[8,1024,256]{2,1,0:T(8,128)(2,1)S(1)} %get-tuple-element.67.refs_2_, ...), custom_call_target="tpu_custom_call" | custom-call | tf_op jit(solution)/shard_map/attend/pallas_call | solution.py:352
  85.3 3.1 %collective-permute-start.26 = (bf16[128,1152]{1,0:T(8,128)(2,1)S(1)}, bf16[128,1152]{1,0:T(8,128)(2,1)S(1)}, u32[]{:S(2)}, u32[]{:S(2)}) collective-permute-start(bf16[128,1152]{1,0:T(8,128)(2,1)S(1)} %get-tuple-element.73), channel_id=1, source_target_pairs={{0,48},{1,17},{16,0},{17,33},{32,16},{33,49},{48,32},{49,1},{2,50}... | collective-permute-start | bytes 884744 | tf_op jit(solution)/shard_map/ppermute | solution.py:48
  88.3 1.0 collective-permute-done.27.got_ref
  89.3 0.5 relay.1
  89.9 0.7 hidden_rows.1
  90.6 3.6 %collective-permute-done.26.b_ref = bf16[128,1152]{1,0:T(8,128)(2,1)S(1)} collective-permute-done((bf16[128,1152]{1,0:T(8,128)(2,1)S(1)}, bf16[128,1152]{1,0:T(8,128)(2,1)S(1)}, u32[]{:S(2)}, u32[]{:S(2)}) %collective-permute-start.26) | collective-permute-done | bytes 294944 | tf_op jit(solution)/shard_map/ppermute | solution.py:48
  94.2 3.7 %collective-permute-done.28.c_ref = bf16[128,1152]{1,0:T(8,128)(2,1)S(1)} collective-permute-done((bf16[128,1152]{1,0:T(8,128)(2,1)S(1)}, bf16[128,1152]{1,0:T(8,128)(2,1)S(1)}, u32[]{:S(2)}, u32[]{:S(2)}) %collective-permute-start.28) | collective-permute-done | bytes 294944 | tf_op jit(solution)/shard_map/ppermute | solution.py:48
  97.8 1.4 %merge.1 = bf16[128,1024]{1,0:T(8,128)(2,1)} custom-call(bf16[128,1152]{1,0:T(8,128)(2,1)S(1)} %get-tuple-element.72.a_ref, bf16[128,1152]{1,0:T(8,128)(2,1)S(1)} %collective-permute-done.26.b_ref, bf16[128,1152]{1,0:T(8,128)(2,1)S(1)} %collective-permute-done.28.c_ref), custom_call_target="tpu_custom_call" | custom-call | tf_op jit(solution)/shard_map/merge/pallas_call | solution.py:389
  (40 shorter events, 0.3 us)
Async XLA Ops:
  0.6 12.1 %collective-permute-start = (bf16[112,576]{1,0:T(8,128)(2,1)}, bf16[112,576]{1,0:T(8,128)(2,1)S(1)}, u32[]{:S(2)}, u32[]{:S(2)}) collective-permute-start(bf16[112,576]{1,0:T(8,128)(2,1)} %param.19), channel_id=1, source_target_pairs={{0,0},{8,1},{64,2},{72,3},{128,4},{136,5},{192,6},{200,7},{1,8},{9... | collective-permute-start | bytes 387080 | tf_op jit(solution)/shard_map/ppermute | solution.py:63
  6.8 26.0 %copy-start.3 = (bf16[128,1536]{1,0:T(8,128)(2,1)S(1)}, bf16[128,1536]{1,0:T(8,128)(2,1)}, u32[]{:S(2)}) copy-start(bf16[128,1536]{1,0:T(8,128)(2,1)} %refs_1_.1) | copy-start | bytes 1179652
  6.9 30.2 %copy-start.5 = (bf16[3584]{0:T(1024)(128)(2,1)S(1)}, bf16[3584]{0:T(1024)(128)(2,1)}, u32[]{:S(2)}) copy-start(bf16[3584]{0:T(1024)(128)(2,1)} %param.18) | copy-start | bytes 21508
  12.7 28.3 %copy-start.6 = (bf16[512]{0:T(512)(128)(2,1)S(1)}, bf16[512]{0:T(512)(128)(2,1)}, u32[]{:S(2)}) copy-start(bf16[512]{0:T(512)(128)(2,1)} %param.20) | copy-start | bytes 3076
  12.7 28.3 %copy-start.4 = (s32[64]{0:T(128)S(1)}, s32[64]{0:T(128)}, u32[]{:S(2)}) copy-start(s32[64]{0:T(128)} %seg.6) | copy-start | bytes 772
  12.7 7.2 %collective-permute-start.1 = (bf16[4,64,896]{2,1,0:T(8,128)(2,1)}, bf16[4,64,896]{2,1,0:T(8,128)(2,1)S(1)}, u32[]{:S(2)}, u32[]{:S(2)}) collective-permute-start(bf16[4,64,896]{2,1,0:T(8,128)(2,1)} %get-tuple-element.41), channel_id=1, source_target_pairs={{0,1},{1,0},{2,3},{3,2},{4,5},{5,4},{6,7},{7,6},{8,9},{9,8},{10,11... | collective-permute-start | bytes 1376264 | tf_op jit(solution)/shard_map/ppermute | solution.py:36
  15.8 9.0 %collective-permute-start.7 = (bf16[1,112,576]{2,1,0:T(8,128)(2,1)S(1)}, bf16[1,112,576]{2,1,0:T(8,128)(2,1)S(1)}, u32[]{:S(2)}, u32[]{:S(2)}) collective-permute-start(bf16[1,112,576]{2,1,0:T(8,128)(2,1)S(1)} %bitcast.3), channel_id=1, source_target_pairs={{0,48},{16,32},{32,16},{48,0},{1,49},{17,33},{33,17},{49,1},{2,50}... | collective-permute-start | bytes 387080 | tf_op jit(solution)/shard_map/ppermute | solution.py:36
  18.5 8.4 %collective-permute-start.6 = (bf16[1,112,576]{2,1,0:T(8,128)(2,1)S(1)}, bf16[1,112,576]{2,1,0:T(8,128)(2,1)S(1)}, u32[]{:S(2)}, u32[]{:S(2)}) collective-permute-start(bf16[1,112,576]{2,1,0:T(8,128)(2,1)S(1)} %bitcast.4), channel_id=1, source_target_pairs={{0,32},{16,48},{32,0},{48,16},{1,33},{17,49},{33,1},{49,17},{2,34}... | collective-permute-start | bytes 387080 | tf_op jit(solution)/shard_map/ppermute | solution.py:36
  19.3 7.6 %collective-permute-start.5 = (bf16[1,112,576]{2,1,0:T(8,128)(2,1)S(1)}, bf16[1,112,576]{2,1,0:T(8,128)(2,1)S(1)}, u32[]{:S(2)}, u32[]{:S(2)}) collective-permute-start(bf16[1,112,576]{2,1,0:T(8,128)(2,1)S(1)} %bitcast.5), channel_id=1, source_target_pairs={{0,16},{16,0},{32,48},{48,32},{1,17},{17,1},{33,49},{49,33},{2,18}... | collective-permute-start | bytes 387080 | tf_op jit(solution)/shard_map/ppermute | solution.py:36
  19.9 1.0 %copy-start.1 = (bf16[4,64,896]{2,1,0:T(8,128)(2,1)S(1)}, bf16[4,64,896]{2,1,0:T(8,128)(2,1)}, u32[]{:S(2)}) copy-start(bf16[4,64,896]{2,1,0:T(8,128)(2,1)} %get-tuple-element.39.keep_ref) | copy-start | bytes 1376260
  20.9 16.4 %copy-start.2 = (bf16[4,64,896]{2,1,0:T(8,128)(2,1)S(1)}, bf16[4,64,896]{2,1,0:T(8,128)(2,1)}, u32[]{:S(2)}) copy-start(bf16[4,64,896]{2,1,0:T(8,128)(2,1)} %get-tuple-element.39.keep_ref) | copy-start | bytes 1376260
  21.0 53.0 %copy-start = (bf16[512,2048]{1,0:T(8,128)(2,1)S(1)}, bf16[512,2048]{1,0:T(8,128)(2,1)}, u32[]{:S(2)}) copy-start(bf16[512,2048]{1,0:T(8,128)(2,1)} %refs_8_.1) | copy-start | bytes 6291460
  21.0 8.0 %collective-permute-start.2 = (bf16[64,896]{1,0:T(8,128)(2,1)S(1)}, bf16[64,896]{1,0:T(8,128)(2,1)S(1)}, u32[]{:S(2)}, u32[]{:S(2)}) collective-permute-start(bf16[64,896]{1,0:T(8,128)(2,1)S(1)} %get-tuple-element.42), channel_id=1, source_target_pairs={{0,2},{2,4},{4,6},{6,0},{1,3},{3,5},{5,7},{7,1},{8,10},{10,12},{12... | collective-permute-start | bytes 344072 | tf_op jit(solution)/shard_map/ppermute | solution.py:32
  21.9 10.3 %collective-permute-start.3 = (bf16[64,896]{1,0:T(8,128)(2,1)S(1)}, bf16[64,896]{1,0:T(8,128)(2,1)S(1)}, u32[]{:S(2)}, u32[]{:S(2)}) collective-permute-start(bf16[64,896]{1,0:T(8,128)(2,1)S(1)} %get-tuple-element.43), channel_id=1, source_target_pairs={{0,4},{2,6},{4,0},{6,2},{1,5},{3,7},{5,1},{7,3},{8,12},{10,14},{12... | collective-permute-start | bytes 344072 | tf_op jit(solution)/shard_map/ppermute | solution.py:32
  24.8 7.9 %collective-permute-start.4 = (bf16[64,896]{1,0:T(8,128)(2,1)S(1)}, bf16[64,896]{1,0:T(8,128)(2,1)S(1)}, u32[]{:S(2)}, u32[]{:S(2)}) collective-permute-start(bf16[64,896]{1,0:T(8,128)(2,1)S(1)} %get-tuple-element.44), channel_id=1, source_target_pairs={{0,6},{2,0},{4,2},{6,4},{1,7},{3,1},{5,3},{7,5},{8,14},{10,8},{12,... | collective-permute-start | bytes 344072 | tf_op jit(solution)/shard_map/ppermute | solution.py:32
  32.8 4.3 %collective-permute-start.8 = (bf16[4,112,576]{2,1,0:T(8,128)(2,1)S(1)}, bf16[4,112,576]{2,1,0:T(8,128)(2,1)S(1)}, u32[]{:S(2)}, u32[]{:S(2)}) collective-permute-start(bf16[4,112,576]{2,1,0:T(8,128)(2,1)S(1)} %pack.2.own_ref), channel_id=1, source_target_pairs={{0,1},{1,0},{2,3},{3,2},{4,5},{5,4},{6,7},{7,6},{8,9},{9,8},{10,11... | collective-permute-start | bytes 1548296 | tf_op jit(solution)/shard_map/ppermute | solution.py:36
  32.9 22.8 %collective-permute-start.15 = (bf16[128,1536]{1,0:T(8,128)(2,1)S(1)}, bf16[128,1536]{1,0:T(8,128)(2,1)S(1)}, u32[]{:S(2)}, u32[]{:S(2)}) collective-permute-start(bf16[128,1536]{1,0:T(8,128)(2,1)S(1)} %copy-done.3), channel_id=1, source_target_pairs={{0,32},{16,48},{32,0},{48,16},{1,33},{17,49},{33,1},{49,17},{2,34}... | collective-permute-start | bytes 1179656 | tf_op jit(solution)/shard_map/ppermute | solution.py:32
  35.7 22.1 %collective-permute-start.16 = (bf16[128,1536]{1,0:T(8,128)(2,1)S(1)}, bf16[128,1536]{1,0:T(8,128)(2,1)S(1)}, u32[]{:S(2)}, u32[]{:S(2)}) collective-permute-start(bf16[128,1536]{1,0:T(8,128)(2,1)S(1)} %copy-done.3), channel_id=1, source_target_pairs={{0,16},{1,49},{16,32},{17,1},{32,48},{33,17},{48,0},{49,33},{2,18}... | collective-permute-start | bytes 1179656 | tf_op jit(solution)/shard_map/ppermute | solution.py:48
  37.6 5.1 %collective-permute-start.11 = (bf16[64,640]{1,0:T(8,128)(2,1)S(1)}, bf16[64,640]{1,0:T(8,128)(2,1)S(1)}, u32[]{:S(2)}, u32[]{:S(2)}) collective-permute-start(bf16[64,640]{1,0:T(8,128)(2,1)S(1)} %get-tuple-element.47.p0), channel_id=1, source_target_pairs={{0,6},{2,0},{4,2},{6,4},{1,7},{3,1},{5,3},{7,5},{8,14},{10,8},{12,... | collective-permute-start | bytes 245768 | tf_op jit(solution)/shard_map/ppermute | solution.py:32
  39.8 9.1 %collective-permute-start.10 = (bf16[64,640]{1,0:T(8,128)(2,1)S(1)}, bf16[64,640]{1,0:T(8,128)(2,1)S(1)}, u32[]{:S(2)}, u32[]{:S(2)}) collective-permute-start(bf16[64,640]{1,0:T(8,128)(2,1)S(1)} %get-tuple-element.47.p0), channel_id=1, source_target_pairs={{0,4},{2,6},{4,0},{6,2},{1,5},{3,7},{5,1},{7,3},{8,12},{10,14},{12... | collective-permute-start | bytes 245768 | tf_op jit(solution)/shard_map/ppermute | solution.py:32
  40.9 8.1 %collective-permute-start.9 = (bf16[64,640]{1,0:T(8,128)(2,1)S(1)}, bf16[64,640]{1,0:T(8,128)(2,1)S(1)}, u32[]{:S(2)}, u32[]{:S(2)}) collective-permute-start(bf16[64,640]{1,0:T(8,128)(2,1)S(1)} %get-tuple-element.47.p0), channel_id=1, source_target_pairs={{0,2},{2,4},{4,6},{6,0},{1,3},{3,5},{5,7},{7,1},{8,10},{10,12},{12... | collective-permute-start | bytes 245768 | tf_op jit(solution)/shard_map/ppermute | solution.py:32
  49.3 14.4 %collective-permute-start.17 = (bf16[64,640]{1,0:T(8,128)(2,1)S(1)}, bf16[64,640]{1,0:T(8,128)(2,1)S(1)}, u32[]{:S(2)}, u32[]{:S(2)}) collective-permute-start(bf16[64,640]{1,0:T(8,128)(2,1)S(1)} %kv_rows.1.refs_0_), channel_id=1, source_target_pairs={{0,8},{8,0},{1,9},{9,1},{2,10},{10,2},{3,11},{11,3},{4,12},{12,4},... | collective-permute-start | bytes 245768 | tf_op jit(solution)/shard_map/ppermute | solution.py:36
  55.7 16.9 %collective-permute-start.25 = (bf16[128,1536]{1,0:T(8,128)(2,1)S(1)}, bf16[128,1536]{1,0:T(8,128)(2,1)S(1)}, u32[]{:S(2)}, u32[]{:S(2)}) collective-permute-start(bf16[128,1536]{1,0:T(8,128)(2,1)S(1)} %copy-done.3), channel_id=1, source_target_pairs={{0,48},{1,17},{16,0},{17,33},{32,16},{33,49},{48,32},{49,1},{2,50}... | collective-permute-start | bytes 1179656 | tf_op jit(solution)/shard_map/ppermute | solution.py:48
  57.4 5.7 %collective-permute-start.12 = (bf16[16,896]{1,0:T(8,128)(2,1)S(1)}, bf16[16,896]{1,0:T(8,128)(2,1)S(1)}, u32[]{:S(2)}, u32[]{:S(2)}) collective-permute-start(bf16[16,896]{1,0:T(8,128)(2,1)S(1)} %get-tuple-element.54), channel_id=1, source_target_pairs={{0,2},{2,4},{4,6},{6,0},{1,3},{3,5},{5,7},{7,1},{8,10},{10,12},{12... | collective-permute-start | bytes 86024 | tf_op jit(solution)/shard_map/ppermute | solution.py:32
  57.5 5.7 %collective-permute-start.13 = (bf16[16,896]{1,0:T(8,128)(2,1)S(1)}, bf16[16,896]{1,0:T(8,128)(2,1)S(1)}, u32[]{:S(2)}, u32[]{:S(2)}) collective-permute-start(bf16[16,896]{1,0:T(8,128)(2,1)S(1)} %get-tuple-element.55), channel_id=1, source_target_pairs={{0,4},{2,6},{4,0},{6,2},{1,5},{3,7},{5,1},{7,3},{8,12},{10,14},{12... | collective-permute-start | bytes 86024 | tf_op jit(solution)/shard_map/ppermute | solution.py:32
  57.8 5.9 %collective-permute-start.14 = (bf16[16,896]{1,0:T(8,128)(2,1)S(1)}, bf16[16,896]{1,0:T(8,128)(2,1)S(1)}, u32[]{:S(2)}, u32[]{:S(2)}) collective-permute-start(bf16[16,896]{1,0:T(8,128)(2,1)S(1)} %get-tuple-element.56), channel_id=1, source_target_pairs={{0,6},{2,0},{4,2},{6,4},{1,7},{3,1},{5,3},{7,5},{8,14},{10,8},{12,... | collective-permute-start | bytes 86024 | tf_op jit(solution)/shard_map/ppermute | solution.py:32
  63.7 5.4 %collective-permute-start.20 = (bf16[128,640]{1,0:T(8,128)(2,1)S(1)}, bf16[128,640]{1,0:T(8,128)(2,1)S(1)}, u32[]{:S(2)}, u32[]{:S(2)}) collective-permute-start(bf16[128,640]{1,0:T(8,128)(2,1)S(1)} %pack.3.refs_0_), channel_id=1, source_target_pairs={{0,64},{64,128},{128,192},{192,0},{1,65},{65,129},{129,193},{193,1... | collective-permute-start | bytes 491528 | tf_op jit(solution)/shard_map/ppermute | solution.py:32
  63.8 6.9 %collective-permute-start.19 = (bf16[128,640]{1,0:T(8,128)(2,1)S(1)}, bf16[128,640]{1,0:T(8,128)(2,1)S(1)}, u32[]{:S(2)}, u32[]{:S(2)}) collective-permute-start(bf16[128,640]{1,0:T(8,128)(2,1)S(1)} %pack.3.refs_0_), channel_id=1, source_target_pairs={{0,128},{64,192},{128,0},{192,64},{1,129},{65,193},{129,1},{193,65... | collective-permute-start | bytes 491528 | tf_op jit(solution)/shard_map/ppermute | solution.py:32
  66.0 6.5 %collective-permute-start.18 = (bf16[128,640]{1,0:T(8,128)(2,1)S(1)}, bf16[128,640]{1,0:T(8,128)(2,1)S(1)}, u32[]{:S(2)}, u32[]{:S(2)}) collective-permute-start(bf16[128,640]{1,0:T(8,128)(2,1)S(1)} %pack.3.refs_0_), channel_id=1, source_target_pairs={{0,192},{64,0},{128,64},{192,128},{1,193},{65,1},{129,65},{193,129... | collective-permute-start | bytes 491528 | tf_op jit(solution)/shard_map/ppermute | solution.py:32
  66.0 6.5 %collective-permute-start.21 = (bf16[128,640]{1,0:T(8,128)(2,1)S(1)}, bf16[128,640]{1,0:T(8,128)(2,1)S(1)}, u32[]{:S(2)}, u32[]{:S(2)}) collective-permute-start(bf16[128,640]{1,0:T(8,128)(2,1)S(1)} %pack.3.refs_0_), channel_id=1, source_target_pairs={{0,1},{1,0},{2,3},{3,2},{4,5},{5,4},{6,7},{7,6},{8,9},{9,8},{10,11... | collective-permute-start | bytes 491528 | tf_op jit(solution)/shard_map/ppermute | solution.py:36
  69.1 3.5 %collective-permute-start.24 = (bf16[128,640]{1,0:T(8,128)(2,1)S(1)}, bf16[128,640]{1,0:T(8,128)(2,1)S(1)}, u32[]{:S(2)}, u32[]{:S(2)}) collective-permute-start(bf16[128,640]{1,0:T(8,128)(2,1)S(1)} %collective-permute-done.20.refs_3_), channel_id=1, source_target_pairs={{0,1},{1,0},{2,3},{3,2},{4,5},{5,4},{6,7},{7,6},{8,9},{9,8},{10,11... | collective-permute-start | bytes 491528 | tf_op jit(solution)/shard_map/ppermute | solution.py:36
  70.7 1.9 %collective-permute-start.23 = (bf16[128,640]{1,0:T(8,128)(2,1)S(1)}, bf16[128,640]{1,0:T(8,128)(2,1)S(1)}, u32[]{:S(2)}, u32[]{:S(2)}) collective-permute-start(bf16[128,640]{1,0:T(8,128)(2,1)S(1)} %collective-permute-done.19.refs_2_), channel_id=1, source_target_pairs={{0,1},{1,0},{2,3},{3,2},{4,5},{5,4},{6,7},{7,6},{8,9},{9,8},{10,11... | collective-permute-start | bytes 491528 | tf_op jit(solution)/shard_map/ppermute | solution.py:36
  72.5 1.4 %collective-permute-start.22 = (bf16[128,640]{1,0:T(8,128)(2,1)S(1)}, bf16[128,640]{1,0:T(8,128)(2,1)S(1)}, u32[]{:S(2)}, u32[]{:S(2)}) collective-permute-start(bf16[128,640]{1,0:T(8,128)(2,1)S(1)} %collective-permute-done.18.refs_1_), channel_id=1, source_target_pairs={{0,1},{1,0},{2,3},{3,2},{4,5},{5,4},{6,7},{7,6},{8,9},{9,8},{10,11... | collective-permute-start | bytes 491528 | tf_op jit(solution)/shard_map/ppermute | solution.py:36
  81.1 8.2 %collective-permute-start.27 = (bf16[128,1152]{1,0:T(8,128)(2,1)S(1)}, bf16[128,1152]{1,0:T(8,128)(2,1)S(1)}, u32[]{:S(2)}, u32[]{:S(2)}) collective-permute-start(bf16[128,1152]{1,0:T(8,128)(2,1)S(1)} %get-tuple-element.74), channel_id=1, source_target_pairs={{0,16},{1,49},{16,32},{17,1},{32,48},{33,17},{48,0},{49,33},{2,18}... | collective-permute-start | bytes 884744 | tf_op jit(solution)/shard_map/ppermute | solution.py:48
  85.3 8.9 %collective-permute-start.26 = (bf16[128,1152]{1,0:T(8,128)(2,1)S(1)}, bf16[128,1152]{1,0:T(8,128)(2,1)S(1)}, u32[]{:S(2)}, u32[]{:S(2)}) collective-permute-start(bf16[128,1152]{1,0:T(8,128)(2,1)S(1)} %get-tuple-element.73), channel_id=1, source_target_pairs={{0,48},{1,17},{16,0},{17,33},{32,16},{33,49},{48,32},{49,1},{2,50}... | collective-permute-start | bytes 884744 | tf_op jit(solution)/shard_map/ppermute | solution.py:48
  89.8 8.0 %collective-permute-start.28 = (bf16[128,1152]{1,0:T(8,128)(2,1)S(1)}, bf16[128,1152]{1,0:T(8,128)(2,1)S(1)}, u32[]{:S(2)}, u32[]{:S(2)}) collective-permute-start(bf16[128,1152]{1,0:T(8,128)(2,1)S(1)} %relay.1), channel_id=1, source_target_pairs={{0,16},{1,49},{16,32},{17,1},{32,48},{33,17},{48,0},{49,33},{2,18}... | collective-permute-start | bytes 884744 | tf_op jit(solution)/shard_map/ppermute | solution.py:48

commit v3 on v2

--- a/solution.py
+++ b/solution.py
@@ -52,15 +52,23 @@
     return lax.optimization_barrier(values)
 
 
-def transposed_block(value):
+def near_block(value):
+    same = ((1, 0), (1, 1), (2, 0), (2, 1))
+    crossing = ((3, 0), (3, 1), (0, 0), (0, 1))
     perm = []
     for y in range(4):
         for x in range(4):
             for zh in range(2):
                 for zl in range(4):
                     for core in range(2):
-                        perm.append((flat(zl, x, core, y, zh), flat(y, x, zh, zl, core)))
+                        source = same[zl] if core == zh else crossing[zl]
+                        perm.append((flat(y ^ zl, x, core, *source), flat(y, x, zh, zl, core)))
     return lax.ppermute(value, AXES, perm)
+
+
+def cross(value):
+    perm = [(zh * 4 + zl, (1 - zh) * 4 + (zl ^ 2)) for zh in range(2) for zl in range(4)]
+    return lax.ppermute(value, ("zh", "zl"), perm)
 
 
 def coords(s):
@@ -69,7 +77,7 @@
 
 
 def params(mib):
-    return pltpu.CompilerParams(vmem_limit_bytes=mib * MIB)
+    return pltpu.CompilerParams(vmem_limit_bytes=int(mib * MIB))
 
 
 def shape(dims, dtype=BF):
@@ -77,8 +85,8 @@
 
 
 def project_kernel(s, x_hbm, ad_hbm, w_hbm, au_hbm, res_hbm, send_ref, keep_ref, x, ad, w, au, res, xr, kept, sem):
-    _, _, _, zl, core = coords(s)
-    columns = [pl.ds(pl.multiple_of((zl + k) % 4 * COLS, 128), COLS) for k in ORDER]
+    y, _, _, zl, core = coords(s)
+    columns = [pl.ds(pl.multiple_of((y ^ ((zl + k) % 4)) * COLS, 128), COLS) for k in ORDER]
 
     def fetch(source, target, index):
         copy = pltpu.make_async_copy(source, target, sem.at[index])
@@ -127,7 +135,7 @@
             pltpu.VMEM((64, COLS), F32),
             pltpu.SemaphoreType.DMA((8,)),
         ],
-        compiler_params=params(56),
+        compiler_params=params(52.5),
         name="project",
     )(scalars, *operands)
 
@@ -203,7 +211,7 @@
 
 
 def latent_kernel(s, keep_ref, got_ref, r1, r2, r3, gain_ref, w_ref, part_ref, h0, h1, h2, h3, hid):
-    _, _, _, zl, _ = coords(s)
+    y, _, _, zl, _ = coords(s)
     total = sum(ref[...].astype(F32) for ref in (keep_ref.at[3], got_ref.at[3], r1, r2, r3))
     hidden = total.astype(BF)
     hid[...] = hidden
@@ -211,7 +219,7 @@
         out[...] = hid[pl.ds(pl.multiple_of(((zl + k) % 4) * 16, 16), 16), :]
     wide = hidden.astype(F32)
     squares = jnp.sum(wide * wide, axis=1, keepdims=True)
-    gain = gain_ref[:, pl.ds(pl.multiple_of(zl * COLS, 128), COLS)].astype(F32)
+    gain = gain_ref[:, pl.ds(pl.multiple_of((y ^ zl) * COLS, 128), COLS)].astype(F32)
     part = dot((wide * gain).astype(BF), w_ref[...])
     lane = lax.broadcasted_iota(jnp.int32, (64, 128), 1)
     high = squares.astype(BF).astype(F32)
@@ -390,9 +398,9 @@
 
 
 def hidden_kernel(s, h0, h1, h2, h3, out_ref):
-    _, _, _, zl, _ = coords(s)
+    y, _, _, zl, _ = coords(s)
     for k, ref in enumerate((h0, h1, h2, h3)):
-        column = pl.multiple_of(((zl + 4 - k) % 4) * COLS, 128)
+        column = pl.multiple_of((y ^ ((zl + 4 - k) % 4)) * COLS, 128)
         out_ref[:, pl.ds(column, COLS)] = ref[...]
 
 
@@ -416,7 +424,7 @@
     scalars = lax.axis_index(AXES).astype(jnp.int32).reshape(1)
     near, away, far, back = 0, 1, 2, 3
 
-    block = transposed_block(latent_key_weight)[None]
+    block = near_block(latent_key_weight)[None]
     send, keep = project(
         scalars,
         attention_input.reshape(4, 2, 16, 1024),
@@ -441,7 +449,7 @@
     p1, p2, p3 = (shift(part, "zl", k) for k in (1, 2, 3))
     rows = kv_rows([part, p1, p2, p3], cosine, sine, latent_norm_gain.reshape(1, -1))
     rows, h1, h2, h3 = tie(rows, h1, h2, h3)
-    beside = swap(rows, "zh")
+    beside = cross(rows)
     pieces = [h0] + [shift(h, "zl", k) for k, h in ((1, h1), (2, h2), (3, h3))]
     both = pack([rows, beside], (q_far, q_back, *pieces[1:]))
     column = [both] + [shift(both, "y", -k) for k in (1, 2, 3)]
@@ -449,12 +457,12 @@
 
     *keys, q_away = tie(*keys, q_away)
     lifted = lift(scalars, segment_ordering, keys, latent_up_weight)
-    relayed, direct = attend((far, back), scalars, segment_ordering, [q_far, q_back], lifted)
+    (relayed,) = attend((far,), scalars, segment_ordering, [q_far], lifted)
     got = turn(relayed, 1)
-    mine, own = attend((away, near), scalars, segment_ordering, [q_away, queries], lifted)
-    direct, own = tie(direct, own)
+    direct, mine = attend((back, away), scalars, segment_ordering, [q_back, q_away], lifted)
     direct = turn(direct, -1)
     passed = turn(relay(got, mine), 1)
+    (own,) = attend((near,), scalars, segment_ordering, [queries], lifted)
     hidden = hidden_rows(scalars, pieces)
     return hidden, merge(own, direct, passed)
 

time: 100 us -> 93.3 us (0.933)
  starting transfers between devices: 43.7 us -> 35.6 us
  Pallas kernels: 20.7 us -> 22 us
    ppermute x10 -> x9, starting transfers between devices: 13.7 us -> 4.38 us  [swap(): return lax.ppermute(value, axis, [(i, i ^ bit) for i in range(size)])]
    ppermute x1 -> x2, starting transfers between devices: 6.19 us -> 9.46 us  [the longest x1 7.06 us: near_block(): return lax.ppermute(value, AXES, perm)]
    ppermute x10 -> x9, waiting for transfers between devices: 2.55 us -> 5.36 us  [swap(): return lax.ppermute(value, axis, [(i, i ^ bit) for i in range(size)])]
    ppermute x5, waiting for transfers between devices: 8.22 us -> 5.69 us  [turn(): return lax.ppermute(value, ('x', 'core'), perm)]
    pallas_call x2 -> x3, Pallas kernels: 7.3 us -> 9.56 us  [attend(): local(kernel, outs, 32, 'attend', 2, len(chunks) + 2)]
    ppermute x5, starting transfers between devices: 6.87 us -> 5.51 us  [turn(): return lax.ppermute(value, ('x', 'core'), perm)]
  transfers between devices with their start and end apart: 29 -> 29, of which waited for: 15 -> 17; matrix products, arithmetic and copies ran while one was open for 0% -> 0% of each run, Pallas kernels for 12% -> 15%
where the time goes in v3:
time: 93.3 us; the launch traced here: 92.5 us
  starting transfers between devices  35.6 us (38%)
  waiting for transfers between devices  32.1 us (34%)
  Pallas kernels  22 us (24%)
  local copies, waits for them, and re-layouts  1.89 us (2%)
    ppermute x13, waiting for transfers between devices, shift(): return lax.ppermute(value, axis, [(i, (i + k) % 4) for i in range(4)])  21.1 us
    ppermute x13, starting transfers between devices, shift(): return lax.ppermute(value, axis, [(i, (i + k) % 4) for i in range(4)])  16.3 us
    pallas_call x3, Pallas kernels, attend(): local(kernel, outs, 32, 'attend', 2, len(chunks) + 2)  9.56 us
    ppermute x1, starting transfers between devices, near_block(): return lax.ppermute(value, AXES, perm)  7.06 us
    ppermute x5, waiting for transfers between devices, turn(): return lax.ppermute(value, ('x', 'core'), perm)  5.69 us
    ppermute x5, starting transfers between devices, turn(): return lax.ppermute(value, ('x', 'core'), perm)  5.51 us
    ppermute x9, waiting for transfers between devices, swap(): return lax.ppermute(value, axis, [(i, i ^ bit) for i in range(size)])  5.36 us
    pallas_call x1, Pallas kernels, project(): pl.pallas_call(project_kernel, in_specs=[pl.BlockSpec(memory_space=pltpu....  4.83 us
  transfers between devices with their start and end apart: 29, of which 17 were waited for; matrix products, arithmetic and copies ran while one was open for 0% of the time, Pallas kernels for 15%

profile of v3, /device:TPU:24, one launch (start us, length us, event | category | flops | bytes accessed | tf_op | source)
XLA Modules:
  0.0 92.5 jit_solution(12516353576754361469)
XLA Ops:
  0.6 7.1 %collective-permute-start = (bf16[112,576]{1,0:T(8,128)(2,1)}, bf16[112,576]{1,0:T(8,128)(2,1)S(1)}, u32[]{:S(2)}, u32[]{:S(2)}) collective-permute-start(bf16[112,576]{1,0:T(8,128)(2,1)} %param.19), channel_id=1, source_target_pairs={{2,0},{14,1},{67,2},{79,3},{132,4},{136,5},{197,6},{201,7},{6,8},{... | collective-permute-start | bytes 387080 | tf_op jit(solution)/shard_map/ppermute | solution.py:66
  7.7 0.9 %copy-done.2 = bf16[128,1024]{1,0:T(8,128)(2,1)S(1)} copy-done((bf16[128,1024]{1,0:T(8,128)(2,1)S(1)}, bf16[128,1024]{1,0:T(8,128)(2,1)}, u32[]{:S(2)}) %copy-start.2) | copy-done | bytes 262168
  8.6 0.9 copy-done.3
  9.5 4.8 %project.1 = (bf16[4,64,896]{2,1,0:T(8,128)(2,1)S(1)}, bf16[4,64,896]{2,1,0:T(8,128)(2,1)S(1)}) custom-call(s32[1]{0:T(128)} %bitcast.s, bf16[4,2,16,1024]{3,2,1,0:T(8,128)(2,1)S(1)} %bitcast.3, bf16[1024,256]{1,0:T(8,128)(2,1)} %ad_hbm.1, bf16[1024,3584]{1,0:T(8,128)(2,1)} %w_hbm.1, bf16[256,3584]{1,0:T(8,128)(2,1)} %au_hbm.1, bf16[16,3584]{1,0:T(8,128)(2,1)S(1)} %copy-done.3), custom_call_target="tpu_custom_call" | custom-call | tf_op jit(solution)/shard_map/project/pallas_call | solution.py:123
  14.5 2.8 %collective-permute-start.7 = (bf16[1,112,576]{2,1,0:T(8,128)(2,1)S(1)}, bf16[1,112,576]{2,1,0:T(8,128)(2,1)S(1)}, u32[]{:S(2)}, u32[]{:S(2)}) collective-permute-start(bf16[1,112,576]{2,1,0:T(8,128)(2,1)S(1)} %bitcast.4), channel_id=1, source_target_pairs={{0,48},{16,32},{32,16},{48,0},{1,49},{17,33},{33,17},{49,1},{2,50}... | collective-permute-start | bytes 387080 | tf_op jit(solution)/shard_map/ppermute | solution.py:36
  17.4 0.8 collective-permute-start.6
  18.2 0.5 collective-permute-start.5
  18.9 2.0 %collective-permute-start.3 = (bf16[64,896]{1,0:T(8,128)(2,1)S(1)}, bf16[64,896]{1,0:T(8,128)(2,1)S(1)}, u32[]{:S(2)}, u32[]{:S(2)}) collective-permute-start(bf16[64,896]{1,0:T(8,128)(2,1)S(1)} %get-tuple-element.39), channel_id=1, source_target_pairs={{0,4},{2,6},{4,0},{6,2},{1,5},{3,7},{5,1},{7,3},{8,12},{10,14},{12... | collective-permute-start | bytes 344072 | tf_op jit(solution)/shard_map/ppermute | solution.py:32
  20.9 3.6 %collective-permute-done.7.refs_3_ = bf16[1,112,576]{2,1,0:T(8,128)(2,1)S(1)} collective-permute-done((bf16[1,112,576]{2,1,0:T(8,128)(2,1)S(1)}, bf16[1,112,576]{2,1,0:T(8,128)(2,1)S(1)}, u32[]{:S(2)}, u32[]{:S(2)}) %collective-permute-start.7) | collective-permute-done | bytes 129056 | tf_op jit(solution)/shard_map/ppermute | solution.py:36
  24.4 0.8 collective-permute-start.4
  25.2 0.3 collective-permute-done.6.refs_2_
  25.6 1.2 %collective-permute-done.2.refs_4_.r1 = bf16[64,896]{1,0:T(8,128)(2,1)S(1)} collective-permute-done((bf16[64,896]{1,0:T(8,128)(2,1)S(1)}, bf16[64,896]{1,0:T(8,128)(2,1)S(1)}, u32[]{:S(2)}, u32[]{:S(2)}) %collective-permute-start.2) | collective-permute-done | bytes 114720 | tf_op jit(solution)/shard_map/ppermute | solution.py:32
  26.8 3.5 %collective-permute-done.3.refs_5_.r2 = bf16[64,896]{1,0:T(8,128)(2,1)S(1)} collective-permute-done((bf16[64,896]{1,0:T(8,128)(2,1)S(1)}, bf16[64,896]{1,0:T(8,128)(2,1)S(1)}, u32[]{:S(2)}, u32[]{:S(2)}) %collective-permute-start.3) | collective-permute-done | bytes 114720 | tf_op jit(solution)/shard_map/ppermute | solution.py:32
  30.7 3.0 %collective-permute-start.16 = (bf16[128,1536]{1,0:T(8,128)(2,1)S(1)}, bf16[128,1536]{1,0:T(8,128)(2,1)S(1)}, u32[]{:S(2)}, u32[]{:S(2)}) collective-permute-start(bf16[128,1536]{1,0:T(8,128)(2,1)S(1)} %copy-done.1), channel_id=1, source_target_pairs={{0,32},{16,48},{32,0},{48,16},{1,33},{17,49},{33,1},{49,17},{2,34}... | collective-permute-start | bytes 1179656 | tf_op jit(solution)/shard_map/ppermute | solution.py:32
  33.7 1.1 %collective-permute-start.17 = (bf16[128,1536]{1,0:T(8,128)(2,1)S(1)}, bf16[128,1536]{1,0:T(8,128)(2,1)S(1)}, u32[]{:S(2)}, u32[]{:S(2)}) collective-permute-start(bf16[128,1536]{1,0:T(8,128)(2,1)S(1)} %copy-done.1), channel_id=1, source_target_pairs={{0,16},{1,49},{16,32},{17,1},{32,48},{33,17},{48,0},{49,33},{2,18}... | collective-permute-start | bytes 1179656 | tf_op jit(solution)/shard_map/ppermute | solution.py:48
  34.8 0.1 assemble.1.w_ref
  35.0 0.3 latent_part.1
  35.3 1.8 %collective-permute-start.11 = (bf16[64,640]{1,0:T(8,128)(2,1)S(1)}, bf16[64,640]{1,0:T(8,128)(2,1)S(1)}, u32[]{:S(2)}, u32[]{:S(2)}) collective-permute-start(bf16[64,640]{1,0:T(8,128)(2,1)S(1)} %get-tuple-element.43.p0), channel_id=1, source_target_pairs={{0,6},{2,0},{4,2},{6,4},{1,7},{3,1},{5,3},{7,5},{8,14},{10,8},{12,... | collective-permute-start | bytes 245768 | tf_op jit(solution)/shard_map/ppermute | solution.py:32
  37.1 1.3 %collective-permute-start.10 = (bf16[64,640]{1,0:T(8,128)(2,1)S(1)}, bf16[64,640]{1,0:T(8,128)(2,1)S(1)}, u32[]{:S(2)}, u32[]{:S(2)}) collective-permute-start(bf16[64,640]{1,0:T(8,128)(2,1)S(1)} %get-tuple-element.43.p0), channel_id=1, source_target_pairs={{0,4},{2,6},{4,0},{6,2},{1,5},{3,7},{5,1},{7,3},{8,12},{10,14},{12... | collective-permute-start | bytes 245768 | tf_op jit(solution)/shard_map/ppermute | solution.py:32
  38.4 0.7 tables.1
  39.1 0.8 collective-permute-done.11.p3
  39.9 6.5 %collective-permute-done.10.p2 = bf16[64,640]{1,0:T(8,128)(2,1)S(1)} collective-permute-done((bf16[64,640]{1,0:T(8,128)(2,1)S(1)}, bf16[64,640]{1,0:T(8,128)(2,1)S(1)}, u32[]{:S(2)}, u32[]{:S(2)}) %collective-permute-start.10) | collective-permute-done | bytes 81952 | tf_op jit(solution)/shard_map/ppermute | solution.py:32
  46.4 0.3 kv_rows.1.refs_0_
  46.7 2.4 %collective-permute-start.15 = (bf16[64,640]{1,0:T(8,128)(2,1)S(1)}, bf16[64,640]{1,0:T(8,128)(2,1)S(1)}, u32[]{:S(2)}, u32[]{:S(2)}) collective-permute-start(bf16[64,640]{1,0:T(8,128)(2,1)S(1)} %kv_rows.1.refs_0_), channel_id=1, source_target_pairs={{0,12},{2,14},{4,8},{6,10},{8,4},{10,6},{12,0},{14,2},{1,13},{3,15... | collective-permute-start | bytes 245768 | tf_op jit(solution)/shard_map/ppermute | solution.py:71
  49.1 0.7 collective-permute-start.25
  49.8 0.6 collective-permute-start.12
  50.4 0.6 collective-permute-start.13
  51.0 2.9 %collective-permute-start.14 = (bf16[16,896]{1,0:T(8,128)(2,1)S(1)}, bf16[16,896]{1,0:T(8,128)(2,1)S(1)}, u32[]{:S(2)}, u32[]{:S(2)}) collective-permute-start(bf16[16,896]{1,0:T(8,128)(2,1)S(1)} %get-tuple-element.52), channel_id=1, source_target_pairs={{0,6},{2,0},{4,2},{6,4},{1,7},{3,1},{5,3},{7,5},{8,14},{10,8},{12,... | collective-permute-start | bytes 86024 | tf_op jit(solution)/shard_map/ppermute | solution.py:32
  53.9 1.6 %collective-permute-done.12.h1.refs_4_ = bf16[16,896]{1,0:T(8,128)(2,1)S(1)} collective-permute-done((bf16[16,896]{1,0:T(8,128)(2,1)S(1)}, bf16[16,896]{1,0:T(8,128)(2,1)S(1)}, u32[]{:S(2)}, u32[]{:S(2)}) %collective-permute-start.12) | collective-permute-done | bytes 28704 | tf_op jit(solution)/shard_map/ppermute | solution.py:32
  55.5 0.5 collective-permute-done.14.h3.refs_6_
  56.0 1.1 %collective-permute-start.20 = (bf16[128,640]{1,0:T(8,128)(2,1)S(1)}, bf16[128,640]{1,0:T(8,128)(2,1)S(1)}, u32[]{:S(2)}, u32[]{:S(2)}) collective-permute-start(bf16[128,640]{1,0:T(8,128)(2,1)S(1)} %pack.3.refs_0_), channel_id=1, source_target_pairs={{0,64},{64,128},{128,192},{192,0},{1,65},{65,129},{129,193},{193,1... | collective-permute-start | bytes 491528 | tf_op jit(solution)/shard_map/ppermute | solution.py:32
  57.1 2.1 %collective-permute-start.19 = (bf16[128,640]{1,0:T(8,128)(2,1)S(1)}, bf16[128,640]{1,0:T(8,128)(2,1)S(1)}, u32[]{:S(2)}, u32[]{:S(2)}) collective-permute-start(bf16[128,640]{1,0:T(8,128)(2,1)S(1)} %pack.3.refs_0_), channel_id=1, source_target_pairs={{0,128},{64,192},{128,0},{192,64},{1,129},{65,193},{129,1},{193,65... | collective-permute-start | bytes 491528 | tf_op jit(solution)/shard_map/ppermute | solution.py:32
  59.2 3.1 %collective-permute-done.20.refs_3_ = bf16[128,640]{1,0:T(8,128)(2,1)S(1)} collective-permute-done((bf16[128,640]{1,0:T(8,128)(2,1)S(1)}, bf16[128,640]{1,0:T(8,128)(2,1)S(1)}, u32[]{:S(2)}, u32[]{:S(2)}) %collective-permute-start.20) | collective-permute-done | bytes 163872 | tf_op jit(solution)/shard_map/ppermute | solution.py:32
  62.3 2.1 %collective-permute-done.19.refs_2_ = bf16[128,640]{1,0:T(8,128)(2,1)S(1)} collective-permute-done((bf16[128,640]{1,0:T(8,128)(2,1)S(1)}, bf16[128,640]{1,0:T(8,128)(2,1)S(1)}, u32[]{:S(2)}, u32[]{:S(2)}) %collective-permute-start.19) | collective-permute-done | bytes 163872 | tf_op jit(solution)/shard_map/ppermute | solution.py:32
  64.4 1.7 %collective-permute-done.18.refs_1_ = bf16[128,640]{1,0:T(8,128)(2,1)S(1)} collective-permute-done((bf16[128,640]{1,0:T(8,128)(2,1)S(1)}, bf16[128,640]{1,0:T(8,128)(2,1)S(1)}, u32[]{:S(2)}, u32[]{:S(2)}) %collective-permute-start.18) | collective-permute-done | bytes 163872 | tf_op jit(solution)/shard_map/ppermute | solution.py:32
  66.1 1.4 %collective-permute-done.22.refs_5_ = bf16[128,640]{1,0:T(8,128)(2,1)S(1)} collective-permute-done((bf16[128,640]{1,0:T(8,128)(2,1)S(1)}, bf16[128,640]{1,0:T(8,128)(2,1)S(1)}, u32[]{:S(2)}, u32[]{:S(2)}) %collective-permute-start.22) | collective-permute-done | bytes 163872 | tf_op jit(solution)/shard_map/ppermute | solution.py:36
  67.5 3.5 %lift.1 = (bf16[8,1024,256]{2,1,0:T(8,128)(2,1)S(1)}, bf16[8,1024,256]{2,1,0:T(8,128)(2,1)S(1)}) custom-call(s32[1]{0:T(128)} %bitcast.s, s32[64]{0:T(128)S(1)} %copy-done.4, bf16[128,640]{1,0:T(8,128)(2,1)S(1)} %pack.3.refs_0_, bf16[128,640]{1,0:T(8,128)(2,1)S(1)} %collective-permute-done.18.refs_1_, bf16[128,640]{1,0:T(8,128)(2,1)S(1)} %collective-permute-done.19.refs_2_, ...), custom_call_target="tpu_custom_call" | custom-call | tf_op jit(solution)/shard_map/lift/pallas_call | solution.py:280
  70.9 3.0 %attend.5 = bf16[128,1152]{1,0:T(8,128)(2,1)S(1)} custom-call(s32[1]{0:T(128)} %bitcast.s, s32[64]{0:T(128)S(1)} %copy-done.4, bf16[128,1536]{1,0:T(8,128)(2,1)S(1)} %collective-permute-done.16.refs_2_.refs_0_, bf16[8,1024,256]{2,1,0:T(8,128)(2,1)S(1)} %get-tuple-element.63.refs_1_.refs_2_, bf16[8,1024,256]{2,1,0:T(8,128)(2,1)S(1)} %get-tuple-element.64.refs_2_.refs_3_), custom_call_target="tpu_custom_call" | custom-call | tf_op jit(solution)/shard_map/attend/pallas_call | solution.py:360
  73.9 1.3 %collective-permute-start.27 = (bf16[128,1152]{1,0:T(8,128)(2,1)S(1)}, bf16[128,1152]{1,0:T(8,128)(2,1)S(1)}, u32[]{:S(2)}, u32[]{:S(2)}) collective-permute-start(bf16[128,1152]{1,0:T(8,128)(2,1)S(1)} %attend.5), channel_id=1, source_target_pairs={{0,16},{1,49},{16,32},{17,1},{32,48},{33,17},{48,0},{49,33},{2,18}... | collective-permute-start | bytes 884744 | tf_op jit(solution)/shard_map/ppermute | solution.py:48
  75.2 3.6 %attend.4 = (bf16[128,1152]{1,0:T(8,128)(2,1)S(1)}, bf16[128,1152]{1,0:T(8,128)(2,1)S(1)}) custom-call(s32[1]{0:T(128)} %bitcast.s, s32[64]{0:T(128)S(1)} %copy-done.4, bf16[128,1536]{1,0:T(8,128)(2,1)S(1)} %collective-permute-done.17.refs_3_.refs_0_, bf16[128,1536]{1,0:T(8,128)(2,1)S(1)} %collective-permute-done.25.refs_1_, ...), custom_call_target="tpu_custom_call" | custom-call | tf_op jit(solution)/shard_map/attend/pallas_call | solution.py:360
  78.9 2.3 %collective-permute-start.26 = (bf16[128,1152]{1,0:T(8,128)(2,1)S(1)}, bf16[128,1152]{1,0:T(8,128)(2,1)S(1)}, u32[]{:S(2)}, u32[]{:S(2)}) collective-permute-start(bf16[128,1152]{1,0:T(8,128)(2,1)S(1)} %get-tuple-element.66), channel_id=1, source_target_pairs={{0,48},{1,17},{16,0},{17,33},{32,16},{33,49},{48,32},{49,1},{2,50}... | collective-permute-start | bytes 884744 | tf_op jit(solution)/shard_map/ppermute | solution.py:48
  81.2 1.0 %collective-permute-done.27.got_ref = bf16[128,1152]{1,0:T(8,128)(2,1)S(1)} collective-permute-done((bf16[128,1152]{1,0:T(8,128)(2,1)S(1)}, bf16[128,1152]{1,0:T(8,128)(2,1)S(1)}, u32[]{:S(2)}, u32[]{:S(2)}) %collective-permute-start.27) | collective-permute-done | bytes 294944 | tf_op jit(solution)/shard_map/ppermute | solution.py:48
  82.1 0.5 relay.1
  82.7 0.7 hidden_rows.1
  83.4 3.0 %attend.3.a_ref = bf16[128,1152]{1,0:T(8,128)(2,1)S(1)} custom-call(s32[1]{0:T(128)} %bitcast.s, s32[64]{0:T(128)S(1)} %copy-done.4, bf16[128,1536]{1,0:T(8,128)(2,1)S(1)} %copy-done.1, bf16[8,1024,256]{2,1,0:T(8,128)(2,1)S(1)} %get-tuple-element.63.refs_1_.refs_2_, bf16[8,1024,256]{2,1,0:T(8,128)(2,1)S(1)} %get-tuple-element.64.refs_2_.refs_3_), custom_call_target="tpu_custom_call" | custom-call | tf_op jit(solution)/shard_map/attend/pallas_call | solution.py:360
  86.4 0.8 collective-permute-done.26.b_ref
  87.1 4.0 %collective-permute-done.28.c_ref = bf16[128,1152]{1,0:T(8,128)(2,1)S(1)} collective-permute-done((bf16[128,1152]{1,0:T(8,128)(2,1)S(1)}, bf16[128,1152]{1,0:T(8,128)(2,1)S(1)}, u32[]{:S(2)}, u32[]{:S(2)}) %collective-permute-start.28) | collective-permute-done | bytes 294944 | tf_op jit(solution)/shard_map/ppermute | solution.py:48
  91.1 1.4 %merge.1 = bf16[128,1024]{1,0:T(8,128)(2,1)} custom-call(bf16[128,1152]{1,0:T(8,128)(2,1)S(1)} %attend.3.a_ref, bf16[128,1152]{1,0:T(8,128)(2,1)S(1)} %collective-permute-done.26.b_ref, bf16[128,1152]{1,0:T(8,128)(2,1)S(1)} %collective-permute-done.28.c_ref), custom_call_target="tpu_custom_call" | custom-call | tf_op jit(solution)/shard_map/merge/pallas_call | solution.py:397
  (41 shorter events, 0.8 us)
Async XLA Ops:
  0.6 13.8 %collective-permute-start = (bf16[112,576]{1,0:T(8,128)(2,1)}, bf16[112,576]{1,0:T(8,128)(2,1)S(1)}, u32[]{:S(2)}, u32[]{:S(2)}) collective-permute-start(bf16[112,576]{1,0:T(8,128)(2,1)} %param.19), channel_id=1, source_target_pairs={{2,0},{14,1},{67,2},{79,3},{132,4},{136,5},{197,6},{201,7},{6,8},{... | collective-permute-start | bytes 387080 | tf_op jit(solution)/shard_map/ppermute | solution.py:66
  7.7 0.9 %copy-start.2 = (bf16[128,1024]{1,0:T(8,128)(2,1)S(1)}, bf16[128,1024]{1,0:T(8,128)(2,1)}, u32[]{:S(2)}) copy-start(bf16[128,1024]{1,0:T(8,128)(2,1)} %param.12) | copy-start | bytes 786436
  8.6 0.9 copy-start.3
  9.5 21.1 %copy-start.1 = (bf16[128,1536]{1,0:T(8,128)(2,1)S(1)}, bf16[128,1536]{1,0:T(8,128)(2,1)}, u32[]{:S(2)}) copy-start(bf16[128,1536]{1,0:T(8,128)(2,1)} %refs_0_.1) | copy-start | bytes 1179652
  9.5 25.3 %copy-start.5 = (bf16[3584]{0:T(1024)(128)(2,1)S(1)}, bf16[3584]{0:T(1024)(128)(2,1)}, u32[]{:S(2)}) copy-start(bf16[3584]{0:T(1024)(128)(2,1)} %param.18) | copy-start | bytes 21508
  14.4 24.0 %copy-start.6 = (bf16[512]{0:T(512)(128)(2,1)S(1)}, bf16[512]{0:T(512)(128)(2,1)}, u32[]{:S(2)}) copy-start(bf16[512]{0:T(512)(128)(2,1)} %param.20) | copy-start | bytes 3076
  14.4 24.0 %copy-start.4 = (s32[64]{0:T(128)S(1)}, s32[64]{0:T(128)}, u32[]{:S(2)}) copy-start(s32[64]{0:T(128)} %seg.8) | copy-start | bytes 772
  14.4 4.3 %collective-permute-start.1 = (bf16[4,64,896]{2,1,0:T(8,128)(2,1)S(1)}, bf16[4,64,896]{2,1,0:T(8,128)(2,1)S(1)}, u32[]{:S(2)}, u32[]{:S(2)}) collective-permute-start(bf16[4,64,896]{2,1,0:T(8,128)(2,1)S(1)} %get-tuple-element.37), channel_id=1, source_target_pairs={{0,1},{1,0},{2,3},{3,2},{4,5},{5,4},{6,7},{7,6},{8,9},{9,8},{10,11... | collective-permute-start | bytes 1376264 | tf_op jit(solution)/shard_map/ppermute | solution.py:36
  14.5 9.9 %collective-permute-start.7 = (bf16[1,112,576]{2,1,0:T(8,128)(2,1)S(1)}, bf16[1,112,576]{2,1,0:T(8,128)(2,1)S(1)}, u32[]{:S(2)}, u32[]{:S(2)}) collective-permute-start(bf16[1,112,576]{2,1,0:T(8,128)(2,1)S(1)} %bitcast.4), channel_id=1, source_target_pairs={{0,48},{16,32},{32,16},{48,0},{1,49},{17,33},{33,17},{49,1},{2,50}... | collective-permute-start | bytes 387080 | tf_op jit(solution)/shard_map/ppermute | solution.py:36
  17.4 8.2 %collective-permute-start.6 = (bf16[1,112,576]{2,1,0:T(8,128)(2,1)S(1)}, bf16[1,112,576]{2,1,0:T(8,128)(2,1)S(1)}, u32[]{:S(2)}, u32[]{:S(2)}) collective-permute-start(bf16[1,112,576]{2,1,0:T(8,128)(2,1)S(1)} %bitcast.5), channel_id=1, source_target_pairs={{0,32},{16,48},{32,0},{48,16},{1,33},{17,49},{33,1},{49,17},{2,34}... | collective-permute-start | bytes 387080 | tf_op jit(solution)/shard_map/ppermute | solution.py:36
  18.2 7.4 %collective-permute-start.5 = (bf16[1,112,576]{2,1,0:T(8,128)(2,1)S(1)}, bf16[1,112,576]{2,1,0:T(8,128)(2,1)S(1)}, u32[]{:S(2)}, u32[]{:S(2)}) collective-permute-start(bf16[1,112,576]{2,1,0:T(8,128)(2,1)S(1)} %bitcast.6), channel_id=1, source_target_pairs={{0,16},{16,0},{32,48},{48,32},{1,17},{17,1},{33,49},{49,33},{2,18}... | collective-permute-start | bytes 387080 | tf_op jit(solution)/shard_map/ppermute | solution.py:36
  18.8 48.7 %copy-start = (bf16[512,2048]{1,0:T(8,128)(2,1)S(1)}, bf16[512,2048]{1,0:T(8,128)(2,1)}, u32[]{:S(2)}) copy-start(bf16[512,2048]{1,0:T(8,128)(2,1)} %refs_8_.1) | copy-start | bytes 6291460
  18.8 8.0 %collective-permute-start.2 = (bf16[64,896]{1,0:T(8,128)(2,1)S(1)}, bf16[64,896]{1,0:T(8,128)(2,1)S(1)}, u32[]{:S(2)}, u32[]{:S(2)}) collective-permute-start(bf16[64,896]{1,0:T(8,128)(2,1)S(1)} %get-tuple-element.38), channel_id=1, source_target_pairs={{0,2},{2,4},{4,6},{6,0},{1,3},{3,5},{5,7},{7,1},{8,10},{10,12},{12... | collective-permute-start | bytes 344072 | tf_op jit(solution)/shard_map/ppermute | solution.py:32
  18.9 11.5 %collective-permute-start.3 = (bf16[64,896]{1,0:T(8,128)(2,1)S(1)}, bf16[64,896]{1,0:T(8,128)(2,1)S(1)}, u32[]{:S(2)}, u32[]{:S(2)}) collective-permute-start(bf16[64,896]{1,0:T(8,128)(2,1)S(1)} %get-tuple-element.39), channel_id=1, source_target_pairs={{0,4},{2,6},{4,0},{6,2},{1,5},{3,7},{5,1},{7,3},{8,12},{10,14},{12... | collective-permute-start | bytes 344072 | tf_op jit(solution)/shard_map/ppermute | solution.py:32
  24.4 6.1 %collective-permute-start.4 = (bf16[64,896]{1,0:T(8,128)(2,1)S(1)}, bf16[64,896]{1,0:T(8,128)(2,1)S(1)}, u32[]{:S(2)}, u32[]{:S(2)}) collective-permute-start(bf16[64,896]{1,0:T(8,128)(2,1)S(1)} %get-tuple-element.40), channel_id=1, source_target_pairs={{0,6},{2,0},{4,2},{6,4},{1,7},{3,1},{5,3},{7,5},{8,14},{10,8},{12,... | collective-permute-start | bytes 344072 | tf_op jit(solution)/shard_map/ppermute | solution.py:32
  30.5 4.3 %collective-permute-start.8 = (bf16[4,112,576]{2,1,0:T(8,128)(2,1)S(1)}, bf16[4,112,576]{2,1,0:T(8,128)(2,1)S(1)}, u32[]{:S(2)}, u32[]{:S(2)}) collective-permute-start(bf16[4,112,576]{2,1,0:T(8,128)(2,1)S(1)} %pack.2.own_ref), channel_id=1, source_target_pairs={{0,1},{1,0},{2,3},{3,2},{4,5},{5,4},{6,7},{7,6},{8,9},{9,8},{10,11... | collective-permute-start | bytes 1548296 | tf_op jit(solution)/shard_map/ppermute | solution.py:36
  30.7 18.4 %collective-permute-start.16 = (bf16[128,1536]{1,0:T(8,128)(2,1)S(1)}, bf16[128,1536]{1,0:T(8,128)(2,1)S(1)}, u32[]{:S(2)}, u32[]{:S(2)}) collective-permute-start(bf16[128,1536]{1,0:T(8,128)(2,1)S(1)} %copy-done.1), channel_id=1, source_target_pairs={{0,32},{16,48},{32,0},{48,16},{1,33},{17,49},{33,1},{49,17},{2,34}... | collective-permute-start | bytes 1179656 | tf_op jit(solution)/shard_map/ppermute | solution.py:32
  33.7 17.3 %collective-permute-start.17 = (bf16[128,1536]{1,0:T(8,128)(2,1)S(1)}, bf16[128,1536]{1,0:T(8,128)(2,1)S(1)}, u32[]{:S(2)}, u32[]{:S(2)}) collective-permute-start(bf16[128,1536]{1,0:T(8,128)(2,1)S(1)} %copy-done.1), channel_id=1, source_target_pairs={{0,16},{1,49},{16,32},{17,1},{32,48},{33,17},{48,0},{49,33},{2,18}... | collective-permute-start | bytes 1179656 | tf_op jit(solution)/shard_map/ppermute | solution.py:48
  35.3 4.6 %collective-permute-start.11 = (bf16[64,640]{1,0:T(8,128)(2,1)S(1)}, bf16[64,640]{1,0:T(8,128)(2,1)S(1)}, u32[]{:S(2)}, u32[]{:S(2)}) collective-permute-start(bf16[64,640]{1,0:T(8,128)(2,1)S(1)} %get-tuple-element.43.p0), channel_id=1, source_target_pairs={{0,6},{2,0},{4,2},{6,4},{1,7},{3,1},{5,3},{7,5},{8,14},{10,8},{12,... | collective-permute-start | bytes 245768 | tf_op jit(solution)/shard_map/ppermute | solution.py:32
  37.1 9.3 %collective-permute-start.10 = (bf16[64,640]{1,0:T(8,128)(2,1)S(1)}, bf16[64,640]{1,0:T(8,128)(2,1)S(1)}, u32[]{:S(2)}, u32[]{:S(2)}) collective-permute-start(bf16[64,640]{1,0:T(8,128)(2,1)S(1)} %get-tuple-element.43.p0), channel_id=1, source_target_pairs={{0,4},{2,6},{4,0},{6,2},{1,5},{3,7},{5,1},{7,3},{8,12},{10,14},{12... | collective-permute-start | bytes 245768 | tf_op jit(solution)/shard_map/ppermute | solution.py:32
  38.4 8.0 %collective-permute-start.9 = (bf16[64,640]{1,0:T(8,128)(2,1)S(1)}, bf16[64,640]{1,0:T(8,128)(2,1)S(1)}, u32[]{:S(2)}, u32[]{:S(2)}) collective-permute-start(bf16[64,640]{1,0:T(8,128)(2,1)S(1)} %get-tuple-element.43.p0), channel_id=1, source_target_pairs={{0,2},{2,4},{4,6},{6,0},{1,3},{3,5},{5,7},{7,1},{8,10},{10,12},{12... | collective-permute-start | bytes 245768 | tf_op jit(solution)/shard_map/ppermute | solution.py:32
  46.7 9.3 %collective-permute-start.15 = (bf16[64,640]{1,0:T(8,128)(2,1)S(1)}, bf16[64,640]{1,0:T(8,128)(2,1)S(1)}, u32[]{:S(2)}, u32[]{:S(2)}) collective-permute-start(bf16[64,640]{1,0:T(8,128)(2,1)S(1)} %kv_rows.1.refs_0_), channel_id=1, source_target_pairs={{0,12},{2,14},{4,8},{6,10},{8,4},{10,6},{12,0},{14,2},{1,13},{3,15... | collective-permute-start | bytes 245768 | tf_op jit(solution)/shard_map/ppermute | solution.py:71
  49.1 17.0 %collective-permute-start.25 = (bf16[128,1536]{1,0:T(8,128)(2,1)S(1)}, bf16[128,1536]{1,0:T(8,128)(2,1)S(1)}, u32[]{:S(2)}, u32[]{:S(2)}) collective-permute-start(bf16[128,1536]{1,0:T(8,128)(2,1)S(1)} %copy-done.1), channel_id=1, source_target_pairs={{0,48},{1,17},{16,0},{17,33},{32,16},{33,49},{48,32},{49,1},{2,50}... | collective-permute-start | bytes 1179656 | tf_op jit(solution)/shard_map/ppermute | solution.py:48
  49.8 5.8 %collective-permute-start.12 = (bf16[16,896]{1,0:T(8,128)(2,1)S(1)}, bf16[16,896]{1,0:T(8,128)(2,1)S(1)}, u32[]{:S(2)}, u32[]{:S(2)}) collective-permute-start(bf16[16,896]{1,0:T(8,128)(2,1)S(1)} %get-tuple-element.50), channel_id=1, source_target_pairs={{0,2},{2,4},{4,6},{6,0},{1,3},{3,5},{5,7},{7,1},{8,10},{10,12},{12... | collective-permute-start | bytes 86024 | tf_op jit(solution)/shard_map/ppermute | solution.py:32
  50.4 5.2 %collective-permute-start.13 = (bf16[16,896]{1,0:T(8,128)(2,1)S(1)}, bf16[16,896]{1,0:T(8,128)(2,1)S(1)}, u32[]{:S(2)}, u32[]{:S(2)}) collective-permute-start(bf16[16,896]{1,0:T(8,128)(2,1)S(1)} %get-tuple-element.51), channel_id=1, source_target_pairs={{0,4},{2,6},{4,0},{6,2},{1,5},{3,7},{5,1},{7,3},{8,12},{10,14},{12... | collective-permute-start | bytes 86024 | tf_op jit(solution)/shard_map/ppermute | solution.py:32
  51.0 5.0 %collective-permute-start.14 = (bf16[16,896]{1,0:T(8,128)(2,1)S(1)}, bf16[16,896]{1,0:T(8,128)(2,1)S(1)}, u32[]{:S(2)}, u32[]{:S(2)}) collective-permute-start(bf16[16,896]{1,0:T(8,128)(2,1)S(1)} %get-tuple-element.52), channel_id=1, source_target_pairs={{0,6},{2,0},{4,2},{6,4},{1,7},{3,1},{5,3},{7,5},{8,14},{10,8},{12,... | collective-permute-start | bytes 86024 | tf_op jit(solution)/shard_map/ppermute | solution.py:32
  56.0 6.3 %collective-permute-start.20 = (bf16[128,640]{1,0:T(8,128)(2,1)S(1)}, bf16[128,640]{1,0:T(8,128)(2,1)S(1)}, u32[]{:S(2)}, u32[]{:S(2)}) collective-permute-start(bf16[128,640]{1,0:T(8,128)(2,1)S(1)} %pack.3.refs_0_), channel_id=1, source_target_pairs={{0,64},{64,128},{128,192},{192,0},{1,65},{65,129},{129,193},{193,1... | collective-permute-start | bytes 491528 | tf_op jit(solution)/shard_map/ppermute | solution.py:32
  57.1 7.2 %collective-permute-start.19 = (bf16[128,640]{1,0:T(8,128)(2,1)S(1)}, bf16[128,640]{1,0:T(8,128)(2,1)S(1)}, u32[]{:S(2)}, u32[]{:S(2)}) collective-permute-start(bf16[128,640]{1,0:T(8,128)(2,1)S(1)} %pack.3.refs_0_), channel_id=1, source_target_pairs={{0,128},{64,192},{128,0},{192,64},{1,129},{65,193},{129,1},{193,65... | collective-permute-start | bytes 491528 | tf_op jit(solution)/shard_map/ppermute | solution.py:32
  59.2 6.8 %collective-permute-start.18 = (bf16[128,640]{1,0:T(8,128)(2,1)S(1)}, bf16[128,640]{1,0:T(8,128)(2,1)S(1)}, u32[]{:S(2)}, u32[]{:S(2)}) collective-permute-start(bf16[128,640]{1,0:T(8,128)(2,1)S(1)} %pack.3.refs_0_), channel_id=1, source_target_pairs={{0,192},{64,0},{128,64},{192,128},{1,193},{65,1},{129,65},{193,129... | collective-permute-start | bytes 491528 | tf_op jit(solution)/shard_map/ppermute | solution.py:32
  59.2 6.8 %collective-permute-start.21 = (bf16[128,640]{1,0:T(8,128)(2,1)S(1)}, bf16[128,640]{1,0:T(8,128)(2,1)S(1)}, u32[]{:S(2)}, u32[]{:S(2)}) collective-permute-start(bf16[128,640]{1,0:T(8,128)(2,1)S(1)} %pack.3.refs_0_), channel_id=1, source_target_pairs={{0,1},{1,0},{2,3},{3,2},{4,5},{5,4},{6,7},{7,6},{8,9},{9,8},{10,11... | collective-permute-start | bytes 491528 | tf_op jit(solution)/shard_map/ppermute | solution.py:36
  62.3 3.8 %collective-permute-start.24 = (bf16[128,640]{1,0:T(8,128)(2,1)S(1)}, bf16[128,640]{1,0:T(8,128)(2,1)S(1)}, u32[]{:S(2)}, u32[]{:S(2)}) collective-permute-start(bf16[128,640]{1,0:T(8,128)(2,1)S(1)} %collective-permute-done.20.refs_3_), channel_id=1, source_target_pairs={{0,1},{1,0},{2,3},{3,2},{4,5},{5,4},{6,7},{7,6},{8,9},{9,8},{10,11... | collective-permute-start | bytes 491528 | tf_op jit(solution)/shard_map/ppermute | solution.py:36
  64.4 1.7 %collective-permute-start.23 = (bf16[128,640]{1,0:T(8,128)(2,1)S(1)}, bf16[128,640]{1,0:T(8,128)(2,1)S(1)}, u32[]{:S(2)}, u32[]{:S(2)}) collective-permute-start(bf16[128,640]{1,0:T(8,128)(2,1)S(1)} %collective-permute-done.19.refs_2_), channel_id=1, source_target_pairs={{0,1},{1,0},{2,3},{3,2},{4,5},{5,4},{6,7},{7,6},{8,9},{9,8},{10,11... | collective-permute-start | bytes 491528 | tf_op jit(solution)/shard_map/ppermute | solution.py:36
  66.1 1.4 %collective-permute-start.22 = (bf16[128,640]{1,0:T(8,128)(2,1)S(1)}, bf16[128,640]{1,0:T(8,128)(2,1)S(1)}, u32[]{:S(2)}, u32[]{:S(2)}) collective-permute-start(bf16[128,640]{1,0:T(8,128)(2,1)S(1)} %collective-permute-done.18.refs_1_), channel_id=1, source_target_pairs={{0,1},{1,0},{2,3},{3,2},{4,5},{5,4},{6,7},{7,6},{8,9},{9,8},{10,11... | collective-permute-start | bytes 491528 | tf_op jit(solution)/shard_map/ppermute | solution.py:36
  73.9 8.2 %collective-permute-start.27 = (bf16[128,1152]{1,0:T(8,128)(2,1)S(1)}, bf16[128,1152]{1,0:T(8,128)(2,1)S(1)}, u32[]{:S(2)}, u32[]{:S(2)}) collective-permute-start(bf16[128,1152]{1,0:T(8,128)(2,1)S(1)} %attend.5), channel_id=1, source_target_pairs={{0,16},{1,49},{16,32},{17,1},{32,48},{33,17},{48,0},{49,33},{2,18}... | collective-permute-start | bytes 884744 | tf_op jit(solution)/shard_map/ppermute | solution.py:48
  78.9 8.2 %collective-permute-start.26 = (bf16[128,1152]{1,0:T(8,128)(2,1)S(1)}, bf16[128,1152]{1,0:T(8,128)(2,1)S(1)}, u32[]{:S(2)}, u32[]{:S(2)}) collective-permute-start(bf16[128,1152]{1,0:T(8,128)(2,1)S(1)} %get-tuple-element.66), channel_id=1, source_target_pairs={{0,48},{1,17},{16,0},{17,33},{32,16},{33,49},{48,32},{49,1},{2,50}... | collective-permute-start | bytes 884744 | tf_op jit(solution)/shard_map/ppermute | solution.py:48
  82.6 8.5 %collective-permute-start.28 = (bf16[128,1152]{1,0:T(8,128)(2,1)S(1)}, bf16[128,1152]{1,0:T(8,128)(2,1)S(1)}, u32[]{:S(2)}, u32[]{:S(2)}) collective-permute-start(bf16[128,1152]{1,0:T(8,128)(2,1)S(1)} %relay.1), channel_id=1, source_target_pairs={{0,16},{1,49},{16,32},{17,1},{32,48},{33,17},{48,0},{49,33},{2,18}... | collective-permute-start | bytes 884744 | tf_op jit(solution)/shard_map/ppermute | solution.py:48

commit v4 on v3

--- a/solution.py
+++ b/solution.py
@@ -389,23 +389,17 @@
     return local(relay_kernel, shape((128, MESSAGE)), 16, "relay", vmem=2)(got, own)
 
 
-def merge_kernel(a_ref, b_ref, c_ref, out_ref):
-    out_ref[...] = merged((a_ref, b_ref, c_ref))
-
-
-def merge(a, b, c):
-    return local(merge_kernel, shape((128, HEADS * VDIM)), 16, "merge", vmem=3)(a, b, c)
-
-
-def hidden_kernel(s, h0, h1, h2, h3, out_ref):
+def final_kernel(s, a_ref, b_ref, c_ref, h0, h1, h2, h3, hidden_ref, attn_ref):
     y, _, _, zl, _ = coords(s)
     for k, ref in enumerate((h0, h1, h2, h3)):
         column = pl.multiple_of((y ^ ((zl + 4 - k) % 4)) * COLS, 128)
-        out_ref[:, pl.ds(column, COLS)] = ref[...]
-
-
-def hidden_rows(scalars, blocks):
-    return local(hidden_kernel, shape((16, 4 * COLS)), 16, "hidden_rows", 1, 4)(scalars, *blocks)
+        hidden_ref[:, pl.ds(column, COLS)] = ref[...]
+    attn_ref[...] = merged((a_ref, b_ref, c_ref))
+
+
+def final(scalars, *operands):
+    outs = [shape((16, 4 * COLS)), shape((128, HEADS * VDIM))]
+    return local(final_kernel, outs, 16, "final", 1, 7)(scalars, *operands)
 
 
 def body(
@@ -451,11 +445,11 @@
     rows, h1, h2, h3 = tie(rows, h1, h2, h3)
     beside = cross(rows)
     pieces = [h0] + [shift(h, "zl", k) for k, h in ((1, h1), (2, h2), (3, h3))]
-    both = pack([rows, beside], (q_far, q_back, *pieces[1:]))
+    both = pack([rows, beside], (q_far,))
     column = [both] + [shift(both, "y", -k) for k in (1, 2, 3)]
     keys = column + [swap(value, "core") for value in column]
 
-    *keys, q_away = tie(*keys, q_away)
+    *keys, q_back, q_away = tie(*keys, q_back, q_away)
     lifted = lift(scalars, segment_ordering, keys, latent_up_weight)
     (relayed,) = attend((far,), scalars, segment_ordering, [q_far], lifted)
     got = turn(relayed, 1)
@@ -463,8 +457,7 @@
     direct = turn(direct, -1)
     passed = turn(relay(got, mine), 1)
     (own,) = attend((near,), scalars, segment_ordering, [queries], lifted)
-    hidden = hidden_rows(scalars, pieces)
-    return hidden, merge(own, direct, passed)
+    return tuple(final(scalars, own, direct, passed, *pieces))
 
 
 def solution(mesh):

time: 93.3 us -> 92 us (0.986)
  starting transfers between devices: 35.6 us -> 37.8 us
  waiting for transfers between devices: 32.1 us -> 30 us
    ppermute x5, waiting for transfers between devices: 5.69 us -> 1.14 us  [turn(): return lax.ppermute(value, ('x', 'core'), perm)]
    ppermute x1, waiting for transfers between devices: 0.01 us -> 3.56 us  [cross(): return lax.ppermute(value, ('zh', 'zl'), perm)]
    ppermute x13, starting transfers between devices: 16.3 us -> 18.4 us  [shift(): return lax.ppermute(value, axis, [(i, (i + k) % 4) for i in range(4)])]
    ppermute x13, waiting for transfers between devices: 21.1 us -> 19.9 us  [shift(): return lax.ppermute(value, axis, [(i, (i + k) % 4) for i in range(4)])]
    pallas_call x2 -> x1, Pallas kernels: 2.04 us -> 1.37 us  [final(): return local(final_kernel, outs, 16, 'final', 1, 7)(scalars, *operands)]
  transfers between devices with their start and end apart: 29 -> 29, of which waited for: 17 -> 14; matrix products, arithmetic and copies ran while one was open for 0% -> 0% of each run, Pallas kernels for 15% -> 15%
where the time goes in v4:
time: 92 us; the launch traced here: 91.8 us
  starting transfers between devices  37.8 us (41%)
  waiting for transfers between devices  30 us (33%)
  Pallas kernels  21.3 us (23%)
  local copies, waits for them, and re-layouts  1.89 us (2%)
    ppermute x13, waiting for transfers between devices, shift(): return lax.ppermute(value, axis, [(i, (i + k) % 4) for i in range(4)])  19.9 us
    ppermute x13, starting transfers between devices, shift(): return lax.ppermute(value, axis, [(i, (i + k) % 4) for i in range(4)])  18.4 us
    pallas_call x3, Pallas kernels, attend(): local(kernel, outs, 32, 'attend', 2, len(chunks) + 2)  9.55 us
    ppermute x1, starting transfers between devices, near_block(): return lax.ppermute(value, AXES, perm)  7.06 us
    ppermute x5, starting transfers between devices, turn(): return lax.ppermute(value, ('x', 'core'), perm)  5.51 us
    ppermute x9, waiting for transfers between devices, swap(): return lax.ppermute(value, axis, [(i, i ^ bit) for i in range(size)])  5.37 us
    pallas_call x1, Pallas kernels, project(): pl.pallas_call(project_kernel, in_specs=[pl.BlockSpec(memory_space=pltpu....  4.83 us
    ppermute x9, starting transfers between devices, swap(): return lax.ppermute(value, axis, [(i, i ^ bit) for i in range(size)])  4.38 us
  transfers between devices with their start and end apart: 29, of which 14 were waited for; matrix products, arithmetic and copies ran while one was open for 0% of the time, Pallas kernels for 15%

profile of v4, /device:TPU:24, one launch (start us, length us, event | category | flops | bytes accessed | tf_op | source)
XLA Modules:
  0.0 91.8 jit_solution(16062691001237585866)
XLA Ops:
  0.6 7.1 %collective-permute-start = (bf16[112,576]{1,0:T(8,128)(2,1)}, bf16[112,576]{1,0:T(8,128)(2,1)S(1)}, u32[]{:S(2)}, u32[]{:S(2)}) collective-permute-start(bf16[112,576]{1,0:T(8,128)(2,1)} %param.19), channel_id=1, source_target_pairs={{2,0},{14,1},{67,2},{79,3},{132,4},{136,5},{197,6},{201,7},{6,8},{... | collective-permute-start | bytes 387080 | tf_op jit(solution)/shard_map/ppermute | solution.py:66
  7.7 0.9 %copy-done.2 = bf16[128,1024]{1,0:T(8,128)(2,1)S(1)} copy-done((bf16[128,1024]{1,0:T(8,128)(2,1)S(1)}, bf16[128,1024]{1,0:T(8,128)(2,1)}, u32[]{:S(2)}) %copy-start.2) | copy-done | bytes 262168
  8.6 0.9 copy-done.3
  9.5 4.8 %project.1 = (bf16[4,64,896]{2,1,0:T(8,128)(2,1)S(1)}, bf16[4,64,896]{2,1,0:T(8,128)(2,1)S(1)}) custom-call(s32[1]{0:T(128)} %bitcast.s, bf16[4,2,16,1024]{3,2,1,0:T(8,128)(2,1)S(1)} %bitcast.3, bf16[1024,256]{1,0:T(8,128)(2,1)} %ad_hbm.1, bf16[1024,3584]{1,0:T(8,128)(2,1)} %w_hbm.1, bf16[256,3584]{1,0:T(8,128)(2,1)} %au_hbm.1, bf16[16,3584]{1,0:T(8,128)(2,1)S(1)} %copy-done.3), custom_call_target="tpu_custom_call" | custom-call | tf_op jit(solution)/shard_map/project/pallas_call | solution.py:123
  14.4 0.1 collective-permute-start.1
  14.5 2.8 %collective-permute-start.7 = (bf16[1,112,576]{2,1,0:T(8,128)(2,1)S(1)}, bf16[1,112,576]{2,1,0:T(8,128)(2,1)S(1)}, u32[]{:S(2)}, u32[]{:S(2)}) collective-permute-start(bf16[1,112,576]{2,1,0:T(8,128)(2,1)S(1)} %bitcast.4), channel_id=1, source_target_pairs={{0,48},{16,32},{32,16},{48,0},{1,49},{17,33},{33,17},{49,1},{2,50}... | collective-permute-start | bytes 387080 | tf_op jit(solution)/shard_map/ppermute | solution.py:36
  17.4 0.8 collective-permute-start.6
  18.2 0.5 collective-permute-start.5
  18.9 2.0 %collective-permute-start.3 = (bf16[64,896]{1,0:T(8,128)(2,1)S(1)}, bf16[64,896]{1,0:T(8,128)(2,1)S(1)}, u32[]{:S(2)}, u32[]{:S(2)}) collective-permute-start(bf16[64,896]{1,0:T(8,128)(2,1)S(1)} %get-tuple-element.40), channel_id=1, source_target_pairs={{0,4},{2,6},{4,0},{6,2},{1,5},{3,7},{5,1},{7,3},{8,12},{10,14},{12... | collective-permute-start | bytes 344072 | tf_op jit(solution)/shard_map/ppermute | solution.py:32
  20.9 3.6 %collective-permute-done.7.refs_3_ = bf16[1,112,576]{2,1,0:T(8,128)(2,1)S(1)} collective-permute-done((bf16[1,112,576]{2,1,0:T(8,128)(2,1)S(1)}, bf16[1,112,576]{2,1,0:T(8,128)(2,1)S(1)}, u32[]{:S(2)}, u32[]{:S(2)}) %collective-permute-start.7) | collective-permute-done | bytes 129056 | tf_op jit(solution)/shard_map/ppermute | solution.py:36
  24.5 0.8 collective-permute-start.4
  25.2 0.3 collective-permute-done.6.refs_2_
  25.5 0.1 collective-permute-done.5.refs_1_
  25.6 1.2 %collective-permute-done.2.refs_4_.r1 = bf16[64,896]{1,0:T(8,128)(2,1)S(1)} collective-permute-done((bf16[64,896]{1,0:T(8,128)(2,1)S(1)}, bf16[64,896]{1,0:T(8,128)(2,1)S(1)}, u32[]{:S(2)}, u32[]{:S(2)}) %collective-permute-start.2) | collective-permute-done | bytes 114720 | tf_op jit(solution)/shard_map/ppermute | solution.py:32
  26.8 3.5 %collective-permute-done.3.refs_5_.r2 = bf16[64,896]{1,0:T(8,128)(2,1)S(1)} collective-permute-done((bf16[64,896]{1,0:T(8,128)(2,1)S(1)}, bf16[64,896]{1,0:T(8,128)(2,1)S(1)}, u32[]{:S(2)}, u32[]{:S(2)}) %collective-permute-start.3) | collective-permute-done | bytes 114720 | tf_op jit(solution)/shard_map/ppermute | solution.py:32
  30.4 0.1 collective-permute-done.4.refs_6_.r3
  30.6 0.1 collective-permute-start.8
  30.7 3.0 %collective-permute-start.13 = (bf16[128,1536]{1,0:T(8,128)(2,1)S(1)}, bf16[128,1536]{1,0:T(8,128)(2,1)S(1)}, u32[]{:S(2)}, u32[]{:S(2)}) collective-permute-start(bf16[128,1536]{1,0:T(8,128)(2,1)S(1)} %copy-done.1), channel_id=1, source_target_pairs={{0,32},{16,48},{32,0},{48,16},{1,33},{17,49},{33,1},{49,17},{2,34}... | collective-permute-start | bytes 1179656 | tf_op jit(solution)/shard_map/ppermute | solution.py:32
  33.7 1.1 %collective-permute-start.21 = (bf16[128,1536]{1,0:T(8,128)(2,1)S(1)}, bf16[128,1536]{1,0:T(8,128)(2,1)S(1)}, u32[]{:S(2)}, u32[]{:S(2)}) collective-permute-start(bf16[128,1536]{1,0:T(8,128)(2,1)S(1)} %copy-done.1), channel_id=1, source_target_pairs={{0,16},{1,49},{16,32},{17,1},{32,48},{33,17},{48,0},{49,33},{2,18}... | collective-permute-start | bytes 1179656 | tf_op jit(solution)/shard_map/ppermute | solution.py:48
  34.9 0.1 assemble.1.w_ref
  35.0 0.3 latent_part.1
  35.3 1.8 %collective-permute-start.11 = (bf16[64,640]{1,0:T(8,128)(2,1)S(1)}, bf16[64,640]{1,0:T(8,128)(2,1)S(1)}, u32[]{:S(2)}, u32[]{:S(2)}) collective-permute-start(bf16[64,640]{1,0:T(8,128)(2,1)S(1)} %get-tuple-element.43.p0), channel_id=1, source_target_pairs={{0,6},{2,0},{4,2},{6,4},{1,7},{3,1},{5,3},{7,5},{8,14},{10,8},{12,... | collective-permute-start | bytes 245768 | tf_op jit(solution)/shard_map/ppermute | solution.py:32
  37.1 1.2 %collective-permute-start.10 = (bf16[64,640]{1,0:T(8,128)(2,1)S(1)}, bf16[64,640]{1,0:T(8,128)(2,1)S(1)}, u32[]{:S(2)}, u32[]{:S(2)}) collective-permute-start(bf16[64,640]{1,0:T(8,128)(2,1)S(1)} %get-tuple-element.43.p0), channel_id=1, source_target_pairs={{0,4},{2,6},{4,0},{6,2},{1,5},{3,7},{5,1},{7,3},{8,12},{10,14},{12... | collective-permute-start | bytes 245768 | tf_op jit(solution)/shard_map/ppermute | solution.py:32
  38.4 0.7 tables.1
  39.1 0.8 collective-permute-done.11.p3
  39.9 6.5 %collective-permute-done.10.p2 = bf16[64,640]{1,0:T(8,128)(2,1)S(1)} collective-permute-done((bf16[64,640]{1,0:T(8,128)(2,1)S(1)}, bf16[64,640]{1,0:T(8,128)(2,1)S(1)}, u32[]{:S(2)}, u32[]{:S(2)}) %collective-permute-start.10) | collective-permute-done | bytes 81952 | tf_op jit(solution)/shard_map/ppermute | solution.py:32
  46.4 0.3 kv_rows.1.refs_0_
  46.7 2.4 %collective-permute-start.12 = (bf16[64,640]{1,0:T(8,128)(2,1)S(1)}, bf16[64,640]{1,0:T(8,128)(2,1)S(1)}, u32[]{:S(2)}, u32[]{:S(2)}) collective-permute-start(bf16[64,640]{1,0:T(8,128)(2,1)S(1)} %kv_rows.1.refs_0_), channel_id=1, source_target_pairs={{0,12},{2,14},{4,8},{6,10},{8,4},{10,6},{12,0},{14,2},{1,13},{3,15... | collective-permute-start | bytes 245768 | tf_op jit(solution)/shard_map/ppermute | solution.py:71
  49.1 0.7 collective-permute-start.22
  49.7 3.6 %collective-permute-done.12.refs_1_ = bf16[64,640]{1,0:T(8,128)(2,1)S(1)} collective-permute-done((bf16[64,640]{1,0:T(8,128)(2,1)S(1)}, bf16[64,640]{1,0:T(8,128)(2,1)S(1)}, u32[]{:S(2)}, u32[]{:S(2)}) %collective-permute-start.12) | collective-permute-done | bytes 81952 | tf_op jit(solution)/shard_map/ppermute | solution.py:71
  53.3 2.3 %collective-permute-start.16 = (bf16[128,640]{1,0:T(8,128)(2,1)S(1)}, bf16[128,640]{1,0:T(8,128)(2,1)S(1)}, u32[]{:S(2)}, u32[]{:S(2)}) collective-permute-start(bf16[128,640]{1,0:T(8,128)(2,1)S(1)} %pack.3.refs_0_), channel_id=1, source_target_pairs={{0,64},{64,128},{128,192},{192,0},{1,65},{65,129},{129,193},{193,1... | collective-permute-start | bytes 491528 | tf_op jit(solution)/shard_map/ppermute | solution.py:32
  55.6 0.2 collective-permute-start.15
  55.8 1.3 %collective-permute-start.14 = (bf16[128,640]{1,0:T(8,128)(2,1)S(1)}, bf16[128,640]{1,0:T(8,128)(2,1)S(1)}, u32[]{:S(2)}, u32[]{:S(2)}) collective-permute-start(bf16[128,640]{1,0:T(8,128)(2,1)S(1)} %pack.3.refs_0_), channel_id=1, source_target_pairs={{0,192},{64,0},{128,64},{192,128},{1,193},{65,1},{129,65},{193,129... | collective-permute-start | bytes 491528 | tf_op jit(solution)/shard_map/ppermute | solution.py:32
  57.1 4.1 %collective-permute-done.16.refs_3_ = bf16[128,640]{1,0:T(8,128)(2,1)S(1)} collective-permute-done((bf16[128,640]{1,0:T(8,128)(2,1)S(1)}, bf16[128,640]{1,0:T(8,128)(2,1)S(1)}, u32[]{:S(2)}, u32[]{:S(2)}) %collective-permute-start.16) | collective-permute-done | bytes 163872 | tf_op jit(solution)/shard_map/ppermute | solution.py:32
  61.3 2.0 %collective-permute-done.15.refs_2_ = bf16[128,640]{1,0:T(8,128)(2,1)S(1)} collective-permute-done((bf16[128,640]{1,0:T(8,128)(2,1)S(1)}, bf16[128,640]{1,0:T(8,128)(2,1)S(1)}, u32[]{:S(2)}, u32[]{:S(2)}) %collective-permute-start.15) | collective-permute-done | bytes 163872 | tf_op jit(solution)/shard_map/ppermute | solution.py:32
  63.3 1.6 %collective-permute-done.14.refs_1_ = bf16[128,640]{1,0:T(8,128)(2,1)S(1)} collective-permute-done((bf16[128,640]{1,0:T(8,128)(2,1)S(1)}, bf16[128,640]{1,0:T(8,128)(2,1)S(1)}, u32[]{:S(2)}, u32[]{:S(2)}) %collective-permute-start.14) | collective-permute-done | bytes 163872 | tf_op jit(solution)/shard_map/ppermute | solution.py:32
  64.9 1.4 %collective-permute-done.18.refs_5_ = bf16[128,640]{1,0:T(8,128)(2,1)S(1)} collective-permute-done((bf16[128,640]{1,0:T(8,128)(2,1)S(1)}, bf16[128,640]{1,0:T(8,128)(2,1)S(1)}, u32[]{:S(2)}, u32[]{:S(2)}) %collective-permute-start.18) | collective-permute-done | bytes 163872 | tf_op jit(solution)/shard_map/ppermute | solution.py:36
  66.3 3.5 %lift.1 = (bf16[8,1024,256]{2,1,0:T(8,128)(2,1)S(1)}, bf16[8,1024,256]{2,1,0:T(8,128)(2,1)S(1)}) custom-call(s32[1]{0:T(128)} %bitcast.s, s32[64]{0:T(128)S(1)} %copy-done.4, bf16[128,640]{1,0:T(8,128)(2,1)S(1)} %pack.3.refs_0_, bf16[128,640]{1,0:T(8,128)(2,1)S(1)} %collective-permute-done.14.refs_1_, bf16[128,640]{1,0:T(8,128)(2,1)S(1)} %collective-permute-done.15.refs_2_, ...), custom_call_target="tpu_custom_call" | custom-call | tf_op jit(solution)/shard_map/lift/pallas_call | solution.py:280
  69.7 3.0 %attend.5 = bf16[128,1152]{1,0:T(8,128)(2,1)S(1)} custom-call(s32[1]{0:T(128)} %bitcast.s, s32[64]{0:T(128)S(1)} %copy-done.4, bf16[128,1536]{1,0:T(8,128)(2,1)S(1)} %collective-permute-done.13.refs_2_.refs_0_, bf16[8,1024,256]{2,1,0:T(8,128)(2,1)S(1)} %get-tuple-element.60.refs_1_.refs_2_, bf16[8,1024,256]{2,1,0:T(8,128)(2,1)S(1)} %get-tuple-element.61.refs_2_.refs_3_), custom_call_target="tpu_custom_call" | custom-call | tf_op jit(solution)/shard_map/attend/pallas_call | solution.py:360
  72.7 1.4 %collective-permute-start.24 = (bf16[128,1152]{1,0:T(8,128)(2,1)S(1)}, bf16[128,1152]{1,0:T(8,128)(2,1)S(1)}, u32[]{:S(2)}, u32[]{:S(2)}) collective-permute-start(bf16[128,1152]{1,0:T(8,128)(2,1)S(1)} %attend.5), channel_id=1, source_target_pairs={{0,16},{1,49},{16,32},{17,1},{32,48},{33,17},{48,0},{49,33},{2,18}... | collective-permute-start | bytes 884744 | tf_op jit(solution)/shard_map/ppermute | solution.py:48
  74.1 3.6 %attend.4 = (bf16[128,1152]{1,0:T(8,128)(2,1)S(1)}, bf16[128,1152]{1,0:T(8,128)(2,1)S(1)}) custom-call(s32[1]{0:T(128)} %bitcast.s, s32[64]{0:T(128)S(1)} %copy-done.4, bf16[128,1536]{1,0:T(8,128)(2,1)S(1)} %collective-permute-done.21.refs_0_, bf16[128,1536]{1,0:T(8,128)(2,1)S(1)} %collective-permute-done.22.refs_1_, ...), custom_call_target="tpu_custom_call" | custom-call | tf_op jit(solution)/shard_map/attend/pallas_call | solution.py:360
  77.8 2.2 %collective-permute-start.23 = (bf16[128,1152]{1,0:T(8,128)(2,1)S(1)}, bf16[128,1152]{1,0:T(8,128)(2,1)S(1)}, u32[]{:S(2)}, u32[]{:S(2)}) collective-permute-start(bf16[128,1152]{1,0:T(8,128)(2,1)S(1)} %get-tuple-element.64), channel_id=1, source_target_pairs={{0,48},{1,17},{16,0},{17,33},{32,16},{33,49},{48,32},{49,1},{2,50}... | collective-permute-start | bytes 884744 | tf_op jit(solution)/shard_map/ppermute | solution.py:48
  80.0 1.1 %collective-permute-done.24.got_ref = bf16[128,1152]{1,0:T(8,128)(2,1)S(1)} collective-permute-done((bf16[128,1152]{1,0:T(8,128)(2,1)S(1)}, bf16[128,1152]{1,0:T(8,128)(2,1)S(1)}, u32[]{:S(2)}, u32[]{:S(2)}) %collective-permute-start.24) | collective-permute-done | bytes 294944 | tf_op jit(solution)/shard_map/ppermute | solution.py:48
  81.1 0.5 relay.1
  81.8 2.8 %collective-permute-start.27 = (bf16[16,896]{1,0:T(8,128)(2,1)S(1)}, bf16[16,896]{1,0:T(8,128)(2,1)S(1)}, u32[]{:S(2)}, u32[]{:S(2)}) collective-permute-start(bf16[16,896]{1,0:T(8,128)(2,1)S(1)} %get-tuple-element.68), channel_id=1, source_target_pairs={{0,4},{2,6},{4,0},{6,2},{1,5},{3,7},{5,1},{7,3},{8,12},{10,14},{12... | collective-permute-start | bytes 86024 | tf_op jit(solution)/shard_map/ppermute | solution.py:32
  84.5 2.9 %collective-permute-start.28 = (bf16[16,896]{1,0:T(8,128)(2,1)S(1)}, bf16[16,896]{1,0:T(8,128)(2,1)S(1)}, u32[]{:S(2)}, u32[]{:S(2)}) collective-permute-start(bf16[16,896]{1,0:T(8,128)(2,1)S(1)} %get-tuple-element.69), channel_id=1, source_target_pairs={{0,6},{2,0},{4,2},{6,4},{1,7},{3,1},{5,3},{7,5},{8,14},{10,8},{12,... | collective-permute-start | bytes 86024 | tf_op jit(solution)/shard_map/ppermute | solution.py:32
  87.4 3.0 %attend.3.a_ref = bf16[128,1152]{1,0:T(8,128)(2,1)S(1)} custom-call(s32[1]{0:T(128)} %bitcast.s, s32[64]{0:T(128)S(1)} %copy-done.4, bf16[128,1536]{1,0:T(8,128)(2,1)S(1)} %copy-done.1, bf16[8,1024,256]{2,1,0:T(8,128)(2,1)S(1)} %get-tuple-element.60.refs_1_.refs_2_, bf16[8,1024,256]{2,1,0:T(8,128)(2,1)S(1)} %get-tuple-element.61.refs_2_.refs_3_), custom_call_target="tpu_custom_call" | custom-call | tf_op jit(solution)/shard_map/attend/pallas_call | solution.py:360
  90.5 1.4 %final.1 = (bf16[16,3584]{1,0:T(8,128)(2,1)}, bf16[128,1024]{1,0:T(8,128)(2,1)}) custom-call(s32[1]{0:T(128)} %bitcast.s, bf16[128,1152]{1,0:T(8,128)(2,1)S(1)} %attend.3.a_ref, bf16[128,1152]{1,0:T(8,128)(2,1)S(1)} %collective-permute-done.23.b_ref, bf16[128,1152]{1,0:T(8,128)(2,1)S(1)} %collective-permute-done.25.c_ref, ...), custom_call_target="tpu_custom_call" | custom-call | tf_op jit(solution)/shard_map/final/pallas_call | solution.py:402
  (40 shorter events, 0.5 us)
Async XLA Ops:
  0.6 13.8 %collective-permute-start = (bf16[112,576]{1,0:T(8,128)(2,1)}, bf16[112,576]{1,0:T(8,128)(2,1)S(1)}, u32[]{:S(2)}, u32[]{:S(2)}) collective-permute-start(bf16[112,576]{1,0:T(8,128)(2,1)} %param.19), channel_id=1, source_target_pairs={{2,0},{14,1},{67,2},{79,3},{132,4},{136,5},{197,6},{201,7},{6,8},{... | collective-permute-start | bytes 387080 | tf_op jit(solution)/shard_map/ppermute | solution.py:66
  7.7 0.9 %copy-start.2 = (bf16[128,1024]{1,0:T(8,128)(2,1)S(1)}, bf16[128,1024]{1,0:T(8,128)(2,1)}, u32[]{:S(2)}) copy-start(bf16[128,1024]{1,0:T(8,128)(2,1)} %param.12) | copy-start | bytes 786436
  8.6 0.9 copy-start.3
  9.5 21.1 %copy-start.1 = (bf16[128,1536]{1,0:T(8,128)(2,1)S(1)}, bf16[128,1536]{1,0:T(8,128)(2,1)}, u32[]{:S(2)}) copy-start(bf16[128,1536]{1,0:T(8,128)(2,1)} %refs_0_.1) | copy-start | bytes 1179652
  9.5 25.3 %copy-start.5 = (bf16[3584]{0:T(1024)(128)(2,1)S(1)}, bf16[3584]{0:T(1024)(128)(2,1)}, u32[]{:S(2)}) copy-start(bf16[3584]{0:T(1024)(128)(2,1)} %param.18) | copy-start | bytes 21508
  14.4 24.0 %copy-start.6 = (bf16[512]{0:T(512)(128)(2,1)S(1)}, bf16[512]{0:T(512)(128)(2,1)}, u32[]{:S(2)}) copy-start(bf16[512]{0:T(512)(128)(2,1)} %param.20) | copy-start | bytes 3076
  14.4 24.0 %copy-start.4 = (s32[64]{0:T(128)S(1)}, s32[64]{0:T(128)}, u32[]{:S(2)}) copy-start(s32[64]{0:T(128)} %seg.8) | copy-start | bytes 772
  14.4 51.9 %copy-start = (bf16[512,2048]{1,0:T(8,128)(2,1)S(1)}, bf16[512,2048]{1,0:T(8,128)(2,1)}, u32[]{:S(2)}) copy-start(bf16[512,2048]{1,0:T(8,128)(2,1)} %refs_8_.1) | copy-start | bytes 6291460
  14.4 4.3 %collective-permute-start.1 = (bf16[4,64,896]{2,1,0:T(8,128)(2,1)S(1)}, bf16[4,64,896]{2,1,0:T(8,128)(2,1)S(1)}, u32[]{:S(2)}, u32[]{:S(2)}) collective-permute-start(bf16[4,64,896]{2,1,0:T(8,128)(2,1)S(1)} %get-tuple-element.38), channel_id=1, source_target_pairs={{0,1},{1,0},{2,3},{3,2},{4,5},{5,4},{6,7},{7,6},{8,9},{9,8},{10,11... | collective-permute-start | bytes 1376264 | tf_op jit(solution)/shard_map/ppermute | solution.py:36
  14.5 9.9 %collective-permute-start.7 = (bf16[1,112,576]{2,1,0:T(8,128)(2,1)S(1)}, bf16[1,112,576]{2,1,0:T(8,128)(2,1)S(1)}, u32[]{:S(2)}, u32[]{:S(2)}) collective-permute-start(bf16[1,112,576]{2,1,0:T(8,128)(2,1)S(1)} %bitcast.4), channel_id=1, source_target_pairs={{0,48},{16,32},{32,16},{48,0},{1,49},{17,33},{33,17},{49,1},{2,50}... | collective-permute-start | bytes 387080 | tf_op jit(solution)/shard_map/ppermute | solution.py:36
  17.4 8.2 %collective-permute-start.6 = (bf16[1,112,576]{2,1,0:T(8,128)(2,1)S(1)}, bf16[1,112,576]{2,1,0:T(8,128)(2,1)S(1)}, u32[]{:S(2)}, u32[]{:S(2)}) collective-permute-start(bf16[1,112,576]{2,1,0:T(8,128)(2,1)S(1)} %bitcast.5), channel_id=1, source_target_pairs={{0,32},{16,48},{32,0},{48,16},{1,33},{17,49},{33,1},{49,17},{2,34}... | collective-permute-start | bytes 387080 | tf_op jit(solution)/shard_map/ppermute | solution.py:36
  18.2 7.4 %collective-permute-start.5 = (bf16[1,112,576]{2,1,0:T(8,128)(2,1)S(1)}, bf16[1,112,576]{2,1,0:T(8,128)(2,1)S(1)}, u32[]{:S(2)}, u32[]{:S(2)}) collective-permute-start(bf16[1,112,576]{2,1,0:T(8,128)(2,1)S(1)} %bitcast.6), channel_id=1, source_target_pairs={{0,16},{16,0},{32,48},{48,32},{1,17},{17,1},{33,49},{49,33},{2,18}... | collective-permute-start | bytes 387080 | tf_op jit(solution)/shard_map/ppermute | solution.py:36
  18.8 8.0 %collective-permute-start.2 = (bf16[64,896]{1,0:T(8,128)(2,1)S(1)}, bf16[64,896]{1,0:T(8,128)(2,1)S(1)}, u32[]{:S(2)}, u32[]{:S(2)}) collective-permute-start(bf16[64,896]{1,0:T(8,128)(2,1)S(1)} %get-tuple-element.39), channel_id=1, source_target_pairs={{0,2},{2,4},{4,6},{6,0},{1,3},{3,5},{5,7},{7,1},{8,10},{10,12},{12... | collective-permute-start | bytes 344072 | tf_op jit(solution)/shard_map/ppermute | solution.py:32
  18.9 11.5 %collective-permute-start.3 = (bf16[64,896]{1,0:T(8,128)(2,1)S(1)}, bf16[64,896]{1,0:T(8,128)(2,1)S(1)}, u32[]{:S(2)}, u32[]{:S(2)}) collective-permute-start(bf16[64,896]{1,0:T(8,128)(2,1)S(1)} %get-tuple-element.40), channel_id=1, source_target_pairs={{0,4},{2,6},{4,0},{6,2},{1,5},{3,7},{5,1},{7,3},{8,12},{10,14},{12... | collective-permute-start | bytes 344072 | tf_op jit(solution)/shard_map/ppermute | solution.py:32
  24.5 6.0 %collective-permute-start.4 = (bf16[64,896]{1,0:T(8,128)(2,1)S(1)}, bf16[64,896]{1,0:T(8,128)(2,1)S(1)}, u32[]{:S(2)}, u32[]{:S(2)}) collective-permute-start(bf16[64,896]{1,0:T(8,128)(2,1)S(1)} %get-tuple-element.41), channel_id=1, source_target_pairs={{0,6},{2,0},{4,2},{6,4},{1,7},{3,1},{5,3},{7,5},{8,14},{10,8},{12,... | collective-permute-start | bytes 344072 | tf_op jit(solution)/shard_map/ppermute | solution.py:32
  30.6 4.3 %collective-permute-start.8 = (bf16[4,112,576]{2,1,0:T(8,128)(2,1)S(1)}, bf16[4,112,576]{2,1,0:T(8,128)(2,1)S(1)}, u32[]{:S(2)}, u32[]{:S(2)}) collective-permute-start(bf16[4,112,576]{2,1,0:T(8,128)(2,1)S(1)} %pack.2.own_ref), channel_id=1, source_target_pairs={{0,1},{1,0},{2,3},{3,2},{4,5},{5,4},{6,7},{7,6},{8,9},{9,8},{10,11... | collective-permute-start | bytes 1548296 | tf_op jit(solution)/shard_map/ppermute | solution.py:36
  30.7 18.4 %collective-permute-start.13 = (bf16[128,1536]{1,0:T(8,128)(2,1)S(1)}, bf16[128,1536]{1,0:T(8,128)(2,1)S(1)}, u32[]{:S(2)}, u32[]{:S(2)}) collective-permute-start(bf16[128,1536]{1,0:T(8,128)(2,1)S(1)} %copy-done.1), channel_id=1, source_target_pairs={{0,32},{16,48},{32,0},{48,16},{1,33},{17,49},{33,1},{49,17},{2,34}... | collective-permute-start | bytes 1179656 | tf_op jit(solution)/shard_map/ppermute | solution.py:32
  33.7 23.4 %collective-permute-start.21 = (bf16[128,1536]{1,0:T(8,128)(2,1)S(1)}, bf16[128,1536]{1,0:T(8,128)(2,1)S(1)}, u32[]{:S(2)}, u32[]{:S(2)}) collective-permute-start(bf16[128,1536]{1,0:T(8,128)(2,1)S(1)} %copy-done.1), channel_id=1, source_target_pairs={{0,16},{1,49},{16,32},{17,1},{32,48},{33,17},{48,0},{49,33},{2,18}... | collective-permute-start | bytes 1179656 | tf_op jit(solution)/shard_map/ppermute | solution.py:48
  35.3 4.6 %collective-permute-start.11 = (bf16[64,640]{1,0:T(8,128)(2,1)S(1)}, bf16[64,640]{1,0:T(8,128)(2,1)S(1)}, u32[]{:S(2)}, u32[]{:S(2)}) collective-permute-start(bf16[64,640]{1,0:T(8,128)(2,1)S(1)} %get-tuple-element.43.p0), channel_id=1, source_target_pairs={{0,6},{2,0},{4,2},{6,4},{1,7},{3,1},{5,3},{7,5},{8,14},{10,8},{12,... | collective-permute-start | bytes 245768 | tf_op jit(solution)/shard_map/ppermute | solution.py:32
  37.1 9.3 %collective-permute-start.10 = (bf16[64,640]{1,0:T(8,128)(2,1)S(1)}, bf16[64,640]{1,0:T(8,128)(2,1)S(1)}, u32[]{:S(2)}, u32[]{:S(2)}) collective-permute-start(bf16[64,640]{1,0:T(8,128)(2,1)S(1)} %get-tuple-element.43.p0), channel_id=1, source_target_pairs={{0,4},{2,6},{4,0},{6,2},{1,5},{3,7},{5,1},{7,3},{8,12},{10,14},{12... | collective-permute-start | bytes 245768 | tf_op jit(solution)/shard_map/ppermute | solution.py:32
  38.4 8.0 %collective-permute-start.9 = (bf16[64,640]{1,0:T(8,128)(2,1)S(1)}, bf16[64,640]{1,0:T(8,128)(2,1)S(1)}, u32[]{:S(2)}, u32[]{:S(2)}) collective-permute-start(bf16[64,640]{1,0:T(8,128)(2,1)S(1)} %get-tuple-element.43.p0), channel_id=1, source_target_pairs={{0,2},{2,4},{4,6},{6,0},{1,3},{3,5},{5,7},{7,1},{8,10},{10,12},{12... | collective-permute-start | bytes 245768 | tf_op jit(solution)/shard_map/ppermute | solution.py:32
  46.7 6.6 %collective-permute-start.12 = (bf16[64,640]{1,0:T(8,128)(2,1)S(1)}, bf16[64,640]{1,0:T(8,128)(2,1)S(1)}, u32[]{:S(2)}, u32[]{:S(2)}) collective-permute-start(bf16[64,640]{1,0:T(8,128)(2,1)S(1)} %kv_rows.1.refs_0_), channel_id=1, source_target_pairs={{0,12},{2,14},{4,8},{6,10},{8,4},{10,6},{12,0},{14,2},{1,13},{3,15... | collective-permute-start | bytes 245768 | tf_op jit(solution)/shard_map/ppermute | solution.py:71
  49.1 15.8 %collective-permute-start.22 = (bf16[128,1536]{1,0:T(8,128)(2,1)S(1)}, bf16[128,1536]{1,0:T(8,128)(2,1)S(1)}, u32[]{:S(2)}, u32[]{:S(2)}) collective-permute-start(bf16[128,1536]{1,0:T(8,128)(2,1)S(1)} %copy-done.1), channel_id=1, source_target_pairs={{0,48},{1,17},{16,0},{17,33},{32,16},{33,49},{48,32},{49,1},{2,50}... | collective-permute-start | bytes 1179656 | tf_op jit(solution)/shard_map/ppermute | solution.py:48
  53.3 7.9 %collective-permute-start.16 = (bf16[128,640]{1,0:T(8,128)(2,1)S(1)}, bf16[128,640]{1,0:T(8,128)(2,1)S(1)}, u32[]{:S(2)}, u32[]{:S(2)}) collective-permute-start(bf16[128,640]{1,0:T(8,128)(2,1)S(1)} %pack.3.refs_0_), channel_id=1, source_target_pairs={{0,64},{64,128},{128,192},{192,0},{1,65},{65,129},{129,193},{193,1... | collective-permute-start | bytes 491528 | tf_op jit(solution)/shard_map/ppermute | solution.py:32
  55.6 7.7 %collective-permute-start.15 = (bf16[128,640]{1,0:T(8,128)(2,1)S(1)}, bf16[128,640]{1,0:T(8,128)(2,1)S(1)}, u32[]{:S(2)}, u32[]{:S(2)}) collective-permute-start(bf16[128,640]{1,0:T(8,128)(2,1)S(1)} %pack.3.refs_0_), channel_id=1, source_target_pairs={{0,128},{64,192},{128,0},{192,64},{1,129},{65,193},{129,1},{193,65... | collective-permute-start | bytes 491528 | tf_op jit(solution)/shard_map/ppermute | solution.py:32
  55.8 9.1 %collective-permute-start.14 = (bf16[128,640]{1,0:T(8,128)(2,1)S(1)}, bf16[128,640]{1,0:T(8,128)(2,1)S(1)}, u32[]{:S(2)}, u32[]{:S(2)}) collective-permute-start(bf16[128,640]{1,0:T(8,128)(2,1)S(1)} %pack.3.refs_0_), channel_id=1, source_target_pairs={{0,192},{64,0},{128,64},{192,128},{1,193},{65,1},{129,65},{193,129... | collective-permute-start | bytes 491528 | tf_op jit(solution)/shard_map/ppermute | solution.py:32
  57.1 7.8 %collective-permute-start.17 = (bf16[128,640]{1,0:T(8,128)(2,1)S(1)}, bf16[128,640]{1,0:T(8,128)(2,1)S(1)}, u32[]{:S(2)}, u32[]{:S(2)}) collective-permute-start(bf16[128,640]{1,0:T(8,128)(2,1)S(1)} %pack.3.refs_0_), channel_id=1, source_target_pairs={{0,1},{1,0},{2,3},{3,2},{4,5},{5,4},{6,7},{7,6},{8,9},{9,8},{10,11... | collective-permute-start | bytes 491528 | tf_op jit(solution)/shard_map/ppermute | solution.py:36
  61.3 3.6 %collective-permute-start.20 = (bf16[128,640]{1,0:T(8,128)(2,1)S(1)}, bf16[128,640]{1,0:T(8,128)(2,1)S(1)}, u32[]{:S(2)}, u32[]{:S(2)}) collective-permute-start(bf16[128,640]{1,0:T(8,128)(2,1)S(1)} %collective-permute-done.16.refs_3_), channel_id=1, source_target_pairs={{0,1},{1,0},{2,3},{3,2},{4,5},{5,4},{6,7},{7,6},{8,9},{9,8},{10,11... | collective-permute-start | bytes 491528 | tf_op jit(solution)/shard_map/ppermute | solution.py:36
  63.3 1.6 %collective-permute-start.19 = (bf16[128,640]{1,0:T(8,128)(2,1)S(1)}, bf16[128,640]{1,0:T(8,128)(2,1)S(1)}, u32[]{:S(2)}, u32[]{:S(2)}) collective-permute-start(bf16[128,640]{1,0:T(8,128)(2,1)S(1)} %collective-permute-done.15.refs_2_), channel_id=1, source_target_pairs={{0,1},{1,0},{2,3},{3,2},{4,5},{5,4},{6,7},{7,6},{8,9},{9,8},{10,11... | collective-permute-start | bytes 491528 | tf_op jit(solution)/shard_map/ppermute | solution.py:36
  64.9 1.4 %collective-permute-start.18 = (bf16[128,640]{1,0:T(8,128)(2,1)S(1)}, bf16[128,640]{1,0:T(8,128)(2,1)S(1)}, u32[]{:S(2)}, u32[]{:S(2)}) collective-permute-start(bf16[128,640]{1,0:T(8,128)(2,1)S(1)} %collective-permute-done.14.refs_1_), channel_id=1, source_target_pairs={{0,1},{1,0},{2,3},{3,2},{4,5},{5,4},{6,7},{7,6},{8,9},{9,8},{10,11... | collective-permute-start | bytes 491528 | tf_op jit(solution)/shard_map/ppermute | solution.py:36
  72.7 8.4 %collective-permute-start.24 = (bf16[128,1152]{1,0:T(8,128)(2,1)S(1)}, bf16[128,1152]{1,0:T(8,128)(2,1)S(1)}, u32[]{:S(2)}, u32[]{:S(2)}) collective-permute-start(bf16[128,1152]{1,0:T(8,128)(2,1)S(1)} %attend.5), channel_id=1, source_target_pairs={{0,16},{1,49},{16,32},{17,1},{32,48},{33,17},{48,0},{49,33},{2,18}... | collective-permute-start | bytes 884744 | tf_op jit(solution)/shard_map/ppermute | solution.py:48
  77.8 12.6 %collective-permute-start.23 = (bf16[128,1152]{1,0:T(8,128)(2,1)S(1)}, bf16[128,1152]{1,0:T(8,128)(2,1)S(1)}, u32[]{:S(2)}, u32[]{:S(2)}) collective-permute-start(bf16[128,1152]{1,0:T(8,128)(2,1)S(1)} %get-tuple-element.64), channel_id=1, source_target_pairs={{0,48},{1,17},{16,0},{17,33},{32,16},{33,49},{48,32},{49,1},{2,50}... | collective-permute-start | bytes 884744 | tf_op jit(solution)/shard_map/ppermute | solution.py:48
  81.6 8.9 %collective-permute-start.25 = (bf16[128,1152]{1,0:T(8,128)(2,1)S(1)}, bf16[128,1152]{1,0:T(8,128)(2,1)S(1)}, u32[]{:S(2)}, u32[]{:S(2)}) collective-permute-start(bf16[128,1152]{1,0:T(8,128)(2,1)S(1)} %relay.1), channel_id=1, source_target_pairs={{0,16},{1,49},{16,32},{17,1},{32,48},{33,17},{48,0},{49,33},{2,18}... | collective-permute-start | bytes 884744 | tf_op jit(solution)/shard_map/ppermute | solution.py:48
  81.7 8.7 %collective-permute-start.26 = (bf16[16,896]{1,0:T(8,128)(2,1)S(1)}, bf16[16,896]{1,0:T(8,128)(2,1)S(1)}, u32[]{:S(2)}, u32[]{:S(2)}) collective-permute-start(bf16[16,896]{1,0:T(8,128)(2,1)S(1)} %get-tuple-element.67), channel_id=1, source_target_pairs={{0,2},{2,4},{4,6},{6,0},{1,3},{3,5},{5,7},{7,1},{8,10},{10,12},{12... | collective-permute-start | bytes 86024 | tf_op jit(solution)/shard_map/ppermute | solution.py:32
  81.8 8.6 %collective-permute-start.27 = (bf16[16,896]{1,0:T(8,128)(2,1)S(1)}, bf16[16,896]{1,0:T(8,128)(2,1)S(1)}, u32[]{:S(2)}, u32[]{:S(2)}) collective-permute-start(bf16[16,896]{1,0:T(8,128)(2,1)S(1)} %get-tuple-element.68), channel_id=1, source_target_pairs={{0,4},{2,6},{4,0},{6,2},{1,5},{3,7},{5,1},{7,3},{8,12},{10,14},{12... | collective-permute-start | bytes 86024 | tf_op jit(solution)/shard_map/ppermute | solution.py:32
  84.5 5.9 %collective-permute-start.28 = (bf16[16,896]{1,0:T(8,128)(2,1)S(1)}, bf16[16,896]{1,0:T(8,128)(2,1)S(1)}, u32[]{:S(2)}, u32[]{:S(2)}) collective-permute-start(bf16[16,896]{1,0:T(8,128)(2,1)S(1)} %get-tuple-element.69), channel_id=1, source_target_pairs={{0,6},{2,0},{4,2},{6,4},{1,7},{3,1},{5,3},{7,5},{8,14},{10,8},{12,... | collective-permute-start | bytes 86024 | tf_op jit(solution)/shard_map/ppermute | solution.py:32

commit v5 on v4

--- a/solution.py
+++ b/solution.py
@@ -253,7 +253,7 @@
 
 def lift_kernel(s, seg, *refs):
     keys = refs[:8]
-    up_ref, key_ref, value_ref, kv = refs[8:]
+    up_ref, key_ref, value_ref, rope_ref, kv = refs[8:]
     y, x, zh, _, _ = coords(s)
     for k in range(4):
         for a in range(2):
@@ -265,17 +265,15 @@
                     row = pl.multiple_of(upper * 512 + (k * 2 + a) * 64 + other * 32, 32)
                     start = a * 64 + half * 32
                     kv[pl.ds(row, 32), :] = keys[4 * other + k][start : start + 32, :]
-    ones = jnp.ones((1024, 128), BF)
+    rope_ref[...] = kv[:, LATENT:]
     for head in range(HEADS):
         lifted = dot(kv[:, :LATENT], up_ref[:, head * 256 : head * 256 + 256]).astype(BF)
-        key_ref[head, :, :NOPE] = lifted[:, :NOPE]
-        key_ref[head, :, NOPE:] = kv[:, LATENT:]
-        value_ref[head, :, :VDIM] = lifted[:, NOPE:]
-        value_ref[head, :, VDIM:] = ones
+        key_ref[head] = lifted[:, :NOPE]
+        value_ref[head] = lifted[:, NOPE:]
 
 
 def lift(scalars, seg, keys, up):
-    outs = [shape((HEADS, 1024, 256))] * 2
+    outs = [shape((HEADS, 1024, 128))] * 2 + [shape((1024, 128))]
     scratch = [pltpu.VMEM((1024, WIDE), BF)]
     return local(lift_kernel, outs, 24, "lift", 2, 9, scratch)(scalars, seg, *keys, up)
 
@@ -289,8 +287,8 @@
 def attend_kernel(chunks, s, seg, *refs):
     count = len(chunks)
     queries = refs[:count]
-    key_ref, value_ref = refs[count : count + 2]
-    outs = refs[count + 2 :]
+    key_ref, value_ref, rope_ref = refs[count : count + 3]
+    outs = refs[count + 3 :]
     y, x, zh, _, core = coords(s)
     hops = (0, 1 + 2 * core, 2, 3 - 2 * core)
     factor = math.log2(math.e) / math.sqrt(NOPE + ROPE)
@@ -320,13 +318,17 @@
     stat_lane = lax.broadcasted_iota(jnp.int32, (2 * rows, 128), 1)
     stats = jnp.zeros((2 * rows, 128), F32)
     across = (((1,), (1,)), ((), ()))
+    ones = jnp.ones((512, 128), BF)
+    wide_key = lambda h, part: jnp.concatenate([key_ref[h, part, :], rope_ref[part, :]], axis=1)
+    wide_value = lambda h, part: jnp.concatenate([value_ref[h, part, :], ones], axis=1)
+    lows, highs = slice(0, 512), slice(512, 1024)
     near, far = [], []
     for head in range(HEADS):
         column = slice(head * 192, head * 192 + 192)
         pieces = [q[r, column] for q, r in zip(queries, low_rows)] + [q[r, column] for q, r in zip(queries, high_rows)]
         query = jnp.concatenate([jnp.concatenate(pieces, axis=0), jnp.zeros((2 * rows, 64), BF)], axis=1)
-        near.append(lax.dot_general(query, key_ref[head, :512, :], across, preferred_element_type=F32))
-        high = lax.dot_general(query[rows:], key_ref[head, 512:, :], across, preferred_element_type=F32)
+        near.append(lax.dot_general(query, wide_key(head, lows), across, preferred_element_type=F32))
+        high = lax.dot_general(query[rows:], wide_key(head, highs), across, preferred_element_type=F32)
         far.append(high + high_bias)
     low = [scores[:rows] + low_bias for scores in near]
     mid = [scores[rows:] for scores in near]
@@ -336,8 +338,8 @@
     low = [weigh(a, t) for a, t in zip(low, low_top)]
     mid = [weigh(a, t) for a, t in zip(mid, high_top)]
     far = [weigh(a, t) for a, t in zip(far, high_top)]
-    first = [dot(jnp.concatenate([a, b], axis=0), value_ref[h, :512, :]) for h, (a, b) in enumerate(zip(low, mid))]
-    second = [dot(a, value_ref[h, 512:, :]) for h, a in enumerate(far)]
+    first = [dot(jnp.concatenate([a, b], axis=0), wide_value(h, lows)) for h, (a, b) in enumerate(zip(low, mid))]
+    second = [dot(a, wide_value(h, highs)) for h, a in enumerate(far)]
     for head in range(HEADS):
         both = jnp.concatenate([first[head][:rows], first[head][rows:] + second[head]], axis=0)
         top = jnp.concatenate([low_top[head], high_top[head]], axis=0)
@@ -357,7 +359,7 @@
 def attend(chunks, scalars, seg, queries, lifted):
     kernel = functools.partial(attend_kernel, chunks)
     outs = [shape((128, MESSAGE))] * len(chunks)
-    return local(kernel, outs, 32, "attend", 2, len(chunks) + 2)(scalars, seg, *queries, *lifted)
+    return local(kernel, outs, 32, "attend", 2, len(chunks) + 3)(scalars, seg, *queries, *lifted)
 
 
 def spread_levels(ref, width, group):

time: 92 us -> 91.5 us (level)
  Pallas kernels: 21.3 us -> 20.2 us
  transfers between devices with their start and end apart: 29 -> 29, of which waited for: 14 -> 14; matrix products, arithmetic and copies ran while one was open for 0% -> 0% of each run, Pallas kernels for 15% -> 14%
where the time goes in v5:
time: 91.5 us; the launch traced here: 91.4 us
  starting transfers between devices  37.8 us (41%)
  waiting for transfers between devices  30.7 us (34%)
  Pallas kernels  20.2 us (22%)
  local copies, waits for them, and re-layouts  1.89 us (2%)
    ppermute x13, waiting for transfers between devices, shift(): return lax.ppermute(value, axis, [(i, (i + k) % 4) for i in range(4)])  19.9 us
    ppermute x13, starting transfers between devices, shift(): return lax.ppermute(value, axis, [(i, (i + k) % 4) for i in range(4)])  18.4 us
    pallas_call x3, Pallas kernels, attend(): local(kernel, outs, 32, 'attend', 2, len(chunks) + 3)  8.91 us
    ppermute x1, starting transfers between devices, near_block(): return lax.ppermute(value, AXES, perm)  7.06 us
    ppermute x5, starting transfers between devices, turn(): return lax.ppermute(value, ('x', 'core'), perm)  5.48 us
    ppermute x9, waiting for transfers between devices, swap(): return lax.ppermute(value, axis, [(i, i ^ bit) for i in range(size)])  5.37 us
    pallas_call x1, Pallas kernels, project(): pl.pallas_call(project_kernel, in_specs=[pl.BlockSpec(memory_space=pltpu....  4.79 us
    ppermute x9, starting transfers between devices, swap(): return lax.ppermute(value, axis, [(i, i ^ bit) for i in range(size)])  4.38 us
  transfers between devices with their start and end apart: 29, of which 14 were waited for; matrix products, arithmetic and copies ran while one was open for 0% of the time, Pallas kernels for 14%

profile of v5, /device:TPU:24, one launch (start us, length us, event | category | flops | bytes accessed | tf_op | source)
XLA Modules:
  0.0 91.4 jit_solution(6199848665249675423)
XLA Ops:
  0.6 7.1 %collective-permute-start = (bf16[112,576]{1,0:T(8,128)(2,1)}, bf16[112,576]{1,0:T(8,128)(2,1)S(1)}, u32[]{:S(2)}, u32[]{:S(2)}) collective-permute-start(bf16[112,576]{1,0:T(8,128)(2,1)} %param.19), channel_id=1, source_target_pairs={{2,0},{14,1},{67,2},{79,3},{132,4},{136,5},{197,6},{201,7},{6,8},{... | collective-permute-start | bytes 387080 | tf_op jit(solution)/shard_map/ppermute | solution.py:66
  7.7 0.9 %copy-done.2 = bf16[128,1024]{1,0:T(8,128)(2,1)S(1)} copy-done((bf16[128,1024]{1,0:T(8,128)(2,1)S(1)}, bf16[128,1024]{1,0:T(8,128)(2,1)}, u32[]{:S(2)}) %copy-start.2) | copy-done | bytes 262168
  8.6 0.9 copy-done.3
  9.5 4.8 %project.1 = (bf16[4,64,896]{2,1,0:T(8,128)(2,1)S(1)}, bf16[4,64,896]{2,1,0:T(8,128)(2,1)S(1)}) custom-call(s32[1]{0:T(128)} %bitcast.s, bf16[4,2,16,1024]{3,2,1,0:T(8,128)(2,1)S(1)} %bitcast.3, bf16[1024,256]{1,0:T(8,128)(2,1)} %ad_hbm.1, bf16[1024,3584]{1,0:T(8,128)(2,1)} %w_hbm.1, bf16[256,3584]{1,0:T(8,128)(2,1)} %au_hbm.1, bf16[16,3584]{1,0:T(8,128)(2,1)S(1)} %copy-done.3), custom_call_target="tpu_custom_call" | custom-call | tf_op jit(solution)/shard_map/project/pallas_call | solution.py:123
  14.4 0.1 collective-permute-start.1
  14.5 2.8 %collective-permute-start.7 = (bf16[1,112,576]{2,1,0:T(8,128)(2,1)S(1)}, bf16[1,112,576]{2,1,0:T(8,128)(2,1)S(1)}, u32[]{:S(2)}, u32[]{:S(2)}) collective-permute-start(bf16[1,112,576]{2,1,0:T(8,128)(2,1)S(1)} %bitcast.4), channel_id=1, source_target_pairs={{0,48},{16,32},{32,16},{48,0},{1,49},{17,33},{33,17},{49,1},{2,50}... | collective-permute-start | bytes 387080 | tf_op jit(solution)/shard_map/ppermute | solution.py:36
  17.3 0.8 collective-permute-start.6
  18.1 0.5 collective-permute-start.5
  18.8 2.0 %collective-permute-start.3 = (bf16[64,896]{1,0:T(8,128)(2,1)S(1)}, bf16[64,896]{1,0:T(8,128)(2,1)S(1)}, u32[]{:S(2)}, u32[]{:S(2)}) collective-permute-start(bf16[64,896]{1,0:T(8,128)(2,1)S(1)} %get-tuple-element.41), channel_id=1, source_target_pairs={{0,4},{2,6},{4,0},{6,2},{1,5},{3,7},{5,1},{7,3},{8,12},{10,14},{12... | collective-permute-start | bytes 344072 | tf_op jit(solution)/shard_map/ppermute | solution.py:32
  20.8 3.6 %collective-permute-done.7.refs_3_ = bf16[1,112,576]{2,1,0:T(8,128)(2,1)S(1)} collective-permute-done((bf16[1,112,576]{2,1,0:T(8,128)(2,1)S(1)}, bf16[1,112,576]{2,1,0:T(8,128)(2,1)S(1)}, u32[]{:S(2)}, u32[]{:S(2)}) %collective-permute-start.7) | collective-permute-done | bytes 129056 | tf_op jit(solution)/shard_map/ppermute | solution.py:36
  24.4 0.8 collective-permute-start.4
  25.2 0.3 collective-permute-done.6.refs_2_
  25.5 0.1 collective-permute-done.5.refs_1_
  25.6 1.2 %collective-permute-done.2.refs_4_.r1 = bf16[64,896]{1,0:T(8,128)(2,1)S(1)} collective-permute-done((bf16[64,896]{1,0:T(8,128)(2,1)S(1)}, bf16[64,896]{1,0:T(8,128)(2,1)S(1)}, u32[]{:S(2)}, u32[]{:S(2)}) %collective-permute-start.2) | collective-permute-done | bytes 114720 | tf_op jit(solution)/shard_map/ppermute | solution.py:32
  26.8 3.5 %collective-permute-done.3.refs_5_.r2 = bf16[64,896]{1,0:T(8,128)(2,1)S(1)} collective-permute-done((bf16[64,896]{1,0:T(8,128)(2,1)S(1)}, bf16[64,896]{1,0:T(8,128)(2,1)S(1)}, u32[]{:S(2)}, u32[]{:S(2)}) %collective-permute-start.3) | collective-permute-done | bytes 114720 | tf_op jit(solution)/shard_map/ppermute | solution.py:32
  30.3 0.1 collective-permute-done.4.refs_6_.r3
  30.5 0.1 collective-permute-start.8
  30.6 3.0 %collective-permute-start.13 = (bf16[128,1536]{1,0:T(8,128)(2,1)S(1)}, bf16[128,1536]{1,0:T(8,128)(2,1)S(1)}, u32[]{:S(2)}, u32[]{:S(2)}) collective-permute-start(bf16[128,1536]{1,0:T(8,128)(2,1)S(1)} %copy-done.1), channel_id=1, source_target_pairs={{0,32},{16,48},{32,0},{48,16},{1,33},{17,49},{33,1},{49,17},{2,34}... | collective-permute-start | bytes 1179656 | tf_op jit(solution)/shard_map/ppermute | solution.py:32
  33.6 1.1 %collective-permute-start.21 = (bf16[128,1536]{1,0:T(8,128)(2,1)S(1)}, bf16[128,1536]{1,0:T(8,128)(2,1)S(1)}, u32[]{:S(2)}, u32[]{:S(2)}) collective-permute-start(bf16[128,1536]{1,0:T(8,128)(2,1)S(1)} %copy-done.1), channel_id=1, source_target_pairs={{0,16},{1,49},{16,32},{17,1},{32,48},{33,17},{48,0},{49,33},{2,18}... | collective-permute-start | bytes 1179656 | tf_op jit(solution)/shard_map/ppermute | solution.py:48
  34.8 0.1 assemble.1.w_ref
  35.0 0.3 latent_part.1
  35.3 1.8 %collective-permute-start.11 = (bf16[64,640]{1,0:T(8,128)(2,1)S(1)}, bf16[64,640]{1,0:T(8,128)(2,1)S(1)}, u32[]{:S(2)}, u32[]{:S(2)}) collective-permute-start(bf16[64,640]{1,0:T(8,128)(2,1)S(1)} %get-tuple-element.44.p0), channel_id=1, source_target_pairs={{0,6},{2,0},{4,2},{6,4},{1,7},{3,1},{5,3},{7,5},{8,14},{10,8},{12,... | collective-permute-start | bytes 245768 | tf_op jit(solution)/shard_map/ppermute | solution.py:32
  37.1 1.2 %collective-permute-start.10 = (bf16[64,640]{1,0:T(8,128)(2,1)S(1)}, bf16[64,640]{1,0:T(8,128)(2,1)S(1)}, u32[]{:S(2)}, u32[]{:S(2)}) collective-permute-start(bf16[64,640]{1,0:T(8,128)(2,1)S(1)} %get-tuple-element.44.p0), channel_id=1, source_target_pairs={{0,4},{2,6},{4,0},{6,2},{1,5},{3,7},{5,1},{7,3},{8,12},{10,14},{12... | collective-permute-start | bytes 245768 | tf_op jit(solution)/shard_map/ppermute | solution.py:32
  38.4 0.7 tables.1
  39.1 0.8 collective-permute-done.11.p3
  39.9 6.5 %collective-permute-done.10.p2 = bf16[64,640]{1,0:T(8,128)(2,1)S(1)} collective-permute-done((bf16[64,640]{1,0:T(8,128)(2,1)S(1)}, bf16[64,640]{1,0:T(8,128)(2,1)S(1)}, u32[]{:S(2)}, u32[]{:S(2)}) %collective-permute-start.10) | collective-permute-done | bytes 81952 | tf_op jit(solution)/shard_map/ppermute | solution.py:32
  46.4 0.3 kv_rows.1.refs_0_
  46.7 2.4 %collective-permute-start.12 = (bf16[64,640]{1,0:T(8,128)(2,1)S(1)}, bf16[64,640]{1,0:T(8,128)(2,1)S(1)}, u32[]{:S(2)}, u32[]{:S(2)}) collective-permute-start(bf16[64,640]{1,0:T(8,128)(2,1)S(1)} %kv_rows.1.refs_0_), channel_id=1, source_target_pairs={{0,12},{2,14},{4,8},{6,10},{8,4},{10,6},{12,0},{14,2},{1,13},{3,15... | collective-permute-start | bytes 245768 | tf_op jit(solution)/shard_map/ppermute | solution.py:71
  49.1 0.7 collective-permute-start.22
  49.8 3.5 %collective-permute-done.12.refs_1_ = bf16[64,640]{1,0:T(8,128)(2,1)S(1)} collective-permute-done((bf16[64,640]{1,0:T(8,128)(2,1)S(1)}, bf16[64,640]{1,0:T(8,128)(2,1)S(1)}, u32[]{:S(2)}, u32[]{:S(2)}) %collective-permute-start.12) | collective-permute-done | bytes 81952 | tf_op jit(solution)/shard_map/ppermute | solution.py:71
  53.3 2.3 %collective-permute-start.16 = (bf16[128,640]{1,0:T(8,128)(2,1)S(1)}, bf16[128,640]{1,0:T(8,128)(2,1)S(1)}, u32[]{:S(2)}, u32[]{:S(2)}) collective-permute-start(bf16[128,640]{1,0:T(8,128)(2,1)S(1)} %pack.3.refs_0_), channel_id=1, source_target_pairs={{0,64},{64,128},{128,192},{192,0},{1,65},{65,129},{129,193},{193,1... | collective-permute-start | bytes 491528 | tf_op jit(solution)/shard_map/ppermute | solution.py:32
  55.6 0.2 collective-permute-start.15
  55.8 1.3 %collective-permute-start.14 = (bf16[128,640]{1,0:T(8,128)(2,1)S(1)}, bf16[128,640]{1,0:T(8,128)(2,1)S(1)}, u32[]{:S(2)}, u32[]{:S(2)}) collective-permute-start(bf16[128,640]{1,0:T(8,128)(2,1)S(1)} %pack.3.refs_0_), channel_id=1, source_target_pairs={{0,192},{64,0},{128,64},{192,128},{1,193},{65,1},{129,65},{193,129... | collective-permute-start | bytes 491528 | tf_op jit(solution)/shard_map/ppermute | solution.py:32
  57.1 4.1 %collective-permute-done.16.refs_3_ = bf16[128,640]{1,0:T(8,128)(2,1)S(1)} collective-permute-done((bf16[128,640]{1,0:T(8,128)(2,1)S(1)}, bf16[128,640]{1,0:T(8,128)(2,1)S(1)}, u32[]{:S(2)}, u32[]{:S(2)}) %collective-permute-start.16) | collective-permute-done | bytes 163872 | tf_op jit(solution)/shard_map/ppermute | solution.py:32
  61.3 2.0 %collective-permute-done.15.refs_2_ = bf16[128,640]{1,0:T(8,128)(2,1)S(1)} collective-permute-done((bf16[128,640]{1,0:T(8,128)(2,1)S(1)}, bf16[128,640]{1,0:T(8,128)(2,1)S(1)}, u32[]{:S(2)}, u32[]{:S(2)}) %collective-permute-start.15) | collective-permute-done | bytes 163872 | tf_op jit(solution)/shard_map/ppermute | solution.py:32
  63.3 1.6 %collective-permute-done.14.refs_1_ = bf16[128,640]{1,0:T(8,128)(2,1)S(1)} collective-permute-done((bf16[128,640]{1,0:T(8,128)(2,1)S(1)}, bf16[128,640]{1,0:T(8,128)(2,1)S(1)}, u32[]{:S(2)}, u32[]{:S(2)}) %collective-permute-start.14) | collective-permute-done | bytes 163872 | tf_op jit(solution)/shard_map/ppermute | solution.py:32
  64.9 1.4 %collective-permute-done.18.refs_5_ = bf16[128,640]{1,0:T(8,128)(2,1)S(1)} collective-permute-done((bf16[128,640]{1,0:T(8,128)(2,1)S(1)}, bf16[128,640]{1,0:T(8,128)(2,1)S(1)}, u32[]{:S(2)}, u32[]{:S(2)}) %collective-permute-start.18) | collective-permute-done | bytes 163872 | tf_op jit(solution)/shard_map/ppermute | solution.py:36
  66.2 3.0 %lift.1 = (bf16[8,1024,128]{2,1,0:T(8,128)(2,1)S(1)}, bf16[8,1024,128]{2,1,0:T(8,128)(2,1)S(1)}, bf16[1024,128]{1,0:T(8,128)(2,1)S(1)}) custom-call(s32[1]{0:T(128)} %bitcast.s, s32[64]{0:T(128)S(1)} %copy-done.4, bf16[128,640]{1,0:T(8,128)(2,1)S(1)} %pack.3.refs_0_, bf16[128,640]{1,0:T(8,128)(2,1)S(1)} %collective-permute-done.14.refs_1_, ...), custom_call_target="tpu_custom_call" | custom-call | tf_op jit(solution)/shard_map/lift/pallas_call | solution.py:278
  69.3 2.8 %attend.5 = bf16[128,1152]{1,0:T(8,128)(2,1)S(1)} custom-call(s32[1]{0:T(128)} %bitcast.s, s32[64]{0:T(128)S(1)} %copy-done.4, bf16[128,1536]{1,0:T(8,128)(2,1)S(1)} %collective-permute-done.13.refs_2_.refs_0_, bf16[8,1024,128]{2,1,0:T(8,128)(2,1)S(1)} %get-tuple-element.61.refs_1_.refs_2_, bf16[8,1024,128]{2,1,0:T(8,128)(2,1)S(1)} %get-tuple-element.62.refs_2_.refs_3_, ...), custom_call_target="tpu_custom_call" | custom-call | tf_op jit(solution)/shard_map/attend/pallas_call | solution.py:362
  72.1 1.5 %collective-permute-start.24 = (bf16[128,1152]{1,0:T(8,128)(2,1)S(1)}, bf16[128,1152]{1,0:T(8,128)(2,1)S(1)}, u32[]{:S(2)}, u32[]{:S(2)}) collective-permute-start(bf16[128,1152]{1,0:T(8,128)(2,1)S(1)} %attend.5), channel_id=1, source_target_pairs={{0,16},{1,49},{16,32},{17,1},{32,48},{33,17},{48,0},{49,33},{2,18}... | collective-permute-start | bytes 884744 | tf_op jit(solution)/shard_map/ppermute | solution.py:48
  73.5 3.3 %attend.4 = (bf16[128,1152]{1,0:T(8,128)(2,1)S(1)}, bf16[128,1152]{1,0:T(8,128)(2,1)S(1)}) custom-call(s32[1]{0:T(128)} %bitcast.s, s32[64]{0:T(128)S(1)} %copy-done.4, bf16[128,1536]{1,0:T(8,128)(2,1)S(1)} %collective-permute-done.21.refs_0_, bf16[128,1536]{1,0:T(8,128)(2,1)S(1)} %collective-permute-done.22.refs_1_, ...), custom_call_target="tpu_custom_call" | custom-call | tf_op jit(solution)/shard_map/attend/pallas_call | solution.py:362
  76.8 2.1 %collective-permute-start.23 = (bf16[128,1152]{1,0:T(8,128)(2,1)S(1)}, bf16[128,1152]{1,0:T(8,128)(2,1)S(1)}, u32[]{:S(2)}, u32[]{:S(2)}) collective-permute-start(bf16[128,1152]{1,0:T(8,128)(2,1)S(1)} %get-tuple-element.66), channel_id=1, source_target_pairs={{0,48},{1,17},{16,0},{17,33},{32,16},{33,49},{48,32},{49,1},{2,50}... | collective-permute-start | bytes 884744 | tf_op jit(solution)/shard_map/ppermute | solution.py:48
  79.0 1.9 %collective-permute-done.24.got_ref = bf16[128,1152]{1,0:T(8,128)(2,1)S(1)} collective-permute-done((bf16[128,1152]{1,0:T(8,128)(2,1)S(1)}, bf16[128,1152]{1,0:T(8,128)(2,1)S(1)}, u32[]{:S(2)}, u32[]{:S(2)}) %collective-permute-start.24) | collective-permute-done | bytes 294944 | tf_op jit(solution)/shard_map/ppermute | solution.py:48
  80.8 0.5 relay.1
  81.5 2.7 %collective-permute-start.27 = (bf16[16,896]{1,0:T(8,128)(2,1)S(1)}, bf16[16,896]{1,0:T(8,128)(2,1)S(1)}, u32[]{:S(2)}, u32[]{:S(2)}) collective-permute-start(bf16[16,896]{1,0:T(8,128)(2,1)S(1)} %get-tuple-element.70), channel_id=1, source_target_pairs={{0,4},{2,6},{4,0},{6,2},{1,5},{3,7},{5,1},{7,3},{8,12},{10,14},{12... | collective-permute-start | bytes 86024 | tf_op jit(solution)/shard_map/ppermute | solution.py:32
  84.3 2.9 %collective-permute-start.28 = (bf16[16,896]{1,0:T(8,128)(2,1)S(1)}, bf16[16,896]{1,0:T(8,128)(2,1)S(1)}, u32[]{:S(2)}, u32[]{:S(2)}) collective-permute-start(bf16[16,896]{1,0:T(8,128)(2,1)S(1)} %get-tuple-element.71), channel_id=1, source_target_pairs={{0,6},{2,0},{4,2},{6,4},{1,7},{3,1},{5,3},{7,5},{8,14},{10,8},{12,... | collective-permute-start | bytes 86024 | tf_op jit(solution)/shard_map/ppermute | solution.py:32
  87.2 2.8 %attend.3.a_ref = bf16[128,1152]{1,0:T(8,128)(2,1)S(1)} custom-call(s32[1]{0:T(128)} %bitcast.s, s32[64]{0:T(128)S(1)} %copy-done.4, bf16[128,1536]{1,0:T(8,128)(2,1)S(1)} %copy-done.1, bf16[8,1024,128]{2,1,0:T(8,128)(2,1)S(1)} %get-tuple-element.61.refs_1_.refs_2_, bf16[8,1024,128]{2,1,0:T(8,128)(2,1)S(1)} %get-tuple-element.62.refs_2_.refs_3_, ...), custom_call_target="tpu_custom_call" | custom-call | tf_op jit(solution)/shard_map/attend/pallas_call | solution.py:362
  90.0 1.4 %final.1 = (bf16[16,3584]{1,0:T(8,128)(2,1)}, bf16[128,1024]{1,0:T(8,128)(2,1)}) custom-call(s32[1]{0:T(128)} %bitcast.s, bf16[128,1152]{1,0:T(8,128)(2,1)S(1)} %attend.3.a_ref, bf16[128,1152]{1,0:T(8,128)(2,1)S(1)} %collective-permute-done.23.b_ref, bf16[128,1152]{1,0:T(8,128)(2,1)S(1)} %collective-permute-done.25.c_ref, ...), custom_call_target="tpu_custom_call" | custom-call | tf_op jit(solution)/shard_map/final/pallas_call | solution.py:404
  (40 shorter events, 0.5 us)
Async XLA Ops:
  0.6 13.7 %collective-permute-start = (bf16[112,576]{1,0:T(8,128)(2,1)}, bf16[112,576]{1,0:T(8,128)(2,1)S(1)}, u32[]{:S(2)}, u32[]{:S(2)}) collective-permute-start(bf16[112,576]{1,0:T(8,128)(2,1)} %param.19), channel_id=1, source_target_pairs={{2,0},{14,1},{67,2},{79,3},{132,4},{136,5},{197,6},{201,7},{6,8},{... | collective-permute-start | bytes 387080 | tf_op jit(solution)/shard_map/ppermute | solution.py:66
  7.7 0.9 %copy-start.2 = (bf16[128,1024]{1,0:T(8,128)(2,1)S(1)}, bf16[128,1024]{1,0:T(8,128)(2,1)}, u32[]{:S(2)}) copy-start(bf16[128,1024]{1,0:T(8,128)(2,1)} %param.12) | copy-start | bytes 786436
  8.6 0.9 copy-start.3
  14.3 16.3 %copy-start.1 = (bf16[128,1536]{1,0:T(8,128)(2,1)S(1)}, bf16[128,1536]{1,0:T(8,128)(2,1)}, u32[]{:S(2)}) copy-start(bf16[128,1536]{1,0:T(8,128)(2,1)} %refs_0_.1) | copy-start | bytes 1179652
  14.4 20.4 %copy-start.5 = (bf16[3584]{0:T(1024)(128)(2,1)S(1)}, bf16[3584]{0:T(1024)(128)(2,1)}, u32[]{:S(2)}) copy-start(bf16[3584]{0:T(1024)(128)(2,1)} %param.18) | copy-start | bytes 21508
  14.4 4.3 %collective-permute-start.1 = (bf16[4,64,896]{2,1,0:T(8,128)(2,1)S(1)}, bf16[4,64,896]{2,1,0:T(8,128)(2,1)S(1)}, u32[]{:S(2)}, u32[]{:S(2)}) collective-permute-start(bf16[4,64,896]{2,1,0:T(8,128)(2,1)S(1)} %get-tuple-element.39), channel_id=1, source_target_pairs={{0,1},{1,0},{2,3},{3,2},{4,5},{5,4},{6,7},{7,6},{8,9},{9,8},{10,11... | collective-permute-start | bytes 1376264 | tf_op jit(solution)/shard_map/ppermute | solution.py:36
  14.5 9.9 %collective-permute-start.7 = (bf16[1,112,576]{2,1,0:T(8,128)(2,1)S(1)}, bf16[1,112,576]{2,1,0:T(8,128)(2,1)S(1)}, u32[]{:S(2)}, u32[]{:S(2)}) collective-permute-start(bf16[1,112,576]{2,1,0:T(8,128)(2,1)S(1)} %bitcast.4), channel_id=1, source_target_pairs={{0,48},{16,32},{32,16},{48,0},{1,49},{17,33},{33,17},{49,1},{2,50}... | collective-permute-start | bytes 387080 | tf_op jit(solution)/shard_map/ppermute | solution.py:36
  17.3 8.2 %collective-permute-start.6 = (bf16[1,112,576]{2,1,0:T(8,128)(2,1)S(1)}, bf16[1,112,576]{2,1,0:T(8,128)(2,1)S(1)}, u32[]{:S(2)}, u32[]{:S(2)}) collective-permute-start(bf16[1,112,576]{2,1,0:T(8,128)(2,1)S(1)} %bitcast.5), channel_id=1, source_target_pairs={{0,32},{16,48},{32,0},{48,16},{1,33},{17,49},{33,1},{49,17},{2,34}... | collective-permute-start | bytes 387080 | tf_op jit(solution)/shard_map/ppermute | solution.py:36
  18.1 7.4 %collective-permute-start.5 = (bf16[1,112,576]{2,1,0:T(8,128)(2,1)S(1)}, bf16[1,112,576]{2,1,0:T(8,128)(2,1)S(1)}, u32[]{:S(2)}, u32[]{:S(2)}) collective-permute-start(bf16[1,112,576]{2,1,0:T(8,128)(2,1)S(1)} %bitcast.6), channel_id=1, source_target_pairs={{0,16},{16,0},{32,48},{48,32},{1,17},{17,1},{33,49},{49,33},{2,18}... | collective-permute-start | bytes 387080 | tf_op jit(solution)/shard_map/ppermute | solution.py:36
  18.7 8.0 %collective-permute-start.2 = (bf16[64,896]{1,0:T(8,128)(2,1)S(1)}, bf16[64,896]{1,0:T(8,128)(2,1)S(1)}, u32[]{:S(2)}, u32[]{:S(2)}) collective-permute-start(bf16[64,896]{1,0:T(8,128)(2,1)S(1)} %get-tuple-element.40), channel_id=1, source_target_pairs={{0,2},{2,4},{4,6},{6,0},{1,3},{3,5},{5,7},{7,1},{8,10},{10,12},{12... | collective-permute-start | bytes 344072 | tf_op jit(solution)/shard_map/ppermute | solution.py:32
  18.8 11.5 %collective-permute-start.3 = (bf16[64,896]{1,0:T(8,128)(2,1)S(1)}, bf16[64,896]{1,0:T(8,128)(2,1)S(1)}, u32[]{:S(2)}, u32[]{:S(2)}) collective-permute-start(bf16[64,896]{1,0:T(8,128)(2,1)S(1)} %get-tuple-element.41), channel_id=1, source_target_pairs={{0,4},{2,6},{4,0},{6,2},{1,5},{3,7},{5,1},{7,3},{8,12},{10,14},{12... | collective-permute-start | bytes 344072 | tf_op jit(solution)/shard_map/ppermute | solution.py:32
  24.4 6.0 %collective-permute-start.4 = (bf16[64,896]{1,0:T(8,128)(2,1)S(1)}, bf16[64,896]{1,0:T(8,128)(2,1)S(1)}, u32[]{:S(2)}, u32[]{:S(2)}) collective-permute-start(bf16[64,896]{1,0:T(8,128)(2,1)S(1)} %get-tuple-element.42), channel_id=1, source_target_pairs={{0,6},{2,0},{4,2},{6,4},{1,7},{3,1},{5,3},{7,5},{8,14},{10,8},{12,... | collective-permute-start | bytes 344072 | tf_op jit(solution)/shard_map/ppermute | solution.py:32
  30.5 4.3 %collective-permute-start.8 = (bf16[4,112,576]{2,1,0:T(8,128)(2,1)S(1)}, bf16[4,112,576]{2,1,0:T(8,128)(2,1)S(1)}, u32[]{:S(2)}, u32[]{:S(2)}) collective-permute-start(bf16[4,112,576]{2,1,0:T(8,128)(2,1)S(1)} %pack.2.own_ref), channel_id=1, source_target_pairs={{0,1},{1,0},{2,3},{3,2},{4,5},{5,4},{6,7},{7,6},{8,9},{9,8},{10,11... | collective-permute-start | bytes 1548296 | tf_op jit(solution)/shard_map/ppermute | solution.py:36
  30.6 18.5 %collective-permute-start.13 = (bf16[128,1536]{1,0:T(8,128)(2,1)S(1)}, bf16[128,1536]{1,0:T(8,128)(2,1)S(1)}, u32[]{:S(2)}, u32[]{:S(2)}) collective-permute-start(bf16[128,1536]{1,0:T(8,128)(2,1)S(1)} %copy-done.1), channel_id=1, source_target_pairs={{0,32},{16,48},{32,0},{48,16},{1,33},{17,49},{33,1},{49,17},{2,34}... | collective-permute-start | bytes 1179656 | tf_op jit(solution)/shard_map/ppermute | solution.py:32
  33.6 23.5 %collective-permute-start.21 = (bf16[128,1536]{1,0:T(8,128)(2,1)S(1)}, bf16[128,1536]{1,0:T(8,128)(2,1)S(1)}, u32[]{:S(2)}, u32[]{:S(2)}) collective-permute-start(bf16[128,1536]{1,0:T(8,128)(2,1)S(1)} %copy-done.1), channel_id=1, source_target_pairs={{0,16},{1,49},{16,32},{17,1},{32,48},{33,17},{48,0},{49,33},{2,18}... | collective-permute-start | bytes 1179656 | tf_op jit(solution)/shard_map/ppermute | solution.py:48
  34.8 3.6 %copy-start.6 = (bf16[512]{0:T(512)(128)(2,1)S(1)}, bf16[512]{0:T(512)(128)(2,1)}, u32[]{:S(2)}) copy-start(bf16[512]{0:T(512)(128)(2,1)} %param.20) | copy-start | bytes 3076
  34.8 3.6 %copy-start.4 = (s32[64]{0:T(128)S(1)}, s32[64]{0:T(128)}, u32[]{:S(2)}) copy-start(s32[64]{0:T(128)} %seg.8) | copy-start | bytes 772
  35.0 31.3 %copy-start = (bf16[512,2048]{1,0:T(8,128)(2,1)S(1)}, bf16[512,2048]{1,0:T(8,128)(2,1)}, u32[]{:S(2)}) copy-start(bf16[512,2048]{1,0:T(8,128)(2,1)} %refs_8_.1) | copy-start | bytes 6291460
  35.3 4.6 %collective-permute-start.11 = (bf16[64,640]{1,0:T(8,128)(2,1)S(1)}, bf16[64,640]{1,0:T(8,128)(2,1)S(1)}, u32[]{:S(2)}, u32[]{:S(2)}) collective-permute-start(bf16[64,640]{1,0:T(8,128)(2,1)S(1)} %get-tuple-element.44.p0), channel_id=1, source_target_pairs={{0,6},{2,0},{4,2},{6,4},{1,7},{3,1},{5,3},{7,5},{8,14},{10,8},{12,... | collective-permute-start | bytes 245768 | tf_op jit(solution)/shard_map/ppermute | solution.py:32
  37.1 9.3 %collective-permute-start.10 = (bf16[64,640]{1,0:T(8,128)(2,1)S(1)}, bf16[64,640]{1,0:T(8,128)(2,1)S(1)}, u32[]{:S(2)}, u32[]{:S(2)}) collective-permute-start(bf16[64,640]{1,0:T(8,128)(2,1)S(1)} %get-tuple-element.44.p0), channel_id=1, source_target_pairs={{0,4},{2,6},{4,0},{6,2},{1,5},{3,7},{5,1},{7,3},{8,12},{10,14},{12... | collective-permute-start | bytes 245768 | tf_op jit(solution)/shard_map/ppermute | solution.py:32
  38.3 8.0 %collective-permute-start.9 = (bf16[64,640]{1,0:T(8,128)(2,1)S(1)}, bf16[64,640]{1,0:T(8,128)(2,1)S(1)}, u32[]{:S(2)}, u32[]{:S(2)}) collective-permute-start(bf16[64,640]{1,0:T(8,128)(2,1)S(1)} %get-tuple-element.44.p0), channel_id=1, source_target_pairs={{0,2},{2,4},{4,6},{6,0},{1,3},{3,5},{5,7},{7,1},{8,10},{10,12},{12... | collective-permute-start | bytes 245768 | tf_op jit(solution)/shard_map/ppermute | solution.py:32
  46.7 6.6 %collective-permute-start.12 = (bf16[64,640]{1,0:T(8,128)(2,1)S(1)}, bf16[64,640]{1,0:T(8,128)(2,1)S(1)}, u32[]{:S(2)}, u32[]{:S(2)}) collective-permute-start(bf16[64,640]{1,0:T(8,128)(2,1)S(1)} %kv_rows.1.refs_0_), channel_id=1, source_target_pairs={{0,12},{2,14},{4,8},{6,10},{8,4},{10,6},{12,0},{14,2},{1,13},{3,15... | collective-permute-start | bytes 245768 | tf_op jit(solution)/shard_map/ppermute | solution.py:71
  49.1 15.8 %collective-permute-start.22 = (bf16[128,1536]{1,0:T(8,128)(2,1)S(1)}, bf16[128,1536]{1,0:T(8,128)(2,1)S(1)}, u32[]{:S(2)}, u32[]{:S(2)}) collective-permute-start(bf16[128,1536]{1,0:T(8,128)(2,1)S(1)} %copy-done.1), channel_id=1, source_target_pairs={{0,48},{1,17},{16,0},{17,33},{32,16},{33,49},{48,32},{49,1},{2,50}... | collective-permute-start | bytes 1179656 | tf_op jit(solution)/shard_map/ppermute | solution.py:48
  53.3 7.9 %collective-permute-start.16 = (bf16[128,640]{1,0:T(8,128)(2,1)S(1)}, bf16[128,640]{1,0:T(8,128)(2,1)S(1)}, u32[]{:S(2)}, u32[]{:S(2)}) collective-permute-start(bf16[128,640]{1,0:T(8,128)(2,1)S(1)} %pack.3.refs_0_), channel_id=1, source_target_pairs={{0,64},{64,128},{128,192},{192,0},{1,65},{65,129},{129,193},{193,1... | collective-permute-start | bytes 491528 | tf_op jit(solution)/shard_map/ppermute | solution.py:32
  55.6 7.7 %collective-permute-start.15 = (bf16[128,640]{1,0:T(8,128)(2,1)S(1)}, bf16[128,640]{1,0:T(8,128)(2,1)S(1)}, u32[]{:S(2)}, u32[]{:S(2)}) collective-permute-start(bf16[128,640]{1,0:T(8,128)(2,1)S(1)} %pack.3.refs_0_), channel_id=1, source_target_pairs={{0,128},{64,192},{128,0},{192,64},{1,129},{65,193},{129,1},{193,65... | collective-permute-start | bytes 491528 | tf_op jit(solution)/shard_map/ppermute | solution.py:32
  55.8 9.1 %collective-permute-start.14 = (bf16[128,640]{1,0:T(8,128)(2,1)S(1)}, bf16[128,640]{1,0:T(8,128)(2,1)S(1)}, u32[]{:S(2)}, u32[]{:S(2)}) collective-permute-start(bf16[128,640]{1,0:T(8,128)(2,1)S(1)} %pack.3.refs_0_), channel_id=1, source_target_pairs={{0,192},{64,0},{128,64},{192,128},{1,193},{65,1},{129,65},{193,129... | collective-permute-start | bytes 491528 | tf_op jit(solution)/shard_map/ppermute | solution.py:32
  57.1 7.8 %collective-permute-start.17 = (bf16[128,640]{1,0:T(8,128)(2,1)S(1)}, bf16[128,640]{1,0:T(8,128)(2,1)S(1)}, u32[]{:S(2)}, u32[]{:S(2)}) collective-permute-start(bf16[128,640]{1,0:T(8,128)(2,1)S(1)} %pack.3.refs_0_), channel_id=1, source_target_pairs={{0,1},{1,0},{2,3},{3,2},{4,5},{5,4},{6,7},{7,6},{8,9},{9,8},{10,11... | collective-permute-start | bytes 491528 | tf_op jit(solution)/shard_map/ppermute | solution.py:36
  61.3 3.6 %collective-permute-start.20 = (bf16[128,640]{1,0:T(8,128)(2,1)S(1)}, bf16[128,640]{1,0:T(8,128)(2,1)S(1)}, u32[]{:S(2)}, u32[]{:S(2)}) collective-permute-start(bf16[128,640]{1,0:T(8,128)(2,1)S(1)} %collective-permute-done.16.refs_3_), channel_id=1, source_target_pairs={{0,1},{1,0},{2,3},{3,2},{4,5},{5,4},{6,7},{7,6},{8,9},{9,8},{10,11... | collective-permute-start | bytes 491528 | tf_op jit(solution)/shard_map/ppermute | solution.py:36
  63.3 1.6 %collective-permute-start.19 = (bf16[128,640]{1,0:T(8,128)(2,1)S(1)}, bf16[128,640]{1,0:T(8,128)(2,1)S(1)}, u32[]{:S(2)}, u32[]{:S(2)}) collective-permute-start(bf16[128,640]{1,0:T(8,128)(2,1)S(1)} %collective-permute-done.15.refs_2_), channel_id=1, source_target_pairs={{0,1},{1,0},{2,3},{3,2},{4,5},{5,4},{6,7},{7,6},{8,9},{9,8},{10,11... | collective-permute-start | bytes 491528 | tf_op jit(solution)/shard_map/ppermute | solution.py:36
  64.8 1.4 %collective-permute-start.18 = (bf16[128,640]{1,0:T(8,128)(2,1)S(1)}, bf16[128,640]{1,0:T(8,128)(2,1)S(1)}, u32[]{:S(2)}, u32[]{:S(2)}) collective-permute-start(bf16[128,640]{1,0:T(8,128)(2,1)S(1)} %collective-permute-done.14.refs_1_), channel_id=1, source_target_pairs={{0,1},{1,0},{2,3},{3,2},{4,5},{5,4},{6,7},{7,6},{8,9},{9,8},{10,11... | collective-permute-start | bytes 491528 | tf_op jit(solution)/shard_map/ppermute | solution.py:36
  72.1 8.8 %collective-permute-start.24 = (bf16[128,1152]{1,0:T(8,128)(2,1)S(1)}, bf16[128,1152]{1,0:T(8,128)(2,1)S(1)}, u32[]{:S(2)}, u32[]{:S(2)}) collective-permute-start(bf16[128,1152]{1,0:T(8,128)(2,1)S(1)} %attend.5), channel_id=1, source_target_pairs={{0,16},{1,49},{16,32},{17,1},{32,48},{33,17},{48,0},{49,33},{2,18}... | collective-permute-start | bytes 884744 | tf_op jit(solution)/shard_map/ppermute | solution.py:48
  76.8 13.2 %collective-permute-start.23 = (bf16[128,1152]{1,0:T(8,128)(2,1)S(1)}, bf16[128,1152]{1,0:T(8,128)(2,1)S(1)}, u32[]{:S(2)}, u32[]{:S(2)}) collective-permute-start(bf16[128,1152]{1,0:T(8,128)(2,1)S(1)} %get-tuple-element.66), channel_id=1, source_target_pairs={{0,48},{1,17},{16,0},{17,33},{32,16},{33,49},{48,32},{49,1},{2,50}... | collective-permute-start | bytes 884744 | tf_op jit(solution)/shard_map/ppermute | solution.py:48
  81.3 8.7 %collective-permute-start.25 = (bf16[128,1152]{1,0:T(8,128)(2,1)S(1)}, bf16[128,1152]{1,0:T(8,128)(2,1)S(1)}, u32[]{:S(2)}, u32[]{:S(2)}) collective-permute-start(bf16[128,1152]{1,0:T(8,128)(2,1)S(1)} %relay.1), channel_id=1, source_target_pairs={{0,16},{1,49},{16,32},{17,1},{32,48},{33,17},{48,0},{49,33},{2,18}... | collective-permute-start | bytes 884744 | tf_op jit(solution)/shard_map/ppermute | solution.py:48
  81.4 8.6 %collective-permute-start.26 = (bf16[16,896]{1,0:T(8,128)(2,1)S(1)}, bf16[16,896]{1,0:T(8,128)(2,1)S(1)}, u32[]{:S(2)}, u32[]{:S(2)}) collective-permute-start(bf16[16,896]{1,0:T(8,128)(2,1)S(1)} %get-tuple-element.69), channel_id=1, source_target_pairs={{0,2},{2,4},{4,6},{6,0},{1,3},{3,5},{5,7},{7,1},{8,10},{10,12},{12... | collective-permute-start | bytes 86024 | tf_op jit(solution)/shard_map/ppermute | solution.py:32
  81.5 8.5 %collective-permute-start.27 = (bf16[16,896]{1,0:T(8,128)(2,1)S(1)}, bf16[16,896]{1,0:T(8,128)(2,1)S(1)}, u32[]{:S(2)}, u32[]{:S(2)}) collective-permute-start(bf16[16,896]{1,0:T(8,128)(2,1)S(1)} %get-tuple-element.70), channel_id=1, source_target_pairs={{0,4},{2,6},{4,0},{6,2},{1,5},{3,7},{5,1},{7,3},{8,12},{10,14},{12... | collective-permute-start | bytes 86024 | tf_op jit(solution)/shard_map/ppermute | solution.py:32
  84.3 5.7 %collective-permute-start.28 = (bf16[16,896]{1,0:T(8,128)(2,1)S(1)}, bf16[16,896]{1,0:T(8,128)(2,1)S(1)}, u32[]{:S(2)}, u32[]{:S(2)}) collective-permute-start(bf16[16,896]{1,0:T(8,128)(2,1)S(1)} %get-tuple-element.71), channel_id=1, source_target_pairs={{0,6},{2,0},{4,2},{6,4},{1,7},{3,1},{5,3},{7,5},{8,14},{10,8},{12,... | collective-permute-start | bytes 86024 | tf_op jit(solution)/shard_map/ppermute | solution.py:32

commit v6 on v5

--- a/solution.py
+++ b/solution.py
@@ -431,8 +431,9 @@
     )
     block, send = tie(block, send)
     got = swap(send, "core")
-    blocks = [block] + [swap(block, "x", k, 4) for k in (1, 2, 3)]
     sums = pair_sum(keep, got, 3)
+    late = pack([block], sums[:1])
+    blocks = [block, swap(block, "x", 1, 4), swap(late, "x", 2, 4), swap(block, "x", 3, 4)]
     r2, r1, r3 = (shift(value, "zl", k) for value, k in zip(sums, ORDER))
     four = pack(blocks, (r1, r2, r3))
     weight = assemble(scalars, four, swap(four, "core"))

time: 91.5 us -> 91 us (level); the launches traced: 91.4 us -> 89.5 us
  waiting for transfers between devices: 30.7 us -> 27.1 us
  starting transfers between devices: 37.8 us -> 39.4 us
    ppermute x9, waiting for transfers between devices: 5.37 us -> 1.98 us  [swap(): return lax.ppermute(value, axis, [(i, i ^ bit) for i in range(size)])]
    ppermute x13, waiting for transfers between devices: 19.9 us -> 21.6 us  [shift(): return lax.ppermute(value, axis, [(i, (i + k) % 4) for i in range(4)])]
    ppermute x1, waiting for transfers between devices: 3.53 us -> 2.18 us  [cross(): return lax.ppermute(value, ('zh', 'zl'), perm)]
    ppermute x5, starting transfers between devices: 5.48 us -> 6.74 us  [turn(): return lax.ppermute(value, ('x', 'core'), perm)]
    ppermute x13, starting transfers between devices: 18.4 us -> 17.3 us  [shift(): return lax.ppermute(value, axis, [(i, (i + k) % 4) for i in range(4)])]
  transfers between devices with their start and end apart: 29 -> 29, of which waited for: 14 -> 12; matrix products, arithmetic and copies ran while one was open for 0% -> 0% of each run, Pallas kernels for 14% -> 14%
where the time goes in v6:
time: 91 us; the launch traced here: 89.5 us
  starting transfers between devices  39.4 us (43%)
  waiting for transfers between devices  27.1 us (30%)
  Pallas kernels  20.2 us (22%)
  local copies, waits for them, and re-layouts  1.89 us (2%)
    ppermute x13, waiting for transfers between devices, shift(): return lax.ppermute(value, axis, [(i, (i + k) % 4) for i in range(4)])  21.6 us
    ppermute x13, starting transfers between devices, shift(): return lax.ppermute(value, axis, [(i, (i + k) % 4) for i in range(4)])  17.3 us
    pallas_call x3, Pallas kernels, attend(): local(kernel, outs, 32, 'attend', 2, len(chunks) + 3)  8.91 us
    ppermute x1, starting transfers between devices, near_block(): return lax.ppermute(value, AXES, perm)  7.06 us
    ppermute x5, starting transfers between devices, turn(): return lax.ppermute(value, ('x', 'core'), perm)  6.74 us
    ppermute x9, starting transfers between devices, swap(): return lax.ppermute(value, axis, [(i, i ^ bit) for i in range(size)])  5.11 us
    pallas_call x1, Pallas kernels, project(): pl.pallas_call(project_kernel, in_specs=[pl.BlockSpec(memory_space=pltpu....  4.79 us
    ppermute x1, starting transfers between devices, cross(): return lax.ppermute(value, ('zh', 'zl'), perm)  3.21 us
  transfers between devices with their start and end apart: 29, of which 12 were waited for; matrix products, arithmetic and copies ran while one was open for 0% of the time, Pallas kernels for 14%

profile of v6, /device:TPU:24, one launch (start us, length us, event | category | flops | bytes accessed | tf_op | source)
XLA Modules:
  0.0 89.5 jit_solution(12542098612152196344)
XLA Ops:
  0.6 7.1 %collective-permute-start = (bf16[112,576]{1,0:T(8,128)(2,1)}, bf16[112,576]{1,0:T(8,128)(2,1)S(1)}, u32[]{:S(2)}, u32[]{:S(2)}) collective-permute-start(bf16[112,576]{1,0:T(8,128)(2,1)} %param.19), channel_id=1, source_target_pairs={{2,0},{14,1},{67,2},{79,3},{132,4},{136,5},{197,6},{201,7},{6,8},{... | collective-permute-start | bytes 387080 | tf_op jit(solution)/shard_map/ppermute | solution.py:66
  7.7 0.9 %copy-done.2 = bf16[128,1024]{1,0:T(8,128)(2,1)S(1)} copy-done((bf16[128,1024]{1,0:T(8,128)(2,1)S(1)}, bf16[128,1024]{1,0:T(8,128)(2,1)}, u32[]{:S(2)}) %copy-start.2) | copy-done | bytes 262168
  8.6 0.9 %copy-done.3 = bf16[16,3584]{1,0:T(8,128)(2,1)S(1)} copy-done((bf16[16,3584]{1,0:T(8,128)(2,1)S(1)}, bf16[16,3584]{1,0:T(8,128)(2,1)}, u32[]{:S(2)}) %copy-start.3) | copy-done | bytes 114712
  9.5 4.8 %project.1 = (bf16[4,64,896]{2,1,0:T(8,128)(2,1)S(1)}, bf16[4,64,896]{2,1,0:T(8,128)(2,1)S(1)}) custom-call(s32[1]{0:T(128)} %bitcast.s, bf16[4,2,16,1024]{3,2,1,0:T(8,128)(2,1)S(1)} %bitcast.7, bf16[1024,256]{1,0:T(8,128)(2,1)} %ad_hbm.1, bf16[1024,3584]{1,0:T(8,128)(2,1)} %w_hbm.1, bf16[256,3584]{1,0:T(8,128)(2,1)} %au_hbm.1, bf16[16,3584]{1,0:T(8,128)(2,1)S(1)} %copy-done.3), custom_call_target="tpu_custom_call" | custom-call | tf_op jit(solution)/shard_map/project/pallas_call | solution.py:123
  14.4 0.1 collective-permute-start.1
  14.5 2.8 %collective-permute-start.7 = (bf16[1,112,576]{2,1,0:T(8,128)(2,1)S(1)}, bf16[1,112,576]{2,1,0:T(8,128)(2,1)S(1)}, u32[]{:S(2)}, u32[]{:S(2)}) collective-permute-start(bf16[1,112,576]{2,1,0:T(8,128)(2,1)S(1)} %bitcast.3), channel_id=1, source_target_pairs={{0,48},{16,32},{32,16},{48,0},{1,49},{17,33},{33,17},{49,1},{2,50}... | collective-permute-start | bytes 387080 | tf_op jit(solution)/shard_map/ppermute | solution.py:36
  17.3 0.2 collective-permute-start.5
  17.6 0.1 pair_sum.1
  17.7 1.8 %collective-permute-start.6 = (bf16[1,112,576]{2,1,0:T(8,128)(2,1)S(1)}, bf16[1,112,576]{2,1,0:T(8,128)(2,1)S(1)}, u32[]{:S(2)}, u32[]{:S(2)}) collective-permute-start(bf16[1,112,576]{2,1,0:T(8,128)(2,1)S(1)} %pack.3), channel_id=1, source_target_pairs={{0,32},{16,48},{32,0},{48,16},{1,33},{17,49},{33,1},{49,17},{2,34}... | collective-permute-start | bytes 387080 | tf_op jit(solution)/shard_map/ppermute | solution.py:36
  19.5 3.8 %collective-permute-start.4 = (bf16[64,896]{1,0:T(8,128)(2,1)S(1)}, bf16[64,896]{1,0:T(8,128)(2,1)S(1)}, u32[]{:S(2)}, u32[]{:S(2)}) collective-permute-start(bf16[64,896]{1,0:T(8,128)(2,1)S(1)} %get-tuple-element.42), channel_id=1, source_target_pairs={{0,6},{2,0},{4,2},{6,4},{1,7},{3,1},{5,3},{7,5},{8,14},{10,8},{12,... | collective-permute-start | bytes 344072 | tf_op jit(solution)/shard_map/ppermute | solution.py:32
  23.3 0.6 collective-permute-done.5.refs_1_
  23.9 3.5 %collective-permute-done.2.refs_4_.r1 = bf16[64,896]{1,0:T(8,128)(2,1)S(1)} collective-permute-done((bf16[64,896]{1,0:T(8,128)(2,1)S(1)}, bf16[64,896]{1,0:T(8,128)(2,1)S(1)}, u32[]{:S(2)}, u32[]{:S(2)}) %collective-permute-start.2) | collective-permute-done | bytes 114720 | tf_op jit(solution)/shard_map/ppermute | solution.py:32
  27.4 0.4 collective-permute-done.4.refs_6_.r3
  27.8 3.9 %collective-permute-done.3.refs_5_.r2 = bf16[64,896]{1,0:T(8,128)(2,1)S(1)} collective-permute-done((bf16[64,896]{1,0:T(8,128)(2,1)S(1)}, bf16[64,896]{1,0:T(8,128)(2,1)S(1)}, u32[]{:S(2)}, u32[]{:S(2)}) %collective-permute-start.3) | collective-permute-done | bytes 114720 | tf_op jit(solution)/shard_map/ppermute | solution.py:32
  31.8 0.1 collective-permute-start.8
  31.9 1.8 %collective-permute-start.13 = (bf16[128,1536]{1,0:T(8,128)(2,1)S(1)}, bf16[128,1536]{1,0:T(8,128)(2,1)S(1)}, u32[]{:S(2)}, u32[]{:S(2)}) collective-permute-start(bf16[128,1536]{1,0:T(8,128)(2,1)S(1)} %copy-done.1), channel_id=1, source_target_pairs={{0,32},{16,48},{32,0},{48,16},{1,33},{17,49},{33,1},{49,17},{2,34}... | collective-permute-start | bytes 1179656 | tf_op jit(solution)/shard_map/ppermute | solution.py:32
  33.6 1.8 %collective-permute-start.21 = (bf16[128,1536]{1,0:T(8,128)(2,1)S(1)}, bf16[128,1536]{1,0:T(8,128)(2,1)S(1)}, u32[]{:S(2)}, u32[]{:S(2)}) collective-permute-start(bf16[128,1536]{1,0:T(8,128)(2,1)S(1)} %copy-done.1), channel_id=1, source_target_pairs={{0,16},{1,49},{16,32},{17,1},{32,48},{33,17},{48,0},{49,33},{2,18}... | collective-permute-start | bytes 1179656 | tf_op jit(solution)/shard_map/ppermute | solution.py:48
  35.5 0.1 assemble.1.w_ref
  35.7 0.3 latent_part.1
  36.0 2.0 %collective-permute-start.11 = (bf16[64,640]{1,0:T(8,128)(2,1)S(1)}, bf16[64,640]{1,0:T(8,128)(2,1)S(1)}, u32[]{:S(2)}, u32[]{:S(2)}) collective-permute-start(bf16[64,640]{1,0:T(8,128)(2,1)S(1)} %get-tuple-element.44.p0), channel_id=1, source_target_pairs={{0,6},{2,0},{4,2},{6,4},{1,7},{3,1},{5,3},{7,5},{8,14},{10,8},{12,... | collective-permute-start | bytes 245768 | tf_op jit(solution)/shard_map/ppermute | solution.py:32
  38.0 0.7 collective-permute-start.9
  38.6 0.7 tables.1
  39.3 1.5 %collective-permute-done.11.p3 = bf16[64,640]{1,0:T(8,128)(2,1)S(1)} collective-permute-done((bf16[64,640]{1,0:T(8,128)(2,1)S(1)}, bf16[64,640]{1,0:T(8,128)(2,1)S(1)}, u32[]{:S(2)}, u32[]{:S(2)}) %collective-permute-start.11) | collective-permute-done | bytes 81952 | tf_op jit(solution)/shard_map/ppermute | solution.py:32
  40.8 4.8 %collective-permute-done.10.p2 = bf16[64,640]{1,0:T(8,128)(2,1)S(1)} collective-permute-done((bf16[64,640]{1,0:T(8,128)(2,1)S(1)}, bf16[64,640]{1,0:T(8,128)(2,1)S(1)}, u32[]{:S(2)}, u32[]{:S(2)}) %collective-permute-start.10) | collective-permute-done | bytes 81952 | tf_op jit(solution)/shard_map/ppermute | solution.py:32
  45.6 0.3 kv_rows.1.refs_0_
  45.9 3.2 %collective-permute-start.12 = (bf16[64,640]{1,0:T(8,128)(2,1)S(1)}, bf16[64,640]{1,0:T(8,128)(2,1)S(1)}, u32[]{:S(2)}, u32[]{:S(2)}) collective-permute-start(bf16[64,640]{1,0:T(8,128)(2,1)S(1)} %kv_rows.1.refs_0_), channel_id=1, source_target_pairs={{0,12},{2,14},{4,8},{6,10},{8,4},{10,6},{12,0},{14,2},{1,13},{3,15... | collective-permute-start | bytes 245768 | tf_op jit(solution)/shard_map/ppermute | solution.py:71
  49.1 1.2 %collective-permute-start.22 = (bf16[128,1536]{1,0:T(8,128)(2,1)S(1)}, bf16[128,1536]{1,0:T(8,128)(2,1)S(1)}, u32[]{:S(2)}, u32[]{:S(2)}) collective-permute-start(bf16[128,1536]{1,0:T(8,128)(2,1)S(1)} %copy-done.1), channel_id=1, source_target_pairs={{0,48},{1,17},{16,0},{17,33},{32,16},{33,49},{48,32},{49,1},{2,50}... | collective-permute-start | bytes 1179656 | tf_op jit(solution)/shard_map/ppermute | solution.py:48
  50.4 2.2 %collective-permute-done.12.refs_1_ = bf16[64,640]{1,0:T(8,128)(2,1)S(1)} collective-permute-done((bf16[64,640]{1,0:T(8,128)(2,1)S(1)}, bf16[64,640]{1,0:T(8,128)(2,1)S(1)}, u32[]{:S(2)}, u32[]{:S(2)}) %collective-permute-start.12) | collective-permute-done | bytes 81952 | tf_op jit(solution)/shard_map/ppermute | solution.py:71
  52.6 2.3 %collective-permute-start.16 = (bf16[128,640]{1,0:T(8,128)(2,1)S(1)}, bf16[128,640]{1,0:T(8,128)(2,1)S(1)}, u32[]{:S(2)}, u32[]{:S(2)}) collective-permute-start(bf16[128,640]{1,0:T(8,128)(2,1)S(1)} %pack.5.refs_0_), channel_id=1, source_target_pairs={{0,64},{64,128},{128,192},{192,0},{1,65},{65,129},{129,193},{193,1... | collective-permute-start | bytes 491528 | tf_op jit(solution)/shard_map/ppermute | solution.py:32
  54.9 1.1 %collective-permute-start.15 = (bf16[128,640]{1,0:T(8,128)(2,1)S(1)}, bf16[128,640]{1,0:T(8,128)(2,1)S(1)}, u32[]{:S(2)}, u32[]{:S(2)}) collective-permute-start(bf16[128,640]{1,0:T(8,128)(2,1)S(1)} %pack.5.refs_0_), channel_id=1, source_target_pairs={{0,128},{64,192},{128,0},{192,64},{1,129},{65,193},{129,1},{193,65... | collective-permute-start | bytes 491528 | tf_op jit(solution)/shard_map/ppermute | solution.py:32
  56.0 0.4 collective-permute-start.14
  56.4 3.9 %collective-permute-done.16.refs_3_ = bf16[128,640]{1,0:T(8,128)(2,1)S(1)} collective-permute-done((bf16[128,640]{1,0:T(8,128)(2,1)S(1)}, bf16[128,640]{1,0:T(8,128)(2,1)S(1)}, u32[]{:S(2)}, u32[]{:S(2)}) %collective-permute-start.16) | collective-permute-done | bytes 163872 | tf_op jit(solution)/shard_map/ppermute | solution.py:32
  60.3 2.0 %collective-permute-done.15.refs_2_ = bf16[128,640]{1,0:T(8,128)(2,1)S(1)} collective-permute-done((bf16[128,640]{1,0:T(8,128)(2,1)S(1)}, bf16[128,640]{1,0:T(8,128)(2,1)S(1)}, u32[]{:S(2)}, u32[]{:S(2)}) %collective-permute-start.15) | collective-permute-done | bytes 163872 | tf_op jit(solution)/shard_map/ppermute | solution.py:32
  62.3 1.6 %collective-permute-done.14.refs_1_ = bf16[128,640]{1,0:T(8,128)(2,1)S(1)} collective-permute-done((bf16[128,640]{1,0:T(8,128)(2,1)S(1)}, bf16[128,640]{1,0:T(8,128)(2,1)S(1)}, u32[]{:S(2)}, u32[]{:S(2)}) %collective-permute-start.14) | collective-permute-done | bytes 163872 | tf_op jit(solution)/shard_map/ppermute | solution.py:32
  64.0 1.4 %collective-permute-done.18.refs_5_ = bf16[128,640]{1,0:T(8,128)(2,1)S(1)} collective-permute-done((bf16[128,640]{1,0:T(8,128)(2,1)S(1)}, bf16[128,640]{1,0:T(8,128)(2,1)S(1)}, u32[]{:S(2)}, u32[]{:S(2)}) %collective-permute-start.18) | collective-permute-done | bytes 163872 | tf_op jit(solution)/shard_map/ppermute | solution.py:36
  65.3 3.0 %lift.1 = (bf16[8,1024,128]{2,1,0:T(8,128)(2,1)S(1)}, bf16[8,1024,128]{2,1,0:T(8,128)(2,1)S(1)}, bf16[1024,128]{1,0:T(8,128)(2,1)S(1)}) custom-call(s32[1]{0:T(128)} %bitcast.s, s32[64]{0:T(128)S(1)} %copy-done.4, bf16[128,640]{1,0:T(8,128)(2,1)S(1)} %pack.5.refs_0_, bf16[128,640]{1,0:T(8,128)(2,1)S(1)} %collective-permute-done.14.refs_1_, ...), custom_call_target="tpu_custom_call" | custom-call | tf_op jit(solution)/shard_map/lift/pallas_call | solution.py:278
  68.4 2.8 %attend.5 = bf16[128,1152]{1,0:T(8,128)(2,1)S(1)} custom-call(s32[1]{0:T(128)} %bitcast.s, s32[64]{0:T(128)S(1)} %copy-done.4, bf16[128,1536]{1,0:T(8,128)(2,1)S(1)} %collective-permute-done.13.refs_2_.refs_0_, bf16[8,1024,128]{2,1,0:T(8,128)(2,1)S(1)} %get-tuple-element.61.refs_1_.refs_2_, bf16[8,1024,128]{2,1,0:T(8,128)(2,1)S(1)} %get-tuple-element.62.refs_2_.refs_3_, ...), custom_call_target="tpu_custom_call" | custom-call | tf_op jit(solution)/shard_map/attend/pallas_call | solution.py:362
  71.2 1.3 %collective-permute-start.24 = (bf16[128,1152]{1,0:T(8,128)(2,1)S(1)}, bf16[128,1152]{1,0:T(8,128)(2,1)S(1)}, u32[]{:S(2)}, u32[]{:S(2)}) collective-permute-start(bf16[128,1152]{1,0:T(8,128)(2,1)S(1)} %attend.5), channel_id=1, source_target_pairs={{0,16},{1,49},{16,32},{17,1},{32,48},{33,17},{48,0},{49,33},{2,18}... | collective-permute-start | bytes 884744 | tf_op jit(solution)/shard_map/ppermute | solution.py:48
  72.5 3.3 %attend.4 = (bf16[128,1152]{1,0:T(8,128)(2,1)S(1)}, bf16[128,1152]{1,0:T(8,128)(2,1)S(1)}) custom-call(s32[1]{0:T(128)} %bitcast.s, s32[64]{0:T(128)S(1)} %copy-done.4, bf16[128,1536]{1,0:T(8,128)(2,1)S(1)} %collective-permute-done.21.refs_0_, bf16[128,1536]{1,0:T(8,128)(2,1)S(1)} %collective-permute-done.22.refs_1_, ...), custom_call_target="tpu_custom_call" | custom-call | tf_op jit(solution)/shard_map/attend/pallas_call | solution.py:362
  75.8 2.3 %collective-permute-start.23 = (bf16[128,1152]{1,0:T(8,128)(2,1)S(1)}, bf16[128,1152]{1,0:T(8,128)(2,1)S(1)}, u32[]{:S(2)}, u32[]{:S(2)}) collective-permute-start(bf16[128,1152]{1,0:T(8,128)(2,1)S(1)} %get-tuple-element.66), channel_id=1, source_target_pairs={{0,48},{1,17},{16,0},{17,33},{32,16},{33,49},{48,32},{49,1},{2,50}... | collective-permute-start | bytes 884744 | tf_op jit(solution)/shard_map/ppermute | solution.py:48
  78.1 1.3 %collective-permute-done.24.got_ref = bf16[128,1152]{1,0:T(8,128)(2,1)S(1)} collective-permute-done((bf16[128,1152]{1,0:T(8,128)(2,1)S(1)}, bf16[128,1152]{1,0:T(8,128)(2,1)S(1)}, u32[]{:S(2)}, u32[]{:S(2)}) %collective-permute-start.24) | collective-permute-done | bytes 294944 | tf_op jit(solution)/shard_map/ppermute | solution.py:48
  79.4 0.5 relay.1
  79.9 0.1 collective-permute-start.25
  80.0 1.0 %collective-permute-start.26 = (bf16[16,896]{1,0:T(8,128)(2,1)S(1)}, bf16[16,896]{1,0:T(8,128)(2,1)S(1)}, u32[]{:S(2)}, u32[]{:S(2)}) collective-permute-start(bf16[16,896]{1,0:T(8,128)(2,1)S(1)} %get-tuple-element.69), channel_id=1, source_target_pairs={{0,2},{2,4},{4,6},{6,0},{1,3},{3,5},{5,7},{7,1},{8,10},{10,12},{12... | collective-permute-start | bytes 86024 | tf_op jit(solution)/shard_map/ppermute | solution.py:32
  81.1 1.3 %collective-permute-start.27 = (bf16[16,896]{1,0:T(8,128)(2,1)S(1)}, bf16[16,896]{1,0:T(8,128)(2,1)S(1)}, u32[]{:S(2)}, u32[]{:S(2)}) collective-permute-start(bf16[16,896]{1,0:T(8,128)(2,1)S(1)} %get-tuple-element.70), channel_id=1, source_target_pairs={{0,4},{2,6},{4,0},{6,2},{1,5},{3,7},{5,1},{7,3},{8,12},{10,14},{12... | collective-permute-start | bytes 86024 | tf_op jit(solution)/shard_map/ppermute | solution.py:32
  82.4 2.9 %collective-permute-start.28 = (bf16[16,896]{1,0:T(8,128)(2,1)S(1)}, bf16[16,896]{1,0:T(8,128)(2,1)S(1)}, u32[]{:S(2)}, u32[]{:S(2)}) collective-permute-start(bf16[16,896]{1,0:T(8,128)(2,1)S(1)} %get-tuple-element.71), channel_id=1, source_target_pairs={{0,6},{2,0},{4,2},{6,4},{1,7},{3,1},{5,3},{7,5},{8,14},{10,8},{12,... | collective-permute-start | bytes 86024 | tf_op jit(solution)/shard_map/ppermute | solution.py:32
  85.3 2.8 %attend.3.a_ref = bf16[128,1152]{1,0:T(8,128)(2,1)S(1)} custom-call(s32[1]{0:T(128)} %bitcast.s, s32[64]{0:T(128)S(1)} %copy-done.4, bf16[128,1536]{1,0:T(8,128)(2,1)S(1)} %copy-done.1, bf16[8,1024,128]{2,1,0:T(8,128)(2,1)S(1)} %get-tuple-element.61.refs_1_.refs_2_, bf16[8,1024,128]{2,1,0:T(8,128)(2,1)S(1)} %get-tuple-element.62.refs_2_.refs_3_, ...), custom_call_target="tpu_custom_call" | custom-call | tf_op jit(solution)/shard_map/attend/pallas_call | solution.py:362
  88.2 1.4 %final.1 = (bf16[16,3584]{1,0:T(8,128)(2,1)}, bf16[128,1024]{1,0:T(8,128)(2,1)}) custom-call(s32[1]{0:T(128)} %bitcast.s, bf16[128,1152]{1,0:T(8,128)(2,1)S(1)} %attend.3.a_ref, bf16[128,1152]{1,0:T(8,128)(2,1)S(1)} %collective-permute-done.23.b_ref, bf16[128,1152]{1,0:T(8,128)(2,1)S(1)} %collective-permute-done.25.c_ref, ...), custom_call_target="tpu_custom_call" | custom-call | tf_op jit(solution)/shard_map/final/pallas_call | solution.py:404
  (41 shorter events, 0.2 us)
Async XLA Ops:
  0.6 13.7 %collective-permute-start = (bf16[112,576]{1,0:T(8,128)(2,1)}, bf16[112,576]{1,0:T(8,128)(2,1)S(1)}, u32[]{:S(2)}, u32[]{:S(2)}) collective-permute-start(bf16[112,576]{1,0:T(8,128)(2,1)} %param.19), channel_id=1, source_target_pairs={{2,0},{14,1},{67,2},{79,3},{132,4},{136,5},{197,6},{201,7},{6,8},{... | collective-permute-start | bytes 387080 | tf_op jit(solution)/shard_map/ppermute | solution.py:66
  7.7 0.9 %copy-start.2 = (bf16[128,1024]{1,0:T(8,128)(2,1)S(1)}, bf16[128,1024]{1,0:T(8,128)(2,1)}, u32[]{:S(2)}) copy-start(bf16[128,1024]{1,0:T(8,128)(2,1)} %param.12) | copy-start | bytes 786436
  8.6 0.9 %copy-start.3 = (bf16[16,3584]{1,0:T(8,128)(2,1)S(1)}, bf16[16,3584]{1,0:T(8,128)(2,1)}, u32[]{:S(2)}) copy-start(bf16[16,3584]{1,0:T(8,128)(2,1)} %res_hbm.1) | copy-start | bytes 344068
  14.3 17.5 %copy-start.1 = (bf16[128,1536]{1,0:T(8,128)(2,1)S(1)}, bf16[128,1536]{1,0:T(8,128)(2,1)}, u32[]{:S(2)}) copy-start(bf16[128,1536]{1,0:T(8,128)(2,1)} %refs_0_.1) | copy-start | bytes 1179652
  14.4 21.1 %copy-start.5 = (bf16[3584]{0:T(1024)(128)(2,1)S(1)}, bf16[3584]{0:T(1024)(128)(2,1)}, u32[]{:S(2)}) copy-start(bf16[3584]{0:T(1024)(128)(2,1)} %param.18) | copy-start | bytes 21508
  14.4 3.2 %collective-permute-start.1 = (bf16[4,64,896]{2,1,0:T(8,128)(2,1)S(1)}, bf16[4,64,896]{2,1,0:T(8,128)(2,1)S(1)}, u32[]{:S(2)}, u32[]{:S(2)}) collective-permute-start(bf16[4,64,896]{2,1,0:T(8,128)(2,1)S(1)} %get-tuple-element.39), channel_id=1, source_target_pairs={{0,1},{1,0},{2,3},{3,2},{4,5},{5,4},{6,7},{7,6},{8,9},{9,8},{10,11... | collective-permute-start | bytes 1376264 | tf_op jit(solution)/shard_map/ppermute | solution.py:36
  14.5 8.9 %collective-permute-start.7 = (bf16[1,112,576]{2,1,0:T(8,128)(2,1)S(1)}, bf16[1,112,576]{2,1,0:T(8,128)(2,1)S(1)}, u32[]{:S(2)}, u32[]{:S(2)}) collective-permute-start(bf16[1,112,576]{2,1,0:T(8,128)(2,1)S(1)} %bitcast.3), channel_id=1, source_target_pairs={{0,48},{16,32},{32,16},{48,0},{1,49},{17,33},{33,17},{49,1},{2,50}... | collective-permute-start | bytes 387080 | tf_op jit(solution)/shard_map/ppermute | solution.py:36
  17.3 6.6 %collective-permute-start.5 = (bf16[1,112,576]{2,1,0:T(8,128)(2,1)S(1)}, bf16[1,112,576]{2,1,0:T(8,128)(2,1)S(1)}, u32[]{:S(2)}, u32[]{:S(2)}) collective-permute-start(bf16[1,112,576]{2,1,0:T(8,128)(2,1)S(1)} %bitcast.4), channel_id=1, source_target_pairs={{0,16},{16,0},{32,48},{48,32},{1,17},{17,1},{33,49},{49,33},{2,18}... | collective-permute-start | bytes 387080 | tf_op jit(solution)/shard_map/ppermute | solution.py:36
  17.7 14.0 %collective-permute-start.6 = (bf16[1,112,576]{2,1,0:T(8,128)(2,1)S(1)}, bf16[1,112,576]{2,1,0:T(8,128)(2,1)S(1)}, u32[]{:S(2)}, u32[]{:S(2)}) collective-permute-start(bf16[1,112,576]{2,1,0:T(8,128)(2,1)S(1)} %pack.3), channel_id=1, source_target_pairs={{0,32},{16,48},{32,0},{48,16},{1,33},{17,49},{33,1},{49,17},{2,34}... | collective-permute-start | bytes 387080 | tf_op jit(solution)/shard_map/ppermute | solution.py:36
  19.5 7.9 %collective-permute-start.2 = (bf16[64,896]{1,0:T(8,128)(2,1)S(1)}, bf16[64,896]{1,0:T(8,128)(2,1)S(1)}, u32[]{:S(2)}, u32[]{:S(2)}) collective-permute-start(bf16[64,896]{1,0:T(8,128)(2,1)S(1)} %get-tuple-element.40), channel_id=1, source_target_pairs={{0,2},{2,4},{4,6},{6,0},{1,3},{3,5},{5,7},{7,1},{8,10},{10,12},{12... | collective-permute-start | bytes 344072 | tf_op jit(solution)/shard_map/ppermute | solution.py:32
  19.5 8.3 %collective-permute-start.4 = (bf16[64,896]{1,0:T(8,128)(2,1)S(1)}, bf16[64,896]{1,0:T(8,128)(2,1)S(1)}, u32[]{:S(2)}, u32[]{:S(2)}) collective-permute-start(bf16[64,896]{1,0:T(8,128)(2,1)S(1)} %get-tuple-element.42), channel_id=1, source_target_pairs={{0,6},{2,0},{4,2},{6,4},{1,7},{3,1},{5,3},{7,5},{8,14},{10,8},{12,... | collective-permute-start | bytes 344072 | tf_op jit(solution)/shard_map/ppermute | solution.py:32
  23.3 8.4 %collective-permute-start.3 = (bf16[64,896]{1,0:T(8,128)(2,1)S(1)}, bf16[64,896]{1,0:T(8,128)(2,1)S(1)}, u32[]{:S(2)}, u32[]{:S(2)}) collective-permute-start(bf16[64,896]{1,0:T(8,128)(2,1)S(1)} %get-tuple-element.41.refs_1_), channel_id=1, source_target_pairs={{0,4},{2,6},{4,0},{6,2},{1,5},{3,7},{5,1},{7,3},{8,12},{10,14},{12... | collective-permute-start | bytes 344072 | tf_op jit(solution)/shard_map/ppermute | solution.py:32
  31.8 3.7 %collective-permute-start.8 = (bf16[4,112,576]{2,1,0:T(8,128)(2,1)S(1)}, bf16[4,112,576]{2,1,0:T(8,128)(2,1)S(1)}, u32[]{:S(2)}, u32[]{:S(2)}) collective-permute-start(bf16[4,112,576]{2,1,0:T(8,128)(2,1)S(1)} %pack.4.own_ref), channel_id=1, source_target_pairs={{0,1},{1,0},{2,3},{3,2},{4,5},{5,4},{6,7},{7,6},{8,9},{9,8},{10,11... | collective-permute-start | bytes 1548296 | tf_op jit(solution)/shard_map/ppermute | solution.py:36
  31.9 17.3 %collective-permute-start.13 = (bf16[128,1536]{1,0:T(8,128)(2,1)S(1)}, bf16[128,1536]{1,0:T(8,128)(2,1)S(1)}, u32[]{:S(2)}, u32[]{:S(2)}) collective-permute-start(bf16[128,1536]{1,0:T(8,128)(2,1)S(1)} %copy-done.1), channel_id=1, source_target_pairs={{0,32},{16,48},{32,0},{48,16},{1,33},{17,49},{33,1},{49,17},{2,34}... | collective-permute-start | bytes 1179656 | tf_op jit(solution)/shard_map/ppermute | solution.py:32
  33.6 22.7 %collective-permute-start.21 = (bf16[128,1536]{1,0:T(8,128)(2,1)S(1)}, bf16[128,1536]{1,0:T(8,128)(2,1)S(1)}, u32[]{:S(2)}, u32[]{:S(2)}) collective-permute-start(bf16[128,1536]{1,0:T(8,128)(2,1)S(1)} %copy-done.1), channel_id=1, source_target_pairs={{0,16},{1,49},{16,32},{17,1},{32,48},{33,17},{48,0},{49,33},{2,18}... | collective-permute-start | bytes 1179656 | tf_op jit(solution)/shard_map/ppermute | solution.py:48
  35.5 3.1 %copy-start.6 = (bf16[512]{0:T(512)(128)(2,1)S(1)}, bf16[512]{0:T(512)(128)(2,1)}, u32[]{:S(2)}) copy-start(bf16[512]{0:T(512)(128)(2,1)} %param.20) | copy-start | bytes 3076
  35.5 3.1 %copy-start.4 = (s32[64]{0:T(128)S(1)}, s32[64]{0:T(128)}, u32[]{:S(2)}) copy-start(s32[64]{0:T(128)} %seg.8) | copy-start | bytes 772
  35.6 29.7 %copy-start = (bf16[512,2048]{1,0:T(8,128)(2,1)S(1)}, bf16[512,2048]{1,0:T(8,128)(2,1)}, u32[]{:S(2)}) copy-start(bf16[512,2048]{1,0:T(8,128)(2,1)} %refs_8_.1) | copy-start | bytes 6291460
  36.0 4.8 %collective-permute-start.11 = (bf16[64,640]{1,0:T(8,128)(2,1)S(1)}, bf16[64,640]{1,0:T(8,128)(2,1)S(1)}, u32[]{:S(2)}, u32[]{:S(2)}) collective-permute-start(bf16[64,640]{1,0:T(8,128)(2,1)S(1)} %get-tuple-element.44.p0), channel_id=1, source_target_pairs={{0,6},{2,0},{4,2},{6,4},{1,7},{3,1},{5,3},{7,5},{8,14},{10,8},{12,... | collective-permute-start | bytes 245768 | tf_op jit(solution)/shard_map/ppermute | solution.py:32
  37.9 7.7 %collective-permute-start.10 = (bf16[64,640]{1,0:T(8,128)(2,1)S(1)}, bf16[64,640]{1,0:T(8,128)(2,1)S(1)}, u32[]{:S(2)}, u32[]{:S(2)}) collective-permute-start(bf16[64,640]{1,0:T(8,128)(2,1)S(1)} %get-tuple-element.44.p0), channel_id=1, source_target_pairs={{0,4},{2,6},{4,0},{6,2},{1,5},{3,7},{5,1},{7,3},{8,12},{10,14},{12... | collective-permute-start | bytes 245768 | tf_op jit(solution)/shard_map/ppermute | solution.py:32
  38.0 7.7 %collective-permute-start.9 = (bf16[64,640]{1,0:T(8,128)(2,1)S(1)}, bf16[64,640]{1,0:T(8,128)(2,1)S(1)}, u32[]{:S(2)}, u32[]{:S(2)}) collective-permute-start(bf16[64,640]{1,0:T(8,128)(2,1)S(1)} %get-tuple-element.44.p0), channel_id=1, source_target_pairs={{0,2},{2,4},{4,6},{6,0},{1,3},{3,5},{5,7},{7,1},{8,10},{10,12},{12... | collective-permute-start | bytes 245768 | tf_op jit(solution)/shard_map/ppermute | solution.py:32
  45.9 6.6 %collective-permute-start.12 = (bf16[64,640]{1,0:T(8,128)(2,1)S(1)}, bf16[64,640]{1,0:T(8,128)(2,1)S(1)}, u32[]{:S(2)}, u32[]{:S(2)}) collective-permute-start(bf16[64,640]{1,0:T(8,128)(2,1)S(1)} %kv_rows.1.refs_0_), channel_id=1, source_target_pairs={{0,12},{2,14},{4,8},{6,10},{8,4},{10,6},{12,0},{14,2},{1,13},{3,15... | collective-permute-start | bytes 245768 | tf_op jit(solution)/shard_map/ppermute | solution.py:71
  49.1 14.8 %collective-permute-start.22 = (bf16[128,1536]{1,0:T(8,128)(2,1)S(1)}, bf16[128,1536]{1,0:T(8,128)(2,1)S(1)}, u32[]{:S(2)}, u32[]{:S(2)}) collective-permute-start(bf16[128,1536]{1,0:T(8,128)(2,1)S(1)} %copy-done.1), channel_id=1, source_target_pairs={{0,48},{1,17},{16,0},{17,33},{32,16},{33,49},{48,32},{49,1},{2,50}... | collective-permute-start | bytes 1179656 | tf_op jit(solution)/shard_map/ppermute | solution.py:48
  52.6 7.7 %collective-permute-start.16 = (bf16[128,640]{1,0:T(8,128)(2,1)S(1)}, bf16[128,640]{1,0:T(8,128)(2,1)S(1)}, u32[]{:S(2)}, u32[]{:S(2)}) collective-permute-start(bf16[128,640]{1,0:T(8,128)(2,1)S(1)} %pack.5.refs_0_), channel_id=1, source_target_pairs={{0,64},{64,128},{128,192},{192,0},{1,65},{65,129},{129,193},{193,1... | collective-permute-start | bytes 491528 | tf_op jit(solution)/shard_map/ppermute | solution.py:32
  54.9 7.4 %collective-permute-start.15 = (bf16[128,640]{1,0:T(8,128)(2,1)S(1)}, bf16[128,640]{1,0:T(8,128)(2,1)S(1)}, u32[]{:S(2)}, u32[]{:S(2)}) collective-permute-start(bf16[128,640]{1,0:T(8,128)(2,1)S(1)} %pack.5.refs_0_), channel_id=1, source_target_pairs={{0,128},{64,192},{128,0},{192,64},{1,129},{65,193},{129,1},{193,65... | collective-permute-start | bytes 491528 | tf_op jit(solution)/shard_map/ppermute | solution.py:32
  56.0 8.0 %collective-permute-start.14 = (bf16[128,640]{1,0:T(8,128)(2,1)S(1)}, bf16[128,640]{1,0:T(8,128)(2,1)S(1)}, u32[]{:S(2)}, u32[]{:S(2)}) collective-permute-start(bf16[128,640]{1,0:T(8,128)(2,1)S(1)} %pack.5.refs_0_), channel_id=1, source_target_pairs={{0,192},{64,0},{128,64},{192,128},{1,193},{65,1},{129,65},{193,129... | collective-permute-start | bytes 491528 | tf_op jit(solution)/shard_map/ppermute | solution.py:32
  56.4 7.6 %collective-permute-start.17 = (bf16[128,640]{1,0:T(8,128)(2,1)S(1)}, bf16[128,640]{1,0:T(8,128)(2,1)S(1)}, u32[]{:S(2)}, u32[]{:S(2)}) collective-permute-start(bf16[128,640]{1,0:T(8,128)(2,1)S(1)} %pack.5.refs_0_), channel_id=1, source_target_pairs={{0,1},{1,0},{2,3},{3,2},{4,5},{5,4},{6,7},{7,6},{8,9},{9,8},{10,11... | collective-permute-start | bytes 491528 | tf_op jit(solution)/shard_map/ppermute | solution.py:36
  60.3 3.7 %collective-permute-start.20 = (bf16[128,640]{1,0:T(8,128)(2,1)S(1)}, bf16[128,640]{1,0:T(8,128)(2,1)S(1)}, u32[]{:S(2)}, u32[]{:S(2)}) collective-permute-start(bf16[128,640]{1,0:T(8,128)(2,1)S(1)} %collective-permute-done.16.refs_3_), channel_id=1, source_target_pairs={{0,1},{1,0},{2,3},{3,2},{4,5},{5,4},{6,7},{7,6},{8,9},{9,8},{10,11... | collective-permute-start | bytes 491528 | tf_op jit(solution)/shard_map/ppermute | solution.py:36
  62.3 1.7 %collective-permute-start.19 = (bf16[128,640]{1,0:T(8,128)(2,1)S(1)}, bf16[128,640]{1,0:T(8,128)(2,1)S(1)}, u32[]{:S(2)}, u32[]{:S(2)}) collective-permute-start(bf16[128,640]{1,0:T(8,128)(2,1)S(1)} %collective-permute-done.15.refs_2_), channel_id=1, source_target_pairs={{0,1},{1,0},{2,3},{3,2},{4,5},{5,4},{6,7},{7,6},{8,9},{9,8},{10,11... | collective-permute-start | bytes 491528 | tf_op jit(solution)/shard_map/ppermute | solution.py:36
  63.9 1.4 %collective-permute-start.18 = (bf16[128,640]{1,0:T(8,128)(2,1)S(1)}, bf16[128,640]{1,0:T(8,128)(2,1)S(1)}, u32[]{:S(2)}, u32[]{:S(2)}) collective-permute-start(bf16[128,640]{1,0:T(8,128)(2,1)S(1)} %collective-permute-done.14.refs_1_), channel_id=1, source_target_pairs={{0,1},{1,0},{2,3},{3,2},{4,5},{5,4},{6,7},{7,6},{8,9},{9,8},{10,11... | collective-permute-start | bytes 491528 | tf_op jit(solution)/shard_map/ppermute | solution.py:36
  71.2 8.2 %collective-permute-start.24 = (bf16[128,1152]{1,0:T(8,128)(2,1)S(1)}, bf16[128,1152]{1,0:T(8,128)(2,1)S(1)}, u32[]{:S(2)}, u32[]{:S(2)}) collective-permute-start(bf16[128,1152]{1,0:T(8,128)(2,1)S(1)} %attend.5), channel_id=1, source_target_pairs={{0,16},{1,49},{16,32},{17,1},{32,48},{33,17},{48,0},{49,33},{2,18}... | collective-permute-start | bytes 884744 | tf_op jit(solution)/shard_map/ppermute | solution.py:48
  75.8 12.4 %collective-permute-start.23 = (bf16[128,1152]{1,0:T(8,128)(2,1)S(1)}, bf16[128,1152]{1,0:T(8,128)(2,1)S(1)}, u32[]{:S(2)}, u32[]{:S(2)}) collective-permute-start(bf16[128,1152]{1,0:T(8,128)(2,1)S(1)} %get-tuple-element.66), channel_id=1, source_target_pairs={{0,48},{1,17},{16,0},{17,33},{32,16},{33,49},{48,32},{49,1},{2,50}... | collective-permute-start | bytes 884744 | tf_op jit(solution)/shard_map/ppermute | solution.py:48
  79.9 8.3 %collective-permute-start.25 = (bf16[128,1152]{1,0:T(8,128)(2,1)S(1)}, bf16[128,1152]{1,0:T(8,128)(2,1)S(1)}, u32[]{:S(2)}, u32[]{:S(2)}) collective-permute-start(bf16[128,1152]{1,0:T(8,128)(2,1)S(1)} %relay.1), channel_id=1, source_target_pairs={{0,16},{1,49},{16,32},{17,1},{32,48},{33,17},{48,0},{49,33},{2,18}... | collective-permute-start | bytes 884744 | tf_op jit(solution)/shard_map/ppermute | solution.py:48
  80.0 8.1 %collective-permute-start.26 = (bf16[16,896]{1,0:T(8,128)(2,1)S(1)}, bf16[16,896]{1,0:T(8,128)(2,1)S(1)}, u32[]{:S(2)}, u32[]{:S(2)}) collective-permute-start(bf16[16,896]{1,0:T(8,128)(2,1)S(1)} %get-tuple-element.69), channel_id=1, source_target_pairs={{0,2},{2,4},{4,6},{6,0},{1,3},{3,5},{5,7},{7,1},{8,10},{10,12},{12... | collective-permute-start | bytes 86024 | tf_op jit(solution)/shard_map/ppermute | solution.py:32
  81.1 7.1 %collective-permute-start.27 = (bf16[16,896]{1,0:T(8,128)(2,1)S(1)}, bf16[16,896]{1,0:T(8,128)(2,1)S(1)}, u32[]{:S(2)}, u32[]{:S(2)}) collective-permute-start(bf16[16,896]{1,0:T(8,128)(2,1)S(1)} %get-tuple-element.70), channel_id=1, source_target_pairs={{0,4},{2,6},{4,0},{6,2},{1,5},{3,7},{5,1},{7,3},{8,12},{10,14},{12... | collective-permute-start | bytes 86024 | tf_op jit(solution)/shard_map/ppermute | solution.py:32
  82.4 5.8 %collective-permute-start.28 = (bf16[16,896]{1,0:T(8,128)(2,1)S(1)}, bf16[16,896]{1,0:T(8,128)(2,1)S(1)}, u32[]{:S(2)}, u32[]{:S(2)}) collective-permute-start(bf16[16,896]{1,0:T(8,128)(2,1)S(1)} %get-tuple-element.71), channel_id=1, source_target_pairs={{0,6},{2,0},{4,2},{6,4},{1,7},{3,1},{5,3},{7,5},{8,14},{10,8},{12,... | collective-permute-start | bytes 86024 | tf_op jit(solution)/shard_map/ppermute | solution.py:32
